TPU v7x, 32 devices: a whole 2x2x4 slice. The times are simulated.
32 devices in a mesh: fsdp: 4 (over y, x), ctx: 2 (over core), tp: 4 (over z).
Axes of the slice: x: 2, y: 2, z: 4, core: 2. Of those that a mesh axis runs over, the one named last changes fastest.
Arguments:
- tokens: bfloat16 [8192, 1536], P(('fsdp', 'ctx')), may hold values from -6 to 6
- routes: int32 [8192, 8], P(('fsdp', 'ctx')), may hold values from 0 to 15, all different within a row; in each aligned block of 1024 rows (0 to 1023, 1024 to 2047, ...) at most 640 rows name the same one
- gain_attn: bfloat16 [1536], P(('fsdp', 'ctx')), may hold values from 0.5 to 1.5
- w_query: bfloat16 [1536, 1536], P(('fsdp', 'ctx'), 'tp'), may hold values from -0.15625 to 0.15625
- key_matrix: bfloat16 [1536, 512], P(('fsdp', 'ctx'), 'tp'), may hold values from -0.15625 to 0.15625
- value_matrix: bfloat16 [1536, 512], P(('fsdp', 'ctx'), 'tp'), may hold values from -0.15625 to 0.15625
- w_out: bfloat16 [1536, 1536], P('tp', ('fsdp', 'ctx')), may hold values from -0.625 to 0.625
- gain_moe: bfloat16 [1536], P(('fsdp', 'ctx')), may hold values from 0.5 to 1.5
- w_router: bfloat16 [1536, 16], P(('fsdp', 'ctx')), may hold values from -0.078125 to 0.078125
- w_gate: bfloat16 [16, 1536, 512], P(None, ('fsdp', 'ctx'), 'tp'), may hold values from -0.15625 to 0.15625
- w_up: bfloat16 [16, 1536, 512], P(None, ('fsdp', 'ctx'), 'tp'), may hold values from -0.15625 to 0.15625
- w_down: bfloat16 [16, 512, 1536], P(None, 'tp', ('fsdp', 'ctx')), may hold values from -0.75 to 0.75
- cotangent: bfloat16 [8192, 1536], P(('fsdp', 'ctx')), may hold values from -6 to 6
Outputs:
- activations: bfloat16 [8192, 1536], P(('fsdp', 'ctx'))
- input_grad: bfloat16 [8192, 1536], P(('fsdp', 'ctx'))
- grad_gain_attn: float32 [1536], P(('fsdp', 'ctx'))
- grad_query: float32 [1536, 1536], P(('fsdp', 'ctx'), 'tp')
- grad_key: float32 [1536, 512], P(('fsdp', 'ctx'), 'tp')
- grad_value: float32 [1536, 512], P(('fsdp', 'ctx'), 'tp')
- grad_out: float32 [1536, 1536], P('tp', ('fsdp', 'ctx'))
- grad_gain_moe: float32 [1536], P(('fsdp', 'ctx'))
- grad_router: float32 [1536, 16], P(('fsdp', 'ctx'))
- grad_gate: float32 [16, 1536, 512], P(None, ('fsdp', 'ctx'), 'tp')
- grad_up: float32 [16, 1536, 512], P(None, ('fsdp', 'ctx'), 'tp')
- grad_down: float32 [16, 512, 1536], P(None, 'tp', ('fsdp', 'ctx'))
Inputs may be any that keep to these rules, and one draw needn't show every extreme that they name: `routes`: each row names 8 different experts; among the 1024 rows of one device no expert is named more than 640 times, and on some device one is named exactly 640 times.
All inputs are finite; a program needn't handle non-finite values.
Results may differ from a plain program's by a relative error of at most 0.017.
Values may be sent and summed in bfloat16 or wider, within the bound.
A program may use at most 384 MiB of HBM per device.

v0:
```python
import math

import jax
import jax.numpy as jnp
from jax import lax
from jax.sharding import PartitionSpec as P

HEAD_SIZE = 64
TOPK = 8
E = 16
SEQUENCE_LENGTH = 1024


epsilon = 1e-06


def placed(ranks, half):
    quarter = half // 2
    steps = jnp.arange(half, dtype=jnp.int32)
    early = ranks * quarter + steps
    late = SEQUENCE_LENGTH - (ranks + 1) * quarter + steps - quarter
    return jnp.where(steps < quarter, early, late)


def angle_tables(token_places):
    halfway = HEAD_SIZE // 2
    freqs = jnp.exp(jnp.arange(halfway, dtype=jnp.float32) * (-2.0 * math.log(10000.0) / HEAD_SIZE))
    angles = token_places.astype(jnp.float32)[:, None] * freqs[None, :]
    return (jnp.cos(angles)[:, None, :], jnp.sin(angles)[:, None, :])


def rotary_embed(vectors, token_places):
    cosine, sine = angle_tables(token_places)
    halfway = HEAD_SIZE // 2
    lower = vectors[..., :halfway]
    upper = vectors[..., halfway:]
    return jnp.concatenate([lower * cosine - upper * sine, upper * cosine + lower * sine], -1)


def rotary_back(grads, token_places):
    cosine, sine = angle_tables(token_places)
    halfway = HEAD_SIZE // 2
    lower = grads[..., :halfway]
    upper = grads[..., halfway:]
    return jnp.concatenate([lower * cosine + upper * sine, upper * cosine - lower * sine], -1)


def norm_back(value_rows, scale, gain, grad):
    scaled = grad * gain
    inner = jnp.mean(scaled * value_rows, -1, keepdims=True)
    return (
        scale * scaled - value_rows * scale * scale * scale * inner,
        jnp.sum(grad * value_rows * scale, 0),
    )


def score_block(grouped_heads, keyed_rows, q_places, k_places):
    scores = jnp.einsum(
        "qkgd,skd->kgqs", grouped_heads, keyed_rows, preferred_element_type=jnp.float32
    ) * (1.0 / math.sqrt(HEAD_SIZE))
    allowed = k_places[None, :] <= q_places[:, None]
    return jnp.where(allowed, scores, -1e30)


def attend(query_rows, key_rows, value_rows, q_places, k_places):
    kv_here = key_rows.shape[-1] // HEAD_SIZE
    q_len = query_rows.shape[0]
    grouped_heads = query_rows.reshape(q_len, kv_here, -1, HEAD_SIZE)
    keyed_rows = key_rows.reshape(-1, kv_here, HEAD_SIZE)
    valued_rows = value_rows.reshape(-1, kv_here, HEAD_SIZE)
    scores = score_block(grouped_heads, keyed_rows, q_places, k_places)
    top = jnp.max(scores, -1, keepdims=True)
    weights = jnp.exp(scores - top)
    total = jnp.sum(weights, -1, keepdims=True)
    probs = (weights / total).astype(jnp.bfloat16)
    mixed = jnp.einsum("kgqs,skd->qkgd", probs, valued_rows, preferred_element_type=jnp.float32)
    return (mixed.reshape(q_len, -1), top + jnp.log(total))


def attend_back(query_rows, key_rows, value_rows, log_total, mixed_grad, q_places, k_places):
    kv_here = key_rows.shape[-1] // HEAD_SIZE
    q_len = query_rows.shape[0]
    k_len = key_rows.shape[0]
    grouped_heads = query_rows.reshape(q_len, kv_here, -1, HEAD_SIZE)
    keyed_rows = key_rows.reshape(k_len, kv_here, HEAD_SIZE)
    valued_rows = value_rows.reshape(k_len, kv_here, HEAD_SIZE)
    out_grouped = mixed_grad.reshape(q_len, kv_here, -1, HEAD_SIZE)
    scores = score_block(grouped_heads, keyed_rows, q_places, k_places)
    probs = jnp.exp(scores - log_total)
    prob_grad = jnp.einsum(
        "qkgd,skd->kgqs", out_grouped, valued_rows, preferred_element_type=jnp.float32
    )
    score_grad = (probs * (prob_grad - jnp.sum(probs * prob_grad, -1, keepdims=True))).astype(
        jnp.bfloat16
    )
    factor = 1.0 / math.sqrt(HEAD_SIZE)
    query_grad = (
        jnp.einsum("kgqs,skd->qkgd", score_grad, keyed_rows, preferred_element_type=jnp.float32)
        * factor
    )
    key_grad = (
        jnp.einsum("kgqs,qkgd->skd", score_grad, grouped_heads, preferred_element_type=jnp.float32)
        * factor
    )
    value_grad = jnp.einsum(
        "kgqs,qkgd->skd",
        probs.astype(jnp.bfloat16),
        out_grouped,
        preferred_element_type=jnp.float32,
    )
    return (
        query_grad.reshape(q_len, -1, HEAD_SIZE),
        key_grad.reshape(k_len, -1),
        value_grad.reshape(k_len, -1),
    )


def slot_table(route_rows, capacity):
    count = route_rows.shape[0]
    flat = route_rows.reshape(-1)
    hits = (flat[:, None] == jnp.arange(E, dtype=jnp.int32)[None, :]).astype(jnp.int32)
    before = jnp.cumsum(hits, 0) - hits
    ranks = jnp.sum(before * hits, 1)
    where_rows = flat * capacity + ranks
    owners = jnp.arange(count * TOPK, dtype=jnp.int32) // TOPK
    table = jnp.full((E * capacity,), count, jnp.int32).at[where_rows].set(owners)
    return (where_rows, table)


def per_device(
    tokens,
    routes,
    gain_attn,
    w_query,
    key_matrix,
    value_matrix,
    w_out,
    gain_moe,
    w_router,
    w_gate,
    w_up,
    w_down,
    cotangent,
):
    f32 = jnp.float32
    bf16 = jnp.bfloat16
    rows = tokens.shape[0]
    ctx_count = lax.axis_size("ctx")
    half = SEQUENCE_LENGTH // ctx_count
    seq_here = rows // half
    capacity = rows * TOPK * 5 // (4 * E)
    local_places = placed(lax.axis_index("ctx"), half)
    all_places = placed(jnp.arange(ctx_count, dtype=jnp.int32)[:, None], half).reshape(-1)
    gain_one, query_w, key_w, value_w, out_w, gain_two, router_w = (
        lax.all_gather(gain_attn, ("fsdp", "ctx"), axis=0, tiled=True),
        lax.all_gather(w_query, ("fsdp", "ctx"), axis=0, tiled=True),
        lax.all_gather(key_matrix, ("fsdp", "ctx"), axis=0, tiled=True),
        lax.all_gather(value_matrix, ("fsdp", "ctx"), axis=0, tiled=True),
        lax.all_gather(w_out, ("fsdp", "ctx"), axis=1, tiled=True),
        lax.all_gather(gain_moe, ("fsdp", "ctx"), axis=0, tiled=True),
        lax.all_gather(w_router, ("fsdp", "ctx"), axis=0, tiled=True),
    )
    gain_one_f = gain_one.astype(f32)
    gain_two_f = gain_two.astype(f32)
    inputs = tokens.astype(f32)
    scale_one = lax.rsqrt(jnp.mean(inputs * inputs, -1, keepdims=True) + epsilon)
    normed = (inputs * scale_one * gain_one_f).astype(bf16)
    heads_here = query_w.shape[1] // HEAD_SIZE
    kv_here = key_w.shape[1] // HEAD_SIZE
    query = jnp.dot(normed, query_w, preferred_element_type=f32)
    key = jnp.dot(normed, key_w, preferred_element_type=f32)
    value = jnp.dot(normed, value_w, preferred_element_type=f32)
    query_rot = rotary_embed(
        query.reshape(seq_here, half, heads_here, HEAD_SIZE), local_places
    ).astype(bf16)
    key_rot = (
        rotary_embed(key.reshape(seq_here, half, kv_here, HEAD_SIZE), local_places)
        .astype(bf16)
        .reshape(seq_here, half, kv_here * HEAD_SIZE)
    )
    value_low = value.astype(bf16).reshape(seq_here, half, kv_here * HEAD_SIZE)
    keys_all, values_all = (
        lax.all_gather(key_rot, "ctx", axis=1, tiled=True),
        lax.all_gather(value_low, "ctx", axis=1, tiled=True),
    )

    def forward_one(pieces):
        return attend(pieces[0], pieces[1], pieces[2], local_places, all_places)

    mixed, log_total = lax.map(forward_one, (query_rot, keys_all, values_all))
    mixed_low = mixed.reshape(rows, heads_here * HEAD_SIZE).astype(bf16)
    head_part = jnp.dot(mixed_low, out_w, preferred_element_type=f32)
    head_total = lax.psum(head_part, "tp")
    state = inputs + head_total
    scale_two = lax.rsqrt(jnp.mean(state * state, -1, keepdims=True) + epsilon)
    normed_two = (state * scale_two * gain_two_f).astype(bf16)
    logits = jnp.dot(normed_two, router_w, preferred_element_type=f32)
    match = routes[:, :, None] == jnp.arange(E, dtype=jnp.int32)[None, None, :]
    picked = jnp.sum(jnp.where(match, logits[:, None, :], 0.0), -1)
    gates = jax.nn.softmax(picked, -1)
    where_rows, table = slot_table(routes, capacity)
    gate_full, up_full, down_full = (
        lax.all_gather(w_gate, ("fsdp", "ctx"), axis=1, tiled=True),
        lax.all_gather(w_up, ("fsdp", "ctx"), axis=1, tiled=True),
        lax.all_gather(w_down, ("fsdp", "ctx"), axis=2, tiled=True),
    )
    padded = jnp.concatenate([normed_two, jnp.zeros((1, normed_two.shape[1]), bf16)], 0)
    buffer = padded[table].reshape(E, capacity, -1)
    gate_pre = jnp.einsum("ecd,edf->ecf", buffer, gate_full, preferred_element_type=f32)
    up_pre = jnp.einsum("ecd,edf->ecf", buffer, up_full, preferred_element_type=f32)
    hidden = (jax.nn.silu(gate_pre) * up_pre).astype(bf16)
    part_out = jnp.einsum("ecf,efd->ecd", hidden, down_full, preferred_element_type=f32)
    picked_rows = part_out.reshape(E * capacity, -1)[where_rows].reshape(rows, TOPK, -1)
    moe_part = jnp.sum(gates[:, :, None] * picked_rows, 1)
    upstream = cotangent.astype(f32)
    dots_part = jnp.sum(picked_rows * upstream[:, None, :], -1)
    moe_total, gate_dots = lax.psum((moe_part, dots_part), "tp")
    activations = (state + moe_total).astype(bf16)
    mix_grad = gates * (gate_dots - jnp.sum(gates * gate_dots, -1, keepdims=True))
    logit_grad = jnp.sum(jnp.where(match, mix_grad[:, :, None], 0.0), 1).astype(bf16)
    slot_rows = (gates[:, :, None] * upstream[:, None, :]).astype(bf16).reshape(rows * TOPK, -1)
    out_grad = (
        jnp.zeros((E * capacity, slot_rows.shape[1]), bf16)
        .at[where_rows]
        .set(slot_rows)
        .reshape(E, capacity, -1)
    )
    gate_back, up_back, down_back = (
        lax.all_gather(w_gate, ("fsdp", "ctx"), axis=1, tiled=True),
        lax.all_gather(w_up, ("fsdp", "ctx"), axis=1, tiled=True),
        lax.all_gather(w_down, ("fsdp", "ctx"), axis=2, tiled=True),
    )
    hidden_grad = jnp.einsum("ecd,efd->ecf", out_grad, down_back, preferred_element_type=f32)
    sigma = jax.nn.sigmoid(gate_pre)
    gate_grad = (hidden_grad * up_pre * sigma * (1.0 + gate_pre * (1.0 - sigma))).astype(bf16)
    up_grad = (hidden_grad * gate_pre * sigma).astype(bf16)
    grad_down = jnp.einsum("ecf,ecd->efd", hidden, out_grad, preferred_element_type=f32)
    grad_gate = jnp.einsum("ecd,ecf->edf", buffer, gate_grad, preferred_element_type=f32)
    grad_up = jnp.einsum("ecd,ecf->edf", buffer, up_grad, preferred_element_type=f32)
    buffer_grad = jnp.einsum("ecf,edf->ecd", gate_grad, gate_back, preferred_element_type=f32)
    buffer_grad = buffer_grad + jnp.einsum(
        "ecf,edf->ecd", up_grad, up_back, preferred_element_type=f32
    )
    normed_two_part = jnp.sum(
        buffer_grad.reshape(E * capacity, -1)[where_rows].reshape(rows, TOPK, -1), 1
    )
    normed_two_grad = lax.psum(normed_two_part, "tp")
    normed_two_grad = normed_two_grad + jnp.einsum(
        "te,de->td", logit_grad, router_w, preferred_element_type=f32
    )
    grad_router = jnp.einsum("td,te->de", normed_two, logit_grad, preferred_element_type=f32)
    state_delta, grad_gain_two = norm_back(state, scale_two, gain_two_f, normed_two_grad)
    state_grad = upstream + state_delta
    state_low = state_grad.astype(bf16)
    grad_out = jnp.einsum("tc,td->cd", mixed_low, state_low, preferred_element_type=f32)
    mixed_grad = jnp.einsum("td,cd->tc", state_low, out_w, preferred_element_type=f32).astype(bf16)
    mixed_grad = mixed_grad.reshape(seq_here, half, heads_here, HEAD_SIZE)

    def backward_one(pieces):
        return attend_back(
            pieces[0], pieces[1], pieces[2], pieces[3], pieces[4], local_places, all_places
        )

    query_grad, key_grad, value_grad = lax.map(
        backward_one, (query_rot, keys_all, values_all, log_total, mixed_grad)
    )
    key_grad, value_grad = (
        lax.psum_scatter(key_grad, "ctx", scatter_dimension=1, tiled=True),
        lax.psum_scatter(value_grad, "ctx", scatter_dimension=1, tiled=True),
    )
    query_low = (
        rotary_back(query_grad, local_places).astype(bf16).reshape(rows, heads_here * HEAD_SIZE)
    )
    key_low = (
        rotary_back(key_grad.reshape(seq_here, half, kv_here, HEAD_SIZE), local_places)
        .astype(bf16)
        .reshape(rows, kv_here * HEAD_SIZE)
    )
    value_grad_low = value_grad.astype(bf16).reshape(rows, kv_here * HEAD_SIZE)
    normed_part = jnp.einsum("tc,dc->td", query_low, query_w, preferred_element_type=f32)
    normed_part = normed_part + jnp.einsum("tc,dc->td", key_low, key_w, preferred_element_type=f32)
    normed_part = normed_part + jnp.einsum(
        "tc,dc->td", value_grad_low, value_w, preferred_element_type=f32
    )
    normed_grad = lax.psum(normed_part.astype(jnp.bfloat16), "tp").astype(jnp.float32)
    input_delta, grad_gain_one = norm_back(inputs, scale_one, gain_one_f, normed_grad)
    input_grad = (state_grad + input_delta).astype(bf16)
    grad_query = jnp.einsum("td,tc->dc", normed, query_low, preferred_element_type=f32)
    grad_key = jnp.einsum("td,tc->dc", normed, key_low, preferred_element_type=f32)
    grad_value = jnp.einsum("td,tc->dc", normed, value_grad_low, preferred_element_type=f32)
    block_grads = (
        lax.psum_scatter(grad_gain_one, ("fsdp", "ctx"), scatter_dimension=0, tiled=True),
        lax.psum_scatter(grad_query, ("fsdp", "ctx"), scatter_dimension=0, tiled=True),
        lax.psum_scatter(grad_key, ("fsdp", "ctx"), scatter_dimension=0, tiled=True),
        lax.psum_scatter(grad_value, ("fsdp", "ctx"), scatter_dimension=0, tiled=True),
        lax.psum_scatter(grad_out, ("fsdp", "ctx"), scatter_dimension=1, tiled=True),
        lax.psum_scatter(grad_gain_two, ("fsdp", "ctx"), scatter_dimension=0, tiled=True),
        lax.psum_scatter(grad_router, ("fsdp", "ctx"), scatter_dimension=0, tiled=True),
    )
    expert_grads = (
        lax.psum_scatter(grad_gate, ("fsdp", "ctx"), scatter_dimension=1, tiled=True),
        lax.psum_scatter(grad_up, ("fsdp", "ctx"), scatter_dimension=1, tiled=True),
        lax.psum_scatter(grad_down, ("fsdp", "ctx"), scatter_dimension=2, tiled=True),
    )
    return (
        activations,
        input_grad,
        block_grads[0],
        block_grads[1],
        block_grads[2],
        block_grads[3],
        block_grads[4],
        block_grads[5],
        block_grads[6],
        expert_grads[0],
        expert_grads[1],
        expert_grads[2],
    )


def solution(mesh):
    placed = (
        P(("fsdp", "ctx"), None),
        P(("fsdp", "ctx"), None),
        P(("fsdp", "ctx")),
        P(("fsdp", "ctx"), "tp"),
        P(("fsdp", "ctx"), "tp"),
        P(("fsdp", "ctx"), "tp"),
        P("tp", ("fsdp", "ctx")),
        P(("fsdp", "ctx")),
        P(("fsdp", "ctx"), None),
        P(None, ("fsdp", "ctx"), "tp"),
        P(None, ("fsdp", "ctx"), "tp"),
        P(None, "tp", ("fsdp", "ctx")),
        P(("fsdp", "ctx"), None),
    )
    return jax.shard_map(
        per_device,
        mesh=mesh,
        in_specs=placed,
        out_specs=(
            P(("fsdp", "ctx"), None),
            P(("fsdp", "ctx"), None),
            P(("fsdp", "ctx")),
            P(("fsdp", "ctx"), "tp"),
            P(("fsdp", "ctx"), "tp"),
            P(("fsdp", "ctx"), "tp"),
            P("tp", ("fsdp", "ctx")),
            P(("fsdp", "ctx")),
            P(("fsdp", "ctx"), None),
            P(None, ("fsdp", "ctx"), "tp"),
            P(None, ("fsdp", "ctx"), "tp"),
            P(None, "tp", ("fsdp", "ctx")),
        ),
        check_vma=False,
    )
```

profile of v0, /device:TPU:0, one launch (start us, length us, event | category | flops | bytes accessed | tf_op | source)
XLA Modules:
  0.0 2349.2 jit_solution(17451131647486834288)
XLA Ops:
  15.6 16.1 all-reduce.7
  82.0 21.5 while.28
  134.3 30.5 %scatter_custom_fusion = s32[10240]{0:T(1024)S(1)} fusion(s32[8192]{0:T(1024)S(1)} %bitcast.326, s32[8192]{0:T(1024)S(1)} %add_select_fusion.2, s32[]{:T(128)} %constant.110.clone.1), kind=kCustom, calls=%fused_computation.151 | custom fusion | bytes 40964 | tf_op jit(solution)/shard_map/scatter | solution.py:126
  176.2 157.3 %all-reduce.12.cloned.1.call-done = f32[1024,1536]{1,0:T(8,128)} async-done(((f32[1024,1536]{1,0:T(8,128)}), f32[1024,1536]{1,0:T(8,128)}) %all-reduce.12.cloned.1.call-update) | async-done | bytes 6291472 | tf_op jit(solution)/shard_map/psum | solution.py:193
  345.5 46.5 %gather_fusion = bf16[10240,1536]{1,0:T(8,128)(2,1)} fusion(bf16[1025,1536]{1,0:T(8,128)(2,1)S(1)} %concatenate.21, s32[10240]{0:T(1024)S(1)} %fusion.64), kind=kCustom, calls=%fused_computation | custom fusion | bytes 62955520 | tf_op jit(solution)/shard_map/gather | solution.py:208
  392.1 15.0 fusion.32
  407.1 145.7 %scatter_custom_fusion.1 = bf16[10240,1536]{1,0:T(8,128)(2,1)} fusion(s32[8192]{0:T(1024)S(1)} %get-tuple-element.299, bf16[8192,1536]{1,0:T(8,128)(2,1)} %fusion.32, s32[8192]{0:T(1024)S(1)} %broadcast_clamp_fusion, bf16[]{:T(256)} %constant.115.clone.1), kind=kCustom, calls=%fused_computation.70 | custom fusion | bytes 31457792 | tf_op jit(solution)/shard_map/scatter | solution.py:225
  552.9 20.4 fusion.82
  573.2 17.6 fusion.81
  590.8 20.4 multiply_convert_fusion.1
  611.2 26.5 %fusion.84 = f32[16,640,1536]{2,1,0:T(8,128)} fusion(bf16[16,640,128]{2,1,0:T(8,128)(2,1)} %get-tuple-element.376, bf16[16,1536,128]{2,1,0:T(8,128)(2,1)} %all-gather.11.cloned.1.call-done), kind=kOutput, calls=%fused_computation.177 | convolution fusion | flops 4026531840 | bytes 71827456 | tf_op jit(solution)/shard_map/ecf,edf->ecd/dot_general | solution.py:240
  637.8 42.1 %convolution_add_fusion = f32[16,640,1536]{2,1,0:T(8,128)} fusion(f32[16,640,1536]{2,1,0:T(8,128)} %fusion.84, bf16[16,640,128]{2,1,0:T(8,128)(2,1)S(1)} %get-tuple-element.375, bf16[16,1536,128]{2,1,0:T(8,128)(2,1)} %all-gather.13.cloned.1.call-done), kind=kOutput, calls=%fused_computation.69 | convolution fusion | flops 4042260480 | bytes 134742016 | tf_op jit(solution)/shard_map/ecf,edf->ecd/dot_general | solution.py:241
  679.9 179.9 %gather_fusion.2 = f32[8192,1536]{1,0:T(8,128)} fusion(f32[10240,1536]{1,0:T(8,128)} %bitcast.284, s32[8192]{0:T(1024)S(1)} %copy-done.41), kind=kCustom, calls=%fused_computation.2 | custom fusion | bytes 100696064 | tf_op jit(solution)/shard_map/gather | solution.py:245
  859.9 21.7 bitcast_reduce_fusion
  881.6 26.5 %fusion.83 = f32[16,640,1536]{2,1,0:T(8,128)} fusion(bf16[16,640,128]{2,1,0:T(8,128)(2,1)S(1)} %copy-done.18, bf16[16,128,1536]{1,2,0:T(8,128)(2,1)} %all-gather.15.cloned.1.call-done), kind=kOutput, calls=%fused_computation.176 | convolution fusion | flops 4026531840 | bytes 71827456 | tf_op jit(solution)/shard_map/ecf,efd->ecd/dot_general | solution.py:212
  908.1 179.9 %gather_fusion.1 = f32[8192,1536]{1,0:T(8,128)} fusion(f32[10240,1536]{1,0:T(8,128)} %bitcast.285, s32[8192]{0:T(1024)S(1)} %copy-done.41), kind=kCustom, calls=%fused_computation.1 | custom fusion | bytes 100696064 | tf_op jit(solution)/shard_map/gather | solution.py:213
  1088.1 67.2 %fusion.34 = (f32[1024,8]{1,0:T(8,128)S(1)}, f32[1024,1536]{1,0:T(8,128)}) fusion(f32[8192,1536]{1,0:T(8,128)} %gather_fusion.1, f32[1024,1536]{1,0:T(8,128)} %convert_element_type.120, f32[1024,8]{1,0:T(8,128)S(1)} %copy-done.21), kind=kLoop, calls=%fused_computation.68 | loop fusion | flops 48750592 | bytes 62980096 | tf_op jit(solution)/shard_map/reduce_sum | solution.py:216
  1155.6 19.4 psum.38
  1175.2 406.7 %all-reduce.16.cloned.1.call-done = (f32[1024,1536]{1,0:T(8,128)}, f32[1024,1536]{1,0:T(8,128)}) async-done(((f32[1024,1536]{1,0:T(8,128)}, f32[1024,1536]{1,0:T(8,128)}), (f32[1024,1536]{1,0:T(8,128)}, f32[1024,1536]{1,0:T(8,128)})) %all-reduce.16.cloned.1.call-update) | async-done | bytes 12582928 | tf_op jit(solution)/shard_map/psum | solution.py:217
  1602.3 98.1 %while.29 = (s32[]{:T(128)}, f32[2,512,6,64]{1,0,3,2:T(2,128)}, f32[2,1024,128]{1,2,0:T(8,128)}, f32[2,1024,128]{2,1,0:T(8,128)}, bf16[2,1024,128]{1,2,0:T(8,128...) while((s32[]{:T(128)}, f32[2,512,6,64]{1,0,3,2:T(2,128)}, ...), condition=%wide.region_26.27_spmd.clone, body=%wide.region_24.26_spmd.clone.sunk | while | flops 2061307392 | bytes 197763888 | solution.py:264
  1636.6 15.0 dynamic_update_slice.37
  1746.4 20.1 fusion.92
  1768.8 20.1 fusion.90
  1790.7 20.2 fusion.91
  1813.4 70.1 %all-reduce.14.cloned.1.call-done = bf16[1024,1536]{1,0:T(8,128)(2,1)} async-done(((bf16[1024,1536]{1,0:T(8,128)(2,1)}), bf16[1024,1536]{1,0:T(8,128)(2,1)}) %all-reduce.14.cloned.1.call-update) | async-done | bytes 3145744 | tf_op jit(solution)/shard_map/psum | solution.py:285
  1887.6 24.1 %all-reduce.5 = (f32[1536]{0:T(1024)S(1)}, f32[1536]{0:T(1024)S(1)}) all-reduce(f32[1536]{0:T(1024)S(1)} %get-tuple-element.305, f32[1536]{0:T(1024)S(1)} %copy-done.61), channel_id=4, replica_groups=mesh['fsdp'=4,'ctx'=2,'tp'=4] {'fsdp','ctx'}, use_global_device_ids=true, to_apply=%region_32.33.clone | all-reduce | flops 3072 | bytes 24576
  1921.1 38.7 %reduce-scatter.21.cloned.1.call-done = f32[192,128]{1,0:T(8,128)} async-done(((f32[1536,128]{1,0:T(8,128)}), f32[192,128]{1,0:T(8,128)}) %reduce-scatter.21.cloned.1.call-update) | async-done | bytes 98320 | tf_op jit(solution)/shard_map/reduce_scatter | solution.py:295
  1959.8 46.3 %reduce-scatter.17.cloned.1.call-done = f32[192,384]{1,0:T(8,128)} async-done(((f32[1536,384]{1,0:T(8,128)}), f32[192,384]{1,0:T(8,128)}) %reduce-scatter.17.cloned.1.call-update) | async-done | bytes 294928 | tf_op jit(solution)/shard_map/reduce_scatter | solution.py:293
  2006.2 46.7 %reduce-scatter.23.cloned.1.call-done = f32[384,192]{0,1:T(8,128)} async-done(((f32[384,1536]{0,1:T(8,128)}), f32[384,192]{0,1:T(8,128)}) %reduce-scatter.23.cloned.1.call-update) | async-done | bytes 294928 | tf_op jit(solution)/shard_map/reduce_scatter | solution.py:296
  2052.8 96.4 %reduce-scatter.29.cloned.1.call-done = f32[16,128,192]{1,2,0:T(8,128)} async-done(((f32[16,128,1536]{1,2,0:T(8,128)}), f32[16,128,192]{1,2,0:T(8,128)}) %reduce-scatter.29.cloned.1.call-update) | async-done | bytes 1572880 | tf_op jit(solution)/shard_map/reduce_scatter | solution.py:303
  2149.2 96.4 %reduce-scatter.25.cloned.1.call-done = f32[16,192,128]{2,1,0:T(8,128)} async-done(((f32[16,1536,128]{2,1,0:T(8,128)}), f32[16,192,128]{2,1,0:T(8,128)}) %reduce-scatter.25.cloned.1.call-update) | async-done | bytes 1572880 | tf_op jit(solution)/shard_map/reduce_scatter | solution.py:301
  2245.5 96.4 %reduce-scatter.27.cloned.1.call-done = f32[16,192,128]{2,1,0:T(8,128)} async-done(((f32[16,1536,128]{2,1,0:T(8,128)}), f32[16,192,128]{2,1,0:T(8,128)}) %reduce-scatter.27.cloned.1.call-update) | async-done | bytes 1572880 | tf_op jit(solution)/shard_map/reduce_scatter | solution.py:302
  (357 shorter events, 300.9 us)
Async XLA Ops:
  7.2 63.9 %all-gather.7.cloned.1.call-start = ((), (), s32[]{:S(2)}) async-start(), calls=%async_computation.10 | async-start | bytes 1327104 | tf_op jit(solution)/shard_map/all_gather | solution.py:156
  7.9 95.7 %all-gather.9.cloned.1.call-start = ((), (), s32[]{:S(2)}) async-start(), calls=%async_computation.11 | async-start | bytes 1327104 | tf_op jit(solution)/shard_map/all_gather | solution.py:159
  8.7 324.9 %all-reduce.12.cloned.1.call-start = ((), (), s32[]{:S(2)}) async-start(), calls=%async_computation.12 | async-start | bytes 12582912 | tf_op jit(solution)/shard_map/psum | solution.py:193
  109.9 443.0 %all-gather.13.cloned.1.call-start = ((), (), s32[]{:S(2)}) async-start(), calls=%async_computation.14 | async-start | bytes 7077888 | tf_op jit(solution)/shard_map/all_gather | solution.py:204
  110.5 462.8 %all-gather.11.cloned.1.call-start = ((), (), s32[]{:S(2)}) async-start(), calls=%async_computation.13 | async-start | bytes 7077888 | tf_op jit(solution)/shard_map/all_gather | solution.py:203
  111.1 479.8 %all-gather.15.cloned.1.call-start = ((), (), s32[]{:S(2)}) async-start(), calls=%async_computation.15 | async-start | bytes 7077888 | tf_op jit(solution)/shard_map/all_gather | solution.py:205
  111.6 1470.3 %all-reduce.16.cloned.1.call-start = ((), (), s32[]{:S(2)}) async-start(), calls=%async_computation.27 | async-start | bytes 25165824 | tf_op jit(solution)/shard_map/psum | solution.py:217
  112.4 224.8 %copy-start.45 = (f32[1536]{0:T(1024)}, f32[1536]{0:T(1024)S(1)}, u32[]{:S(2)}) copy-start(f32[1536]{0:T(1024)S(1)} %convert_element_type.114) | copy-start | bytes 18436
  121.8 216.0 %copy-start.37 = (bf16[1536,16]{0,1:T(8,128)(2,1)}, bf16[1536,16]{0,1:T(8,128)(2,1)S(1)}, u32[]{:S(2)}) copy-start(bf16[1536,16]{0,1:T(8,128)(2,1)S(1)} %reshape.411) | copy-start | bytes 147460
  130.0 203.5 %copy-start.3 = (bf16[1024,1536]{1,0:T(8,128)(2,1)S(1)}, bf16[1024,1536]{1,0:T(8,128)(2,1)}, u32[]{:S(2)}) copy-start(bf16[1024,1536]{1,0:T(8,128)(2,1)} %param.17) | copy-start | bytes 9437188
  908.1 179.9 %copy-start.21 = (f32[1024,8]{1,0:T(8,128)S(1)}, f32[1024,8]{1,0:T(8,128)}, u32[]{:S(2)}) copy-start(f32[1024,8]{1,0:T(8,128)} %copy-done.20) | copy-start | bytes 98308
  1155.3 426.6 %copy-start.38 = (bf16[1536,16]{0,1:T(8,128)(2,1)S(1)}, bf16[1536,16]{0,1:T(8,128)(2,1)}, u32[]{:S(2)}) copy-start(bf16[1536,16]{0,1:T(8,128)(2,1)} %copy-done.37) | copy-start | bytes 147460
  1155.3 426.6 %copy-start.46 = (f32[1536]{0:T(1024)S(1)}, f32[1536]{0:T(1024)}, u32[]{:S(2)}) copy-start(f32[1536]{0:T(1024)} %copy-done.45) | copy-start | bytes 18436
  1155.3 426.6 %copy-start.50 = (f32[1024]{0:T(1024)S(1)}, f32[1024]{0:T(1024)}, u32[]{:S(2)}) copy-start(f32[1024]{0:T(1024)} %copy-done.49) | copy-start | bytes 12292
  1155.3 433.1 %slice-start.3 = ((s8[6291456]{0:T(1024)(128)(4,1)}), s8[2097152]{0:T(1024)(128)(4,1)S(1)}, s32[]{:S(2)}) async-start(s8[6291456]{0:T(1024)(128)(4,1)} %bitcast.294), calls=%async_computation.31 | async-start | bytes 4194304
  1155.4 557.7 %reduce-scatter.13.cloned.1.call-start = ((), (), s32[]{:S(2)}) async-start(), calls=%async_computation.16 | async-start | bytes 1572864 | tf_op jit(solution)/shard_map/reduce_scatter | solution.py:268
  1175.2 413.2 %copy-start.39 = (bf16[1024,16]{0,1:T(8,128)(2,1)}, bf16[1024,16]{0,1:T(8,128)(2,1)S(1)}, u32[]{:S(2)}) copy-start(bf16[1024,16]{0,1:T(8,128)(2,1)S(1)} %select_reduce_fusion) | copy-start | bytes 98308
  1602.3 99.0 %copy-start.40 = (bf16[1024,16]{0,1:T(8,128)(2,1)S(1)}, bf16[1024,16]{0,1:T(8,128)(2,1)}, u32[]{:S(2)}) copy-start(bf16[1024,16]{0,1:T(8,128)(2,1)} %copy-done.39) | copy-start | bytes 98308
  1700.5 20.3 reduce-scatter.15.cloned.1.call-start
  1701.2 110.5 %reduce-scatter.31.cloned.1.call-start = ((), (), s32[]{:S(2)}) async-start(), calls=%async_computation.26 | async-start | bytes 884736
  1705.5 178.0 %all-reduce.14.cloned.1.call-start = ((), (), s32[]{:S(2)}) async-start(), calls=%async_computation.18 | async-start | bytes 6291456 | tf_op jit(solution)/shard_map/psum | solution.py:285
  1730.1 191.0 %reduce-scatter.19.cloned.1.call-start = ((), (), s32[]{:S(2)}) async-start(), calls=%async_computation.20 | async-start | bytes 884736 | tf_op jit(solution)/shard_map/reduce_scatter | solution.py:294
  1732.1 227.7 %reduce-scatter.21.cloned.1.call-start = ((), (), s32[]{:S(2)}) async-start(), calls=%async_computation.21 | async-start | bytes 884736 | tf_op jit(solution)/shard_map/reduce_scatter | solution.py:295
  1735.0 271.1 %reduce-scatter.17.cloned.1.call-start = ((), (), s32[]{:S(2)}) async-start(), calls=%async_computation.19 | async-start | bytes 2654208 | tf_op jit(solution)/shard_map/reduce_scatter | solution.py:293
  1739.6 313.2 %reduce-scatter.23.cloned.1.call-start = ((), (), s32[]{:S(2)}) async-start(), calls=%async_computation.22 | async-start | bytes 2654208 | tf_op jit(solution)/shard_map/reduce_scatter | solution.py:296
  1746.4 402.8 %reduce-scatter.29.cloned.1.call-start = ((), (), s32[]{:S(2)}) async-start(), calls=%async_computation.25 | async-start | bytes 14155776 | tf_op jit(solution)/shard_map/reduce_scatter | solution.py:303
  1766.6 478.9 %reduce-scatter.25.cloned.1.call-start = ((), (), s32[]{:S(2)}) async-start(), calls=%async_computation.23 | async-start | bytes 14155776 | tf_op jit(solution)/shard_map/reduce_scatter | solution.py:301
  1788.9 553.0 %reduce-scatter.27.cloned.1.call-start = ((), (), s32[]{:S(2)}) async-start(), calls=%async_computation.24 | async-start | bytes 14155776 | tf_op jit(solution)/shard_map/reduce_scatter | solution.py:302
  1810.8 72.6 %copy-start.4 = (bf16[1024,1536]{1,0:T(8,128)(2,1)S(1)}, bf16[1024,1536]{1,0:T(8,128)(2,1)}, u32[]{:S(2)}) copy-start(bf16[1024,1536]{1,0:T(8,128)(2,1)} %param.17) | copy-start | bytes 9437188
  1810.8 72.6 %copy-start.44 = (f32[1536]{0:T(1024)S(1)}, f32[1536]{0:T(1024)}, u32[]{:S(2)}) copy-start(f32[1536]{0:T(1024)} %copy-done.43) | copy-start | bytes 18436
  1810.8 72.6 %copy-start.54 = (f32[1024]{0:T(1024)S(1)}, f32[1024]{0:T(1024)}, u32[]{:S(2)}) copy-start(f32[1024]{0:T(1024)} %copy-done.53) | copy-start | bytes 12292
  1810.9 76.8 %copy-start.61 = (f32[1536]{0:T(1024)S(1)}, f32[1536]{0:T(1024)}, u32[]{:S(2)}) copy-start(f32[1536]{0:T(1024)} %get-tuple-element.303) | copy-start | bytes 18436
  (59 other events, 568.5 us)
Sparse Core Ops, SparseCore 0:
  9.9 27.1 all-gather.6
  38.9 24.2 all-gather.8
  110.0 223.5 all-reduce.11
  335.3 44.4 all-gather.12
  381.5 45.5 all-gather.10
  428.9 45.5 all-gather.14
  1155.5 426.3 all-reduce.15
  1700.6 7.4 reduce-scatter.12
  1711.0 9.6 reduce-scatter.14
  1723.8 36.1 reduce-scatter.30
  1762.3 121.0 all-reduce.13
  1887.0 33.9 reduce-scatter.18
  1924.8 34.9 reduce-scatter.20
  1963.6 42.5 reduce-scatter.16
  2010.3 42.4 reduce-scatter.22
  2056.8 92.3 reduce-scatter.28
  2153.1 92.3 reduce-scatter.24
  2249.5 92.3 reduce-scatter.26
where the time goes:
time: 2370 us; the launch traced here: 2350 us
  waiting for transfers between devices  1060 us (45%)
  local copies, waits for them, and re-layouts  664 us (28%)
  matrix products  328 us (14%)
  other arithmetic  181 us (8%)
  blocking collectives  93.3 us (4%)
    psum x1, waiting for transfers between devices, per_device(): moe_total, gate_dots = lax.psum((moe_part, dots_part), 'tp')  407 us
    gather x1, local copies, waits for them, and re-layouts, per_device(): buffer_grad.reshape(E * capacity, -1)[where_rows].reshape(rows, TOPK, -1)  180 us
    gather x1, local copies, waits for them, and re-layouts, per_device(): part_out.reshape(E * capacity, -1)[where_rows].reshape(rows, TOPK, -1)  180 us
    psum x1, waiting for transfers between devices, per_device(): head_total = lax.psum(head_part, 'tp')  157 us
    scatter x2, local copies, waits for them, and re-layouts, per_device(): out_grad = jnp.zeros((E * capacity, slot_rows.shape[1]), bf16).at[where_r...  146 us
    reduce_scatter x1, waiting for transfers between devices, per_device(): lax.psum_scatter(grad_down, ('fsdp', 'ctx'), scatter_dimension=2, tiled=T...  96.4 us
    reduce_scatter x1, waiting for transfers between devices, per_device(): lax.psum_scatter(grad_up, ('fsdp', 'ctx'), scatter_dimension=1, tiled=True)  96.4 us
    reduce_scatter x1, waiting for transfers between devices, per_device(): lax.psum_scatter(grad_gate, ('fsdp', 'ctx'), scatter_dimension=1, tiled=T...  96.4 us
  transfers between devices with their start and end apart: 18, of which 11 were waited for; matrix products, arithmetic and copies ran while one was open for 20% of the time, Pallas kernels for 0%

commit v1 on v0

v1 whole, which is shorter than its diff:
```python
import math

import jax
import jax.numpy as jnp
from jax import lax
from jax.sharding import PartitionSpec as P

HEAD_SIZE = 64
TOPK = 8
E = 16
SEQUENCE_LENGTH = 1024


epsilon = 1e-06


def placed(ranks, half):
    quarter = half // 2
    steps = jnp.arange(half, dtype=jnp.int32)
    early = ranks * quarter + steps
    late = SEQUENCE_LENGTH - (ranks + 1) * quarter + steps - quarter
    return jnp.where(steps < quarter, early, late)


def angle_tables(token_places):
    halfway = HEAD_SIZE // 2
    freqs = jnp.exp(jnp.arange(halfway, dtype=jnp.float32) * (-2.0 * math.log(10000.0) / HEAD_SIZE))
    angles = token_places.astype(jnp.float32)[:, None] * freqs[None, :]
    return (jnp.cos(angles)[:, None, :], jnp.sin(angles)[:, None, :])


def rotary_embed(vectors, token_places):
    cosine, sine = angle_tables(token_places)
    halfway = HEAD_SIZE // 2
    lower = vectors[..., :halfway]
    upper = vectors[..., halfway:]
    return jnp.concatenate([lower * cosine - upper * sine, upper * cosine + lower * sine], -1)


def rotary_back(grads, token_places):
    cosine, sine = angle_tables(token_places)
    halfway = HEAD_SIZE // 2
    lower = grads[..., :halfway]
    upper = grads[..., halfway:]
    return jnp.concatenate([lower * cosine + upper * sine, upper * cosine - lower * sine], -1)


def norm_back(value_rows, scale, gain, grad):
    scaled = grad * gain
    inner = jnp.mean(scaled * value_rows, -1, keepdims=True)
    return (
        scale * scaled - value_rows * scale * scale * scale * inner,
        jnp.sum(grad * value_rows * scale, 0),
    )


def score_block(grouped_heads, keyed_rows, q_places, k_places):
    scores = jnp.einsum(
        "qkgd,skd->kgqs", grouped_heads, keyed_rows, preferred_element_type=jnp.float32
    ) * (1.0 / math.sqrt(HEAD_SIZE))
    allowed = k_places[None, :] <= q_places[:, None]
    return jnp.where(allowed, scores, -1e30)


def attend(query_rows, key_rows, value_rows, q_places, k_places):
    kv_here = key_rows.shape[-1] // HEAD_SIZE
    q_len = query_rows.shape[0]
    grouped_heads = query_rows.reshape(q_len, kv_here, -1, HEAD_SIZE)
    keyed_rows = key_rows.reshape(-1, kv_here, HEAD_SIZE)
    valued_rows = value_rows.reshape(-1, kv_here, HEAD_SIZE)
    scores = score_block(grouped_heads, keyed_rows, q_places, k_places)
    top = jnp.max(scores, -1, keepdims=True)
    weights = jnp.exp(scores - top)
    total = jnp.sum(weights, -1, keepdims=True)
    probs = (weights / total).astype(jnp.bfloat16)
    mixed = jnp.einsum("kgqs,skd->qkgd", probs, valued_rows, preferred_element_type=jnp.float32)
    return (mixed.reshape(q_len, -1), top + jnp.log(total))


def attend_back(query_rows, key_rows, value_rows, log_total, mixed_grad, q_places, k_places):
    kv_here = key_rows.shape[-1] // HEAD_SIZE
    q_len = query_rows.shape[0]
    k_len = key_rows.shape[0]
    grouped_heads = query_rows.reshape(q_len, kv_here, -1, HEAD_SIZE)
    keyed_rows = key_rows.reshape(k_len, kv_here, HEAD_SIZE)
    valued_rows = value_rows.reshape(k_len, kv_here, HEAD_SIZE)
    out_grouped = mixed_grad.reshape(q_len, kv_here, -1, HEAD_SIZE)
    scores = score_block(grouped_heads, keyed_rows, q_places, k_places)
    probs = jnp.exp(scores - log_total)
    prob_grad = jnp.einsum(
        "qkgd,skd->kgqs", out_grouped, valued_rows, preferred_element_type=jnp.float32
    )
    score_grad = (probs * (prob_grad - jnp.sum(probs * prob_grad, -1, keepdims=True))).astype(
        jnp.bfloat16
    )
    factor = 1.0 / math.sqrt(HEAD_SIZE)
    query_grad = (
        jnp.einsum("kgqs,skd->qkgd", score_grad, keyed_rows, preferred_element_type=jnp.float32)
        * factor
    )
    key_grad = (
        jnp.einsum("kgqs,qkgd->skd", score_grad, grouped_heads, preferred_element_type=jnp.float32)
        * factor
    )
    value_grad = jnp.einsum(
        "kgqs,qkgd->skd",
        probs.astype(jnp.bfloat16),
        out_grouped,
        preferred_element_type=jnp.float32,
    )
    return (
        query_grad.reshape(q_len, -1, HEAD_SIZE),
        key_grad.reshape(k_len, -1),
        value_grad.reshape(k_len, -1),
    )


def per_device(
    tokens,
    routes,
    gain_attn,
    w_query,
    key_matrix,
    value_matrix,
    w_out,
    gain_moe,
    w_router,
    w_gate,
    w_up,
    w_down,
    cotangent,
):
    f32 = jnp.float32
    bf16 = jnp.bfloat16
    rows, width = tokens.shape
    ctx_count = lax.axis_size("ctx")
    half = SEQUENCE_LENGTH // ctx_count
    seq_here = rows // half
    both = ("fsdp", "ctx")
    local_places = placed(lax.axis_index("ctx"), half)
    all_places = placed(jnp.arange(ctx_count, dtype=jnp.int32)[:, None], half).reshape(-1)
    q_wide, k_wide, o_wide = w_query.shape[1], key_matrix.shape[1], w_out.shape[0]
    small = jnp.concatenate(
        [
            w_query,
            key_matrix,
            value_matrix,
            w_out.T,
            w_router,
            gain_attn[:, None],
            gain_moe[:, None],
        ],
        1,
    )
    cuts = (q_wide, k_wide, k_wide, o_wide, E, 1, 1)
    pad = -small.shape[1] % 128
    small = jnp.pad(small, ((0, 0), (0, pad)))
    small_full = lax.all_gather(small, both, axis=0, tiled=True)
    qkv_wide = q_wide + 2 * k_wide
    qkv_w = small_full[:, :qkv_wide]
    out_wt = small_full[:, qkv_wide : qkv_wide + o_wide]
    router_w = small_full[:, qkv_wide + o_wide : qkv_wide + o_wide + E]
    gain_one_f = small_full[:, qkv_wide + o_wide + E].astype(f32)
    gain_two_f = small_full[:, qkv_wide + o_wide + E + 1].astype(f32)
    gate_up = jnp.concatenate([w_gate, w_up], -1)
    gate_up_full = lax.all_gather(gate_up, both, axis=1, tiled=True)
    down_full = lax.all_gather(jnp.swapaxes(w_down, 1, 2), both, axis=1, tiled=True)
    inputs = tokens.astype(f32)
    scale_one = lax.rsqrt(jnp.mean(inputs * inputs, -1, keepdims=True) + epsilon)
    normed = (inputs * scale_one * gain_one_f).astype(bf16)
    heads_here = q_wide // HEAD_SIZE
    kv_here = k_wide // HEAD_SIZE
    qkv = jnp.dot(normed, qkv_w, preferred_element_type=f32)
    rot = (
        rotary_embed(
            qkv[:, : q_wide + k_wide].reshape(seq_here, half, heads_here + kv_here, HEAD_SIZE),
            local_places,
        )
        .astype(bf16)
        .reshape(seq_here, half, q_wide + k_wide)
    )
    query_rot = rot[:, :, :q_wide]
    key_value = jnp.concatenate(
        [rot[:, :, q_wide:], qkv[:, q_wide + k_wide :].astype(bf16).reshape(seq_here, half, -1)], -1
    )
    kv_all = lax.all_gather(key_value, "ctx", axis=1, tiled=True)
    keys_all, values_all = kv_all[:, :, :k_wide], kv_all[:, :, k_wide:]

    def forward_one(pieces):
        return attend(pieces[0], pieces[1], pieces[2], local_places, all_places)

    mixed, log_total = lax.map(forward_one, (query_rot, keys_all, values_all))
    mixed_low = mixed.reshape(rows, q_wide).astype(bf16)
    head_part = lax.dot_general(
        mixed_low, out_wt, (((1,), (1,)), ((), ())), preferred_element_type=f32
    )
    head_total = lax.psum(head_part.astype(bf16), "tp").astype(f32)
    state = inputs + head_total
    scale_two = lax.rsqrt(jnp.mean(state * state, -1, keepdims=True) + epsilon)
    normed_two = (state * scale_two * gain_two_f).astype(bf16)
    logits = jnp.dot(normed_two, router_w, preferred_element_type=f32)
    named = jnp.any(routes[:, :, None] == jnp.arange(E, dtype=jnp.int32)[None, None, :], 1)
    top = jnp.max(jnp.where(named, logits, -jnp.inf), -1, keepdims=True)
    raised = jnp.where(named, jnp.exp(jnp.where(named, logits, top) - top), 0.0)
    gates = raised / jnp.sum(raised, -1, keepdims=True)
    upstream = cotangent.astype(f32)

    ffn = w_gate.shape[2]
    gu = jnp.einsum("td,edf->etf", normed_two, gate_up_full, preferred_element_type=f32)
    gate_pre, up_pre = gu[:, :, :ffn], gu[:, :, ffn:]
    sigma = jax.nn.sigmoid(gate_pre)
    hidden = (gate_pre * sigma * up_pre).astype(bf16).astype(f32)
    gate_e = gates.T[:, :, None]
    hidden_gated = (gate_e * hidden).astype(bf16)
    moe_part = jnp.einsum("etf,edf->td", hidden_gated, down_full, preferred_element_type=f32)
    raw = jnp.einsum("td,edf->etf", cotangent, down_full, preferred_element_type=f32)
    dots_part = jnp.sum(hidden * raw, -1).T
    moe_total = lax.psum(moe_part.astype(bf16), "tp").astype(f32)
    gate_dots = lax.psum(dots_part, "tp")
    activations = (state + moe_total).astype(bf16)
    gate_dots = jnp.where(named, gate_dots, 0.0)
    mix_grad = gates * (gate_dots - jnp.sum(gates * gate_dots, -1, keepdims=True))
    logit_grad = mix_grad.astype(bf16)
    hidden_grad = raw * gate_e
    gate_grad = (hidden_grad * up_pre * sigma * (1.0 + gate_pre * (1.0 - sigma))).astype(bf16)
    up_grad = (hidden_grad * gate_pre * sigma).astype(bf16)
    gu_grad = jnp.concatenate([gate_grad, up_grad], -1)
    normed_two_part = jnp.einsum("etf,edf->td", gu_grad, gate_up_full, preferred_element_type=f32)
    normed_two_grad = lax.psum(normed_two_part.astype(bf16), "tp").astype(f32)
    grad_gu = jnp.einsum("td,etf->edf", normed_two, gu_grad, preferred_element_type=f32)
    grad_dn = jnp.einsum("td,etf->edf", cotangent, hidden_gated, preferred_element_type=f32)
    grad_gu = lax.psum_scatter(grad_gu.astype(bf16), both, scatter_dimension=1, tiled=True)
    grad_dn = lax.psum_scatter(grad_dn.astype(bf16), both, scatter_dimension=1, tiled=True)
    grad_gu = grad_gu.astype(f32)
    grad_dn = jnp.swapaxes(grad_dn.astype(f32), 1, 2)

    normed_two_grad = normed_two_grad + jnp.einsum(
        "te,de->td", logit_grad, router_w, preferred_element_type=f32
    )
    grad_router = jnp.einsum("td,te->de", normed_two, logit_grad, preferred_element_type=f32)
    state_delta, grad_gain_two = norm_back(state, scale_two, gain_two_f, normed_two_grad)
    state_grad = upstream + state_delta
    state_low = state_grad.astype(bf16)
    grad_out = jnp.einsum("td,tc->dc", state_low, mixed_low, preferred_element_type=f32)
    mixed_grad = jnp.dot(state_low, out_wt, preferred_element_type=f32).astype(bf16)
    mixed_grad = mixed_grad.reshape(seq_here, half, heads_here, HEAD_SIZE)

    def backward_one(pieces):
        return attend_back(
            pieces[0], pieces[1], pieces[2], pieces[3], pieces[4], local_places, all_places
        )

    query_rot4 = query_rot.reshape(seq_here, half, heads_here, HEAD_SIZE)
    query_grad, key_grad, value_grad = lax.map(
        backward_one, (query_rot4, keys_all, values_all, log_total, mixed_grad)
    )
    kv_grad = jnp.concatenate([key_grad, value_grad], -1)
    kv_grad = lax.psum_scatter(kv_grad, "ctx", scatter_dimension=1, tiled=True)
    key_grad, value_grad = kv_grad[:, :, :k_wide], kv_grad[:, :, k_wide:]
    qk_grad = jnp.concatenate(
        [query_grad, key_grad.reshape(seq_here, half, kv_here, HEAD_SIZE)], 2
    )
    qkv_low = jnp.concatenate(
        [
            rotary_back(qk_grad, local_places).reshape(rows, q_wide + k_wide),
            value_grad.reshape(rows, k_wide),
        ],
        1,
    ).astype(bf16)
    normed_part = lax.dot_general(
        qkv_low, qkv_w, (((1,), (1,)), ((), ())), preferred_element_type=f32
    )
    normed_grad = lax.psum(normed_part.astype(bf16), "tp").astype(f32)
    input_delta, grad_gain_one = norm_back(inputs, scale_one, gain_one_f, normed_grad)
    input_grad = (state_grad + input_delta).astype(bf16)
    grad_qkv = jnp.einsum("td,tc->dc", normed, qkv_low, preferred_element_type=f32)
    grad_small = jnp.concatenate(
        [grad_qkv, grad_out, grad_router, grad_gain_one[:, None], grad_gain_two[:, None]], 1
    ).astype(bf16)
    grad_small = jnp.pad(grad_small, ((0, 0), (0, pad)))
    grad_small = lax.psum_scatter(grad_small, both, scatter_dimension=0, tiled=True).astype(f32)
    parts, at = [], 0
    for wide in cuts:
        parts.append(grad_small[:, at : at + wide])
        at += wide
    return (
        activations,
        input_grad,
        parts[5][:, 0],
        parts[0],
        parts[1],
        parts[2],
        parts[3].T,
        parts[6][:, 0],
        parts[4],
        grad_gu[:, :, :ffn],
        grad_gu[:, :, ffn:],
        grad_dn,
    )


def solution(mesh):
    placed = (
        P(("fsdp", "ctx"), None),
        P(("fsdp", "ctx"), None),
        P(("fsdp", "ctx")),
        P(("fsdp", "ctx"), "tp"),
        P(("fsdp", "ctx"), "tp"),
        P(("fsdp", "ctx"), "tp"),
        P("tp", ("fsdp", "ctx")),
        P(("fsdp", "ctx")),
        P(("fsdp", "ctx"), None),
        P(None, ("fsdp", "ctx"), "tp"),
        P(None, ("fsdp", "ctx"), "tp"),
        P(None, "tp", ("fsdp", "ctx")),
        P(("fsdp", "ctx"), None),
    )
    return jax.shard_map(
        per_device,
        mesh=mesh,
        in_specs=placed,
        out_specs=(
            P(("fsdp", "ctx"), None),
            P(("fsdp", "ctx"), None),
            P(("fsdp", "ctx")),
            P(("fsdp", "ctx"), "tp"),
            P(("fsdp", "ctx"), "tp"),
            P(("fsdp", "ctx"), "tp"),
            P("tp", ("fsdp", "ctx")),
            P(("fsdp", "ctx")),
            P(("fsdp", "ctx"), None),
            P(None, ("fsdp", "ctx"), "tp"),
            P(None, ("fsdp", "ctx"), "tp"),
            P(None, "tp", ("fsdp", "ctx")),
        ),
        check_vma=False,
    )
```

time: 2370 us -> 1130 us (0.48)
  local copies, waits for them, and re-layouts: 664 us -> 147 us
  waiting for transfers between devices: 1060 us -> 706 us
  matrix products: 328 us -> 185 us
  other arithmetic: 181 us -> 62.2 us
  blocking collectives: 93.3 us -> 0 us
    gather x3 -> x0, local copies, waits for them, and re-layouts: 406 us -> none  [the longest x1 180 us: per_device(): buffer_grad.reshape(E * capacity, -1)[where_rows].reshape(rows, TOPK, -1)]
    reduce_scatter x9 -> x3, waiting for transfers between devices: 425 us -> 118 us  [the longest x1 84.9 us: per_device(): lax.psum_scatter(grad_gu.astype(bf16), both, scatter_dimension=1, tiled=T...]
    psum x3 -> x4, waiting for transfers between devices: 634 us -> 406 us  [the longest x1 152 us: per_device(): moe_total = lax.psum(moe_part.astype(bf16), 'tp').astype(f32)]
    scatter x3 -> x0, local copies, waits for them, and re-layouts: 176 us -> none  [the longest x2 146 us: per_device(): out_grad = jnp.zeros((E * capacity, slot_rows.shape[1]), bf16).at[where_r...]
    dot_general x21 -> x13, matrix products: 264 us -> 127 us  [the longest x1 20.5 us: per_device(): jnp.einsum('td,edf->etf', normed_two, gate_up_full, preferred_element_typ...]
    all_gather x5 -> x4, waiting for transfers between devices: 0.03 us -> 133 us  [the longest x1 65.4 us: per_device(): gate_up_full = lax.all_gather(gate_up, both, axis=1, tiled=True)]
    reduce_sum x6 -> x1, other arithmetic: 89.6 us -> 0.03 us  [per_device(): gates = raised / jnp.sum(raised, -1, keepdims=True)]
    unnamed x19 -> x13, waiting for transfers between devices: 3.85 us -> 47.7 us
  transfers between devices with their start and end apart: 18 -> 12, of which waited for: 11 -> 11; matrix products, arithmetic and copies ran while one was open for 20% -> 16% of each run, Pallas kernels for 0% -> 0%
where the time goes in v1:
time: 1130 us; the launch traced here: 1120 us
  waiting for transfers between devices  706 us (62%)
  matrix products  185 us (16%)
  local copies, waits for them, and re-layouts  147 us (13%)
  other arithmetic  62.2 us (6%)
  between operations  15.1 us (1%)
    psum x1, waiting for transfers between devices, per_device(): moe_total = lax.psum(moe_part.astype(bf16), 'tp').astype(f32)  152 us
    psum x1, waiting for transfers between devices, per_device(): normed_two_grad = lax.psum(normed_two_part.astype(bf16), 'tp').astype(f32)  122 us
    psum x1, waiting for transfers between devices, per_device(): head_total = lax.psum(head_part.astype(bf16), 'tp').astype(f32)  118 us
    reduce_scatter x1, waiting for transfers between devices, per_device(): lax.psum_scatter(grad_gu.astype(bf16), both, scatter_dimension=1, tiled=T...  84.9 us
    all_gather x1, waiting for transfers between devices, per_device(): gate_up_full = lax.all_gather(gate_up, both, axis=1, tiled=True)  65.4 us
    unnamed x13, waiting for transfers between devices  47.7 us
    dynamic_update_slice x10, local copies, waits for them, and re-layouts, per_device(): lax.map(backward_one, (query_rot4, keys_all, values_all, log_total, mixed...  34.4 us
    all_gather x1, waiting for transfers between devices, per_device(): small_full = lax.all_gather(small, both, axis=0, tiled=True)  33.8 us
  transfers between devices with their start and end apart: 12, of which 11 were waited for; matrix products, arithmetic and copies ran while one was open for 16% of the time, Pallas kernels for 0%

profile of v1, /device:TPU:0, one launch (start us, length us, event | category | flops | bytes accessed | tf_op | source)
XLA Modules:
  0.0 1117.7 jit_solution(2756204936464496673)
XLA Ops:
  16.5 33.8 %all-gather.5.cloned.1.call-done = bf16[1536,1152]{1,0:T(8,128)(2,1)} async-done(((bf16[192,1152]{1,0:T(8,128)(2,1)}), bf16[1536,1152]{1,0:T(8,128)(2,1)}) %all-gather.5.cloned.1.call-update) | async-done | bytes 3538960 | tf_op jit(solution)/shard_map/all_gather | solution.py:158
  67.0 7.3 all-gather.7.cloned.1.call-done
  76.4 23.5 %while.28 = (s32[]{:T(128)}, bf16[2,512,384]{2,1,0:T(8,128)(2,1)S(1)}, f32[2,2,3,512,1]{3,2,1,4,0:T(4,128)}, bf16[2,1024,128]{1,2,0:T(8,128)(2,1)}, bf16[2,1024,...) while((s32[]{:T(128)}, ...), condition=%wide.region_4.5_spmd.clone, body=%wide.region_1.4_spmd.clone.sunk | while | flops 843582976 | bytes 44688036 | solution.py:192
  110.0 118.2 %all-reduce.8.cloned.1.call-done = bf16[1024,1536]{1,0:T(8,128)(2,1)} async-done(((bf16[1024,1536]{1,0:T(8,128)(2,1)}), bf16[1024,1536]{1,0:T(8,128)(2,1)}) %all-reduce.8.cloned.1.call-update) | async-done | bytes 3145744 | tf_op jit(solution)/shard_map/psum | solution.py:197
  236.3 65.4 %all-gather.9.cloned.1.call-done = bf16[16,1536,256]{2,1,0:T(8,128)(2,1)} async-done(((bf16[16,192,256]{2,1,0:T(8,128)(2,1)}), bf16[16,1536,256]{2,1,0:T(8,128)(2,1)}) %all-gather.9.cloned.1.call-update) | async-done | bytes 12582928 | tf_op jit(solution)/shard_map/all_gather | solution.py:166
  301.7 20.5 %convolution_bitcast_fusion.1 = f32[16,1024,256]{1,2,0:T(8,128)} fusion(bf16[16,1536,256]{2,1,0:T(8,128)(2,1)} %all-gather.9.cloned.1.call-done, bf16[1024,1536]{1,0:T(8,128)(2,1)} %copy-done.9), kind=kOutput, calls=%fused_computation.65 | convolution fusion | flops 12884901888 | bytes 32505856 | tf_op jit(solution)/shard_map/td,edf->etf/dot_general | solution.py:209
  322.2 26.8 %all-gather.11.cloned.1.call-done = bf16[16,1536,128]{2,1,0:T(8,128)(2,1)} async-done(((bf16[16,192,128]{2,1,0:T(8,128)(2,1)}), bf16[16,1536,128]{2,1,0:T(8,128)(2,1)}) %all-gather.11.cloned.1.call-update) | async-done | bytes 6291472 | tf_op jit(solution)/shard_map/all_gather | solution.py:167
  349.0 19.8 %multiply_convert_fusion.1 = (bf16[16,1024,128]{1,2,0:T(8,128)(2,1)}, bf16[16,1024,128]{1,2,0:T(8,128)(2,1)}, f32[16,1024]{1,0:T(8,128)}, bf16[16,1024,128]{1,2,0:T(8,128)(2,1)}) fusion(f32[16,1024,256]{1,2,0:T(8,128)} %convolution_bitcast_fusion.1, f32[16,1024]{1,0:T(8,128)S(1)} %fusion.76, bf16[16,1536,128]{2,1,0:T(8,128)(2,1)} %all-gather.11.cloned.1.call-done, ...), kind=kOutput, calls=%fused_computation.71 | convolution fusion | flops 6484377600 | bytes 38928384 | tf_op jit(solution)/shard_map/td,edf->etf/dot_general | solution.py:216
  368.8 19.4 %bitcast_convert_fusion = bf16[1024,1536]{1,0:T(8,128)(2,1)} fusion(bf16[16,1536,256]{2,1,0:T(8,128)(2,1)} %all-gather.9.cloned.1.call-done, bf16[16,1024,128]{1,2,0:T(8,128)(2,1)} %get-tuple-element.360, bf16[16,1024,128]{1,2,0:T(8,128)(2,1)} %get-tuple-element.359), kind=kOutput, calls=%fused_computation.88 | convolution fusion | flops 12903251968 | bytes 24117248 | tf_op jit(solution)/shard_map/etf,edf->td/dot_general | solution.py:228
  388.3 14.6 %all-reduce.12.cloned.1.call-done = f32[1024,16]{0,1:T(8,128)} async-done(((f32[1024,16]{0,1:T(8,128)}), f32[1024,16]{0,1:T(8,128)}) %all-reduce.12.cloned.1.call-update) | async-done | bytes 65552 | tf_op jit(solution)/shard_map/psum | solution.py:219
  404.7 122.1 %all-reduce.10.cloned.1.call-done = bf16[1024,1536]{1,0:T(8,128)(2,1)} async-done(((bf16[1024,1536]{1,0:T(8,128)(2,1)}), bf16[1024,1536]{1,0:T(8,128)(2,1)}) %all-reduce.10.cloned.1.call-update) | async-done | bytes 3145744 | tf_op jit(solution)/shard_map/psum | solution.py:229
  526.8 5.6 multiply_reduce_fusion
  543.0 101.4 %while.29 = (s32[]{:T(128)}, f32[2,512,6,64]{1,0,3,2:T(2,128)}, f32[2,1024,128]{2,1,0:T(8,128)}, f32[2,1024,128]{2,1,0:T(8,128)}, bf16[2,1024,128]{1,2,0:T(8,128...) while((s32[]{:T(128)}, f32[2,512,6,64]{1,0,3,2:T(2,128)}, ...), condition=%wide.region_18.19_spmd.clone, body=%wide.region_16.18_spmd.clone.sunk | while | flops 2061307392 | bytes 211395344 | solution.py:254
  554.2 11.1 fusion.153
  566.7 6.9 fusion.154
  577.8 15.0 %dynamic_update_slice.35 = f32[2,512,6,64]{1,0,3,2:T(2,128)} dynamic-update-slice(f32[2,512,6,64]{1,0,3,2:T(2,128)} %get-tuple-element.603, f32[1,512,6,64]{1,0,3,2:T(1,128)S(1)} %copy.180, s32[]{:T(128)S(6)} %copy.204, s32[]{:T(128)} %constant.45.clone.1..sunk, s32[]{:T(128)} %constant.45.clone.1..sunk, s32[]{:T(128)} %constant.45.clone.1..sunk) | dynamic-update-slice | bytes 1572868 | tf_op jit(solution)/shard_map/while/body/jit(dynamic_update_index_in_dim)/dynamic_update_slice | solution.py:254
  604.7 11.1 fusion.153
  617.2 6.9 fusion.154
  628.3 15.0 %dynamic_update_slice.35 = f32[2,512,6,64]{1,0,3,2:T(2,128)} dynamic-update-slice(f32[2,512,6,64]{1,0,3,2:T(2,128)} %get-tuple-element.603, f32[1,512,6,64]{1,0,3,2:T(1,128)S(1)} %copy.180, s32[]{:T(128)S(6)} %copy.204, s32[]{:T(128)} %constant.45.clone.1..sunk, s32[]{:T(128)} %constant.45.clone.1..sunk, s32[]{:T(128)} %constant.45.clone.1..sunk) | dynamic-update-slice | bytes 1572868 | tf_op jit(solution)/shard_map/while/body/jit(dynamic_update_index_in_dim)/dynamic_update_slice | solution.py:254
  647.5 11.6 %bitcast_convert_fusion.1 = bf16[1024,1536]{1,0:T(8,128)(2,1)} fusion(bf16[16,1536,128]{2,1,0:T(8,128)(2,1)} %all-gather.11.cloned.1.call-done, bf16[16,1024,128]{1,2,0:T(8,128)(2,1)} %get-tuple-element.362, f32[16,1024]{1,0:T(8,128)S(1)} %copy-done.29), kind=kOutput, calls=%fused_computation.89 | convolution fusion | flops 6450315264 | bytes 13697024 | tf_op jit(solution)/shard_map/etf,edf->td/dot_general | solution.py:215
  672.1 10.8 convert_bitcast_fusion
  682.9 9.1 copy.126
  693.9 19.6 %fusion.31 = bf16[16,1536,256]{1,2,0:T(8,128)(2,1)} fusion(bf16[16,1024,128]{1,2,0:T(8,128)(2,1)} %get-tuple-element.360, bf16[16,1024,128]{1,2,0:T(8,128)(2,1)} %get-tuple-element.359, bf16[1024,1536]{1,0:T(8,128)(2,1)S(1)} %copy-done.10), kind=kOutput, calls=%fused_computation.62 | convolution fusion | flops 12907970560 | bytes 24117248 | tf_op jit(solution)/shard_map/td,etf->edf/dot_general | solution.py:230
  713.5 17.1 %copy.125 = bf16[16,1536,256]{2,0,1:T(8,128)(2,1)} copy(bf16[16,1536,256]{1,2,0:T(8,128)(2,1)} %fusion.31) | data formatting | bytes 25165824 | tf_op jit(solution)/shard_map/convert_element_type | solution.py:232
  731.9 5.6 convolution_convert_fusion.4
  741.1 151.5 %all-reduce.14.cloned.1.call-done = (bf16[1024,1536]{1,0:T(8,128)(2,1)}, bf16[1024,1536]{1,0:T(8,128)(2,1)}) async-done(((bf16[1024,1536]{1,0:T(8,128)(2,1)}, bf16[1024,1536]{1,0:T(8,128)(2,1)}), (bf16[1024,1536]{1,0:T(8,128)(2,1)}, bf16[1024,1536]{1,0:T(8,128)(2,1)})) %all-reduce.14.cloned.1.call-update) | async-done | bytes 6291472 | tf_op jit(solution)/shard_map/psum | solution.py:218
  897.0 16.3 %concatenate.43 = bf16[1536,1042]{0,1:T(8,128)(2,1)} concatenate(bf16[1536,640]{0,1:T(8,128)(2,1)} %convolution_convert_fusion.3, bf16[1536,384]{0,1:T(8,128)(2,1)} %convolution_convert_fusion.4, bf16[1536,16]{0,1:T(8,128)(2,1)S(1)} %convolution_convert_fusion.5, bf16[1536,1]{0,1:T(2,128)(2,1)S(1)} %broadcast_in_dim.117, bf16[1536,1]{0,1:T(2,128)(2,1)S(1)} %broadcast_in_dim.118), dimensions={1} | concatenate | bytes 6402048 | tf_op jit(solution)/shard_map/concatenate | solution.py:277
  913.3 5.4 copy.167
  923.1 33.5 %reduce-scatter.11.cloned.1.call-done = bf16[16,192,128]{2,0,1:T(8,128)(2,1)} async-done(((bf16[16,1536,128]{2,0,1:T(8,128)(2,1)}), bf16[16,192,128]{2,0,1:T(8,128)(2,1)}) %reduce-scatter.11.cloned.1.call-update) | async-done | bytes 786448 | tf_op jit(solution)/shard_map/reduce_scatter | solution.py:233
  959.6 8.4 fusion.42
  968.0 84.9 %reduce-scatter.9.cloned.1.call-done = bf16[16,192,256]{2,0,1:T(8,128)(2,1)} async-done(((bf16[16,1536,256]{2,0,1:T(8,128)(2,1)}), bf16[16,192,256]{2,0,1:T(8,128)(2,1)}) %reduce-scatter.9.cloned.1.call-update) | async-done | bytes 1572880 | tf_op jit(solution)/shard_map/reduce_scatter | solution.py:232
  1057.8 47.0 %reduce-scatter.13.cloned.1.call-done = bf16[192,1152]{1,0:T(8,128)(2,1)} async-done(((bf16[1536,1152]{1,0:T(8,128)(2,1)}), bf16[192,1152]{1,0:T(8,128)(2,1)}) %reduce-scatter.13.cloned.1.call-update) | async-done | bytes 442384
  (237 shorter events, 161.6 us)
Async XLA Ops:
  7.2 44.8 %copy-start.2 = (bf16[1024,1536]{1,0:T(8,128)(2,1)S(1)}, bf16[1024,1536]{1,0:T(8,128)(2,1)}, u32[]{:S(2)}) copy-start(bf16[1024,1536]{1,0:T(8,128)(2,1)} %param.17) | copy-start | bytes 9437188
  7.2 43.1 %all-gather.5.cloned.1.call-start = ((), (), s32[]{:S(2)}) async-start(), calls=%async_computation.4 | async-start | bytes 3981312 | tf_op jit(solution)/shard_map/all_gather | solution.py:158
  13.5 60.8 %all-gather.7.cloned.1.call-start = ((), (), s32[]{:S(2)}) async-start(), calls=%async_computation.5 | async-start | bytes 1572864 | tf_op jit(solution)/shard_map/all_gather | solution.py:186
  16.1 40.1 %copy-start.30 = (f32[1024]{0:T(1024)}, f32[1024]{0:T(1024)S(1)}, u32[]{:S(2)}) copy-start(f32[1024]{0:T(1024)S(1)} %add_rsqrt_fusion.1) | copy-start | bytes 12292
  16.4 45.1 %copy-start.18 = (f32[512,32]{0,1:T(8,128)}, f32[512,32]{0,1:T(8,128)S(1)}, u32[]{:S(2)}) copy-start(f32[512,32]{0,1:T(8,128)S(1)} %get-tuple-element.375) | copy-start | bytes 196612
  16.5 45.1 %copy-start.20 = (f32[512,32]{0,1:T(8,128)}, f32[512,32]{0,1:T(8,128)S(1)}, u32[]{:S(2)}) copy-start(f32[512,32]{0,1:T(8,128)S(1)} %get-tuple-element.376) | copy-start | bytes 196612
  65.1 163.1 %all-reduce.8.cloned.1.call-start = ((), (), s32[]{:S(2)}) async-start(), calls=%async_computation.6 | async-start | bytes 6291456 | tf_op jit(solution)/shard_map/psum | solution.py:197
  105.8 122.4 %copy-start.3 = (bf16[1024,1536]{1,0:T(8,128)(2,1)S(1)}, bf16[1024,1536]{1,0:T(8,128)(2,1)}, u32[]{:S(2)}) copy-start(bf16[1024,1536]{1,0:T(8,128)(2,1)} %param.17) | copy-start | bytes 9437188
  105.8 195.9 %all-gather.9.cloned.1.call-start = ((), (), s32[]{:S(2)}) async-start(), calls=%async_computation.7 | async-start | bytes 14155776 | tf_op jit(solution)/shard_map/all_gather | solution.py:166
  108.7 240.3 %all-gather.11.cloned.1.call-start = ((), (), s32[]{:S(2)}) async-start(), calls=%async_computation.8 | async-start | bytes 7077888 | tf_op jit(solution)/shard_map/all_gather | solution.py:167
  109.3 293.6 %all-reduce.12.cloned.1.call-start = ((), (), s32[]{:S(2)}) async-start(), calls=%async_computation.10 | async-start | bytes 131072 | tf_op jit(solution)/shard_map/psum | solution.py:219
  236.3 112.7 %copy-start.28 = (f32[16,1024]{1,0:T(8,128)}, f32[16,1024]{1,0:T(8,128)S(1)}, u32[]{:S(2)}) copy-start(f32[16,1024]{1,0:T(8,128)S(1)} %fusion.76) | copy-start | bytes 196612
  368.8 158.0 %all-reduce.10.cloned.1.call-start = ((), (), s32[]{:S(2)}) async-start(), calls=%async_computation.9 | async-start | bytes 6291456 | tf_op jit(solution)/shard_map/psum | solution.py:229
  388.2 270.9 %reduce-scatter.7.cloned.1.call-start = ((), (), s32[]{:S(2)}) async-start(), calls=%async_computation.11 | async-start | bytes 3145728 | tf_op jit(solution)/shard_map/reduce_scatter | solution.py:258
  404.7 127.8 %copy-start.24 = (bf16[1024,16]{0,1:T(8,128)(2,1)}, bf16[1024,16]{0,1:T(8,128)(2,1)S(1)}, u32[]{:S(2)}) copy-start(bf16[1024,16]{0,1:T(8,128)(2,1)S(1)} %multiply_convert_fusion.4) | copy-start | bytes 98308
  526.8 5.6 copy-start.7
  526.8 5.6 copy-start.14
  538.0 5.0 copy-start.12
  549.4 4.5 copy-start
  554.2 12.6 %copy-start.1 = (f32[2,1024,512,3]{2,1,3,0:T(8,128)S(1)}, f32[2,1024,512,3]{2,1,3,0:T(8,128)}, u32[]{:S(2)}) copy-start(f32[2,1024,512,3]{2,1,3,0:T(8,128)} %copy-done) | copy-start | bytes 37748740 | tf_op jit(solution)/shard_map/while
  604.7 12.6 %copy-start.1 = (f32[2,1024,512,3]{2,1,3,0:T(8,128)S(1)}, f32[2,1024,512,3]{2,1,3,0:T(8,128)}, u32[]{:S(2)}) copy-start(f32[2,1024,512,3]{2,1,3,0:T(8,128)} %copy-done) | copy-start | bytes 37748740 | tf_op jit(solution)/shard_map/while
  647.4 245.2 %all-reduce.14.cloned.1.call-start = ((), (), s32[]{:S(2)}) async-start(), calls=%async_computation.15 | async-start | bytes 12582912 | tf_op jit(solution)/shard_map/psum | solution.py:218
  647.5 14.2 %copy-start.13 = (f32[2,512,6,64]{1,0,3,2:T(2,128)S(1)}, f32[2,512,6,64]{1,0,3,2:T(2,128)}, u32[]{:S(2)}) copy-start(f32[2,512,6,64]{1,0,3,2:T(2,128)} %get-tuple-element.116) | copy-start | bytes 4718596
  647.5 14.2 %copy-start.19 = (f32[512,32]{0,1:T(8,128)S(1)}, f32[512,32]{0,1:T(8,128)}, u32[]{:S(2)}) copy-start(f32[512,32]{0,1:T(8,128)} %copy-done.18) | copy-start | bytes 196612
  647.5 14.2 %copy-start.21 = (f32[512,32]{0,1:T(8,128)S(1)}, f32[512,32]{0,1:T(8,128)}, u32[]{:S(2)}) copy-start(f32[512,32]{0,1:T(8,128)} %copy-done.20) | copy-start | bytes 196612
  670.2 286.4 %reduce-scatter.11.cloned.1.call-start = ((), (), s32[]{:S(2)}) async-start(), calls=%async_computation.13 | async-start | bytes 7077888 | tf_op jit(solution)/shard_map/reduce_scatter | solution.py:233
  692.0 360.9 %reduce-scatter.9.cloned.1.call-start = ((), (), s32[]{:S(2)}) async-start(), calls=%async_computation.12 | async-start | bytes 14155776 | tf_op jit(solution)/shard_map/reduce_scatter | solution.py:232
  730.6 374.2 %reduce-scatter.13.cloned.1.call-start = ((), (), s32[]{:S(2)}) async-start(), calls=%async_computation.14 | async-start | bytes 3981312
  731.8 5.6 copy-start.4
  731.9 5.6 copy-start.17
  731.9 5.6 copy-start.27
  731.9 5.6 copy-start.31
  (16 other events, 39.7 us)
Sparse Core Ops, SparseCore 0:
  13.6 36.6 all-gather.4
  65.2 9.0 all-gather.6
  105.9 122.2 all-reduce.7
  230.5 71.1 all-gather.8
  303.4 45.5 all-gather.10
  368.9 33.9 all-reduce.11
  406.0 120.7 all-reduce.9
  647.5 8.5 reduce-scatter.6
  670.3 222.2 all-reduce.13
  895.8 60.6 reduce-scatter.10
  960.5 92.3 reduce-scatter.8
  1056.6 48.0 reduce-scatter.12

commit v2 on v1

v2 whole, which is shorter than its diff:
```python
import functools
import math

import jax
import jax.numpy as jnp
from jax import lax
from jax.experimental import pallas as pl
from jax.experimental.pallas import tpu as pltpu
from jax.sharding import PartitionSpec as P

HEAD_SIZE = 64
TOPK = 8
E = 16
SEQUENCE_LENGTH = 1024
LANES = 128
VMEM_BYTES = 58 * 2**20

epsilon = 1e-06
f32 = jnp.float32
bf16 = jnp.bfloat16
MESH = pl.DeviceIdType.MESH
WHOLE = pl.BlockSpec(memory_space=pltpu.VMEM)


def placed(ranks, half):
    quarter = half // 2
    steps = jnp.arange(half, dtype=jnp.int32)
    early = ranks * quarter + steps
    late = SEQUENCE_LENGTH - (ranks + 1) * quarter + steps - quarter
    return jnp.where(steps < quarter, early, late)


def angle_tables(token_places):
    halfway = HEAD_SIZE // 2
    freqs = jnp.exp(
        jnp.arange(halfway, dtype=f32) * (-2.0 * math.log(10000.0) / HEAD_SIZE)
    )
    angles = token_places.astype(f32)[:, None] * freqs[None, :]
    copies = LANES // halfway
    return jnp.tile(jnp.cos(angles), (1, copies)), jnp.tile(jnp.sin(angles), (1, copies))


def aligned(start, size):
    return pl.ds(pl.multiple_of(start, size), size)


def dot(a, b, at=(1, 0)):
    return lax.dot_general(a, b, (((at[0],), (at[1],)), ((), ())), preferred_element_type=f32)


def swapped_halves(y):
    wide, halfway = y.shape[1], HEAD_SIZE // 2
    lane = lax.broadcasted_iota(jnp.int32, y.shape, 1)
    lower = lax.rem(lane, HEAD_SIZE) < halfway
    return jnp.where(lower, -pltpu.roll(y, wide - halfway, 1), pltpu.roll(y, halfway, 1))


def widened(table, wide):
    return jnp.concatenate([table] * (wide // LANES), 1)


def line_scratch(rows, width, chunks):
    buffer = pltpu.VMEM((rows, width), bf16)
    sems = pltpu.SemaphoreType.DMA((chunks,))
    return [buffer] * 4 + [sems] * 4


def line_barrier(n, me, others=()):
    barrier = pltpu.get_barrier_semaphore()

    @pl.when(me > 0)
    def _():
        pl.semaphore_signal(
            barrier, inc=1, device_id={"tp": lax.rem(me + n - 1, n)}, device_id_type=MESH
        )

    @pl.when(me < n - 1)
    def _():
        pl.semaphore_signal(
            barrier, inc=1, device_id={"tp": lax.rem(me + 1, n)}, device_id_type=MESH
        )

    for other in others:
        pl.semaphore_signal(barrier, inc=1, device_id=other, device_id_type=MESH)
    count = jnp.where(me > 0, 1, 0) + jnp.where(me < n - 1, 1, 0) + len(others)
    pl.semaphore_wait(barrier, count)


class Line:
    def __init__(self, n, me, chunks, own, finish, scratch):
        self.n, self.me, self.chunks, self.own, self.finish = n, me, chunks, own, finish
        self.from_left, self.from_right, self.to_right, self.to_left = scratch[:4]
        self.send_right, self.recv_left, self.send_left, self.recv_right = scratch[4:]
        self.size = own.shape[0] // chunks
        self.steps = chunks + n - 1

    def clear(self):
        @pl.when(self.me == 0)
        def _():
            self.from_left[...] = jnp.zeros_like(self.from_left)

        @pl.when(self.me == self.n - 1)
        def _():
            self.from_right[...] = jnp.zeros_like(self.from_right)

    def rows(self, c):
        return aligned(c * self.size, self.size)

    def right(self, c):
        return pltpu.make_async_remote_copy(
            src_ref=self.to_right.at[self.rows(c)],
            dst_ref=self.from_left.at[self.rows(c)],
            send_sem=self.send_right.at[c],
            recv_sem=self.recv_left.at[c],
            device_id={"tp": lax.rem(self.me + 1, self.n)},
            device_id_type=MESH,
        )

    def left(self, c):
        return pltpu.make_async_remote_copy(
            src_ref=self.to_left.at[self.rows(c)],
            dst_ref=self.from_right.at[self.rows(c)],
            send_sem=self.send_left.at[c],
            recv_sem=self.recv_right.at[c],
            device_id={"tp": lax.rem(self.me + self.n - 1, self.n)},
            device_id_type=MESH,
        )

    def step(self, t):
        n, me, chunks = self.n, self.me, self.chunks
        to_go = t - me

        @pl.when((me < n - 1) & (to_go >= 0) & (to_go < chunks))
        def _():
            rows = self.rows(to_go)

            @pl.when(me > 0)
            def _():
                self.right(to_go).wait_recv()

            total = self.own[rows].astype(f32) + self.from_left[rows].astype(f32)
            self.to_right[rows] = total.astype(bf16)
            self.right(to_go).start()

        to_come = t - (n - 1 - me)

        @pl.when((me > 0) & (to_come >= 0) & (to_come < chunks))
        def _():
            rows = self.rows(to_come)

            @pl.when(me < n - 1)
            def _():
                self.left(to_come).wait_recv()

            total = self.own[rows].astype(f32) + self.from_right[rows].astype(f32)
            self.to_left[rows] = total.astype(bf16)
            self.left(to_come).start()

        done = t - jnp.maximum(me, n - 1 - me)

        @pl.when((done >= 0) & (done < chunks))
        def _():
            @pl.when(me == 0)
            def _():
                self.left(done).wait_recv()

            @pl.when(me == n - 1)
            def _():
                self.right(done).wait_recv()

            rows = self.rows(done)
            total = (
                self.own[rows].astype(f32)
                + self.from_left[rows].astype(f32)
                + self.from_right[rows].astype(f32)
            )
            self.finish(done, rows, total)

    def sent(self):
        def one(c, carry):
            @pl.when(self.me < self.n - 1)
            def _():
                self.right(c).wait_send()

            @pl.when(self.me > 0)
            def _():
                self.left(c).wait_send()

            return carry

        lax.fori_loop(0, self.chunks, one, 0)


def loop(low, high, body):
    lax.fori_loop(low, high, lambda i, carry: (body(i), carry)[1], 0)


def folded(values):
    rows, width = values.shape
    return jnp.sum(values.reshape(rows // 8, 8, width), 0)


class Places:
    def __init__(self, nc):
        self.nc = nc
        self.c = lax.axis_index("ctx")
        self.quarter = SEQUENCE_LENGTH // nc // 2

    def slot(self, rank, part):
        return rank if part == 0 else 2 * self.nc - 1 - rank

    def rows(self, rank, part):
        return aligned(self.slot(rank, part) * self.quarter, self.quarter)

    def own(self, s, part):
        return aligned((2 * s + part) * self.quarter, self.quarter)

    def keys(self, part):
        return self.quarter * (self.nc if part == 0 else 2 * self.nc)

    def after(self, o):
        return lax.rem(self.c + o, self.nc)

    def before(self, o):
        return lax.rem(self.c + self.nc - o, self.nc)


def front_kernel(
    n,
    nc,
    x_ref,
    wqkv_ref,
    wout_ref,
    router_ref,
    named_ref,
    gain_one_ref,
    gain_two_ref,
    cos_ref,
    sin_ref,
    query_ref,
    kv_ref,
    mixed_ref,
    state_ref,
    normed_ref,
    gates_ref,
    kv_all,
    own,
    send_kv,
    recv_kv,
    *scratch,
):
    me = lax.axis_index("tp")
    places = Places(nc)
    quarter = places.quarter
    seqs = kv_ref.shape[0]
    q_wide, k_wide = query_ref.shape[1], kv_ref.shape[2] // 2
    group = q_wide // k_wide

    def finish(c, rows, total):
        state = x_ref[rows].astype(f32) + total
        scale = lax.rsqrt(jnp.mean(state * state, -1, keepdims=True) + epsilon)
        normed = (state * scale * gain_two_ref[...]).astype(bf16)
        state_ref[rows] = state
        normed_ref[rows] = normed
        named = named_ref[rows] > 0.5
        logits = jnp.where(named, dot(normed, router_ref[...]), -1e30)
        top = jnp.max(logits, -1, keepdims=True)
        raised = jnp.where(named, jnp.exp(logits - top), 0.0)
        gates_ref[rows] = raised / jnp.sum(raised, -1, keepdims=True)

    line = Line(n, me, own.shape[0] // 128, own, finish, scratch)
    line_barrier(n, me, [{"ctx": places.after(o)} for o in range(1, nc)])
    line.clear()

    def kv_copy(s, part, o, rank):
        where = kv_all.at[s, places.rows(rank, part)]
        return pltpu.make_async_remote_copy(
            src_ref=where,
            dst_ref=where,
            send_sem=send_kv.at[o - 1, s, part],
            recv_sem=recv_kv.at[o - 1, s, part],
            device_id={"ctx": places.after(o)},
            device_id_type=MESH,
        )

    def project(s):
        for part in range(2):
            rows = places.own(s, part)
            x = x_ref[rows].astype(f32)
            scale = lax.rsqrt(jnp.mean(x * x, -1, keepdims=True) + epsilon)
            normed = (x * scale * gain_one_ref[...]).astype(bf16)
            qkv = dot(normed, wqkv_ref[...])
            qk = qkv[:, : q_wide + k_wide]
            here = pl.ds(part * quarter, quarter)
            cos, sin = widened(cos_ref[here], q_wide + k_wide), widened(sin_ref[here], q_wide + k_wide)
            rot = qk * cos + swapped_halves(qk) * sin
            query_ref[rows] = (rot[:, :q_wide] * (1.0 / math.sqrt(HEAD_SIZE))).astype(bf16)
            slot = places.rows(places.c, part)
            kv_all[s, slot, :k_wide] = rot[:, q_wide:].astype(bf16)
            kv_all[s, slot, k_wide:] = qkv[:, q_wide + k_wide :].astype(bf16)
            for o in range(1, nc):
                kv_copy(s, part, o, places.c).start()

    loop(0, seqs, project)

    def attend(s):
        for part in range(2):
            for o in range(1, nc):
                kv_copy(s, part, o, places.before(o)).wait_recv()
        for part in range(2):
            rows = places.own(s, part)
            keys = places.keys(part)
            base = places.slot(places.c, part) * quarter
            allowed = lax.broadcasted_iota(jnp.int32, (quarter, keys), 1) <= (
                base + lax.broadcasted_iota(jnp.int32, (quarter, keys), 0)
            )
            for h in range(q_wide // HEAD_SIZE):
                at = h // group * HEAD_SIZE
                query = query_ref[rows, h * HEAD_SIZE : (h + 1) * HEAD_SIZE]
                key = kv_all[s, :keys, at : at + HEAD_SIZE]
                value = kv_all[s, :keys, k_wide + at : k_wide + at + HEAD_SIZE]
                scores = jnp.where(allowed, dot(query, key, (1, 1)), -1e30)
                raised = jnp.exp(scores - jnp.max(scores, -1, keepdims=True))
                probs = (raised * (1.0 / jnp.sum(raised, -1, keepdims=True))).astype(bf16)
                mixed_ref[rows, h * HEAD_SIZE : (h + 1) * HEAD_SIZE] = dot(probs, value).astype(bf16)
            own[rows] = dot(mixed_ref[rows], wout_ref[...], (1, 1)).astype(bf16)
            per = quarter // line.size
            for i in range(per):
                line.step((2 * s + part) * per + i)

    loop(0, seqs, attend)
    loop(line.chunks, line.steps, line.step)
    kv_ref[...] = kv_all[...]
    line.sent()

    def kv_sent(s):
        for part in range(2):
            for o in range(1, nc):
                kv_copy(s, part, o, places.c).wait_send()

    loop(0, seqs, kv_sent)


def moe_kernel(x_ref, dy_ref, gates_ref, w_ref, hidden_ref, grad_ref, dots_ref, out_ref, dx_ref):
    rows = x_ref.shape[0]
    pair = hidden_ref.shape[1] // (E // 2)
    single = pair // 2
    gu_wide = grad_ref.shape[1]
    lane = lax.broadcasted_iota(jnp.int32, (rows, LANES), 1)
    first = lax.broadcasted_iota(jnp.int32, (rows, pair), 1) < single
    dots_ref[...] = jnp.zeros_like(dots_ref)

    def experts(p):
        gu = dot(x_ref[...], w_ref[:, aligned(p * 2 * pair, 2 * pair)])
        raw = dot(dy_ref[...], w_ref[:, aligned(gu_wide + p * pair, pair)])
        gate_pre, up_pre = gu[:, :pair], gu[:, pair:]
        gates = gates_ref[...]
        gate = jnp.where(
            first,
            jnp.sum(jnp.where(lane == 2 * p, gates, 0.0), 1, keepdims=True),
            jnp.sum(jnp.where(lane == 2 * p + 1, gates, 0.0), 1, keepdims=True),
        )
        sigma = jax.nn.sigmoid(gate_pre)
        silu = gate_pre * sigma
        hidden = (silu * up_pre).astype(bf16).astype(f32)
        hidden_ref[:, aligned(p * pair, pair)] = (hidden * gate).astype(bf16)
        both = hidden * raw
        dots_ref[...] += jnp.where(
            lane == 2 * p, jnp.sum(both[:, :single], 1, keepdims=True), 0.0
        ) + jnp.where(lane == 2 * p + 1, jnp.sum(both[:, single:], 1, keepdims=True), 0.0)
        dh = raw * gate
        grad_ref[:, aligned(p * 2 * pair, pair)] = (
            dh * up_pre * (sigma + silu * (1.0 - sigma))
        ).astype(bf16)
        grad_ref[:, aligned(p * 2 * pair + pair, pair)] = (dh * silu).astype(bf16)

    loop(0, E // 2, experts)
    tile = 256

    def outward(i):
        at = aligned(i * tile, tile)
        out_ref[:, at] = dot(hidden_ref[...], w_ref[at, gu_wide:], (1, 1)).astype(bf16)
        dx_ref[:, at] = dot(grad_ref[...], w_ref[at, :gu_wide], (1, 1)).astype(bf16)

    loop(0, out_ref.shape[1] // tile, outward)


def weight_kernel(gu_blocks, x_ref, dy_ref, grad_ref, hidden_ref, out_ref):
    step = pl.program_id(0)

    @pl.when(step < gu_blocks)
    def _():
        out_ref[...] = dot(x_ref[...], grad_ref[...]).astype(bf16)

    @pl.when(step >= gu_blocks)
    def _():
        out_ref[...] = dot(dy_ref[...], hidden_ref[...]).astype(bf16)


def middle_kernel(
    n,
    own,
    state_ref,
    dy_ref,
    gates_ref,
    dots_ref,
    router_ref,
    gain_ref,
    dstate_ref,
    dlogits_ref,
    dgain_ref,
    *scratch,
):
    me = lax.axis_index("tp")
    dgain_ref[...] = jnp.zeros_like(dgain_ref)

    def finish(c, rows, total):
        gates = gates_ref[rows]
        lane = lax.broadcasted_iota(jnp.int32, gates.shape, 1)
        product = gates * dots_ref[rows]
        dlogits = product - gates * jnp.sum(product, -1, keepdims=True)
        dlogits = jnp.where(lane < E, dlogits, 0.0).astype(bf16)
        dlogits_ref[rows] = dlogits
        dn = total + dot(dlogits, router_ref[...], (1, 1))
        state = state_ref[rows]
        scale = lax.rsqrt(jnp.mean(state * state, -1, keepdims=True) + epsilon)
        unit = state * scale
        scaled = dn * gain_ref[...]
        inner = jnp.mean(scaled * unit, -1, keepdims=True)
        dstate_ref[rows] = dy_ref[rows].astype(f32) + scale * (scaled - unit * inner)
        dgain_ref[...] += folded(dn * unit)

    line = Line(n, me, own.shape[0] // 64, own, finish, scratch)
    line_barrier(n, me)
    line.clear()
    loop(0, line.steps, line.step)
    line.sent()


def output_kernel(n, own, state_ref, out_ref, *scratch):
    me = lax.axis_index("tp")

    def finish(c, rows, total):
        out_ref[rows] = (state_ref[rows] + total).astype(bf16)

    line = Line(n, me, own.shape[0] // 64, own, finish, scratch)
    line_barrier(n, me)
    line.clear()
    loop(0, line.steps, line.step)
    line.sent()


def back_kernel(
    nc,
    dstate_ref,
    wout_ref,
    query_ref,
    kv_ref,
    cos_ref,
    sin_ref,
    low_ref,
    dqkv_ref,
    dmixed,
    dquery,
    dkv,
    dkv_in,
    send_kv,
    recv_kv,
):
    places = Places(nc)
    quarter = places.quarter
    seqs = kv_ref.shape[0]
    q_wide, k_wide = query_ref.shape[1], kv_ref.shape[2] // 2
    group = q_wide // k_wide
    factor = 1.0 / math.sqrt(HEAD_SIZE)
    barrier = pltpu.get_barrier_semaphore()
    for o in range(1, nc):
        pl.semaphore_signal(
            barrier, inc=1, device_id={"ctx": places.after(o)}, device_id_type=MESH
        )
    pl.semaphore_wait(barrier, nc - 1)

    def kv_copy(s, part, o, rank):
        return pltpu.make_async_remote_copy(
            src_ref=dkv.at[s, places.rows(rank, part)],
            dst_ref=dkv_in.at[o - 1, s, part],
            send_sem=send_kv.at[o - 1, s, part],
            recv_sem=recv_kv.at[o - 1, s, part],
            device_id={"ctx": places.after(o)},
            device_id_type=MESH,
        )

    def attend(s):
        for part in (1, 0):
            rows = places.own(s, part)
            keys = places.keys(part)
            low = dstate_ref[rows].astype(bf16)
            low_ref[rows] = low
            dmixed[...] = dot(low, wout_ref[...]).astype(bf16)
            base = places.slot(places.c, part) * quarter
            allowed = lax.broadcasted_iota(jnp.int32, (keys, quarter), 0) <= (
                base + lax.broadcasted_iota(jnp.int32, (keys, quarter), 1)
            )
            for k in range(k_wide // HEAD_SIZE):
                at = k * HEAD_SIZE
                key = kv_ref[s, :keys, at : at + HEAD_SIZE]
                value = kv_ref[s, :keys, k_wide + at : k_wide + at + HEAD_SIZE]
                dkey = dvalue = None
                for h in range(k * group, (k + 1) * group):
                    head = slice(h * HEAD_SIZE, (h + 1) * HEAD_SIZE)
                    query = query_ref[rows, head]
                    dout = dmixed[:, head]
                    scores = jnp.where(allowed, dot(key, query, (1, 1)), -1e30)
                    raised = jnp.exp(scores - jnp.max(scores, 0, keepdims=True))
                    probs = raised * (1.0 / jnp.sum(raised, 0, keepdims=True))
                    product = probs * dot(value, dout, (1, 1))
                    dscores = product - probs * jnp.sum(product, 0, keepdims=True)
                    dscores = dscores.astype(bf16)
                    dquery[rows, head] = dot(dscores, key, (0, 0)) * factor
                    dk, dv = dot(dscores, query), dot(probs.astype(bf16), dout)
                    dkey = dk if dkey is None else dkey + dk
                    dvalue = dv if dvalue is None else dvalue + dv
                for start, add in ((at, dkey), (k_wide + at, dvalue)):
                    lanes = slice(start, start + HEAD_SIZE)
                    if part == 1:
                        dkv[s, :keys, lanes] = add
                    else:
                        dkv[s, :keys, lanes] += add
        for part in range(2):
            for o in range(1, nc):
                kv_copy(s, part, o, places.after(o)).start()

    loop(0, seqs, attend)

    def turn_back(s):
        for part in range(2):
            rows = places.own(s, part)
            mine = dkv[s, places.rows(places.c, part)]
            for o in range(1, nc):
                kv_copy(s, part, o, places.after(o)).wait()
                mine = mine + dkv_in[o - 1, s, part]
            turned = jnp.concatenate([dquery[rows], mine[:, :k_wide]], 1)
            here = pl.ds(part * quarter, quarter)
            cos, sin = widened(cos_ref[here], q_wide + k_wide), widened(sin_ref[here], q_wide + k_wide)
            dqkv_ref[rows, : q_wide + k_wide] = (
                turned * cos - swapped_halves(turned) * sin
            ).astype(bf16)
            dqkv_ref[rows, q_wide + k_wide :] = mine[:, k_wide:].astype(bf16)

    loop(0, seqs, turn_back)


def tail_kernel(
    n, dqkv_ref, wqkv_ref, x_ref, dstate_ref, gain_ref, out_ref, dgain_ref, own, *scratch
):
    me = lax.axis_index("tp")
    dgain_ref[...] = jnp.zeros_like(dgain_ref)

    def finish(c, rows, total):
        x = x_ref[rows].astype(f32)
        scale = lax.rsqrt(jnp.mean(x * x, -1, keepdims=True) + epsilon)
        unit = x * scale
        scaled = total * gain_ref[...]
        inner = jnp.mean(scaled * unit, -1, keepdims=True)
        out_ref[rows] = (dstate_ref[rows] + scale * (scaled - unit * inner)).astype(bf16)
        dgain_ref[...] += folded(total * unit)

    line = Line(n, me, own.shape[0] // 64, own, finish, scratch)
    line_barrier(n, me)
    line.clear()
    block = 256

    def start(i):
        rows = aligned(i * block, block)
        own[rows] = dot(dqkv_ref[rows], wqkv_ref[...], (1, 1)).astype(bf16)
        for j in range(block // line.size):
            line.step(i * (block // line.size) + j)

    loop(0, own.shape[0] // block, start)
    loop(line.chunks, line.steps, line.step)
    line.sent()


def call(kernel, outs, scratch, collective_id, operands, flops=0):
    total = sum(math.prod(o.shape) * o.dtype.itemsize for o in [*outs, *operands])
    return pl.pallas_call(
        kernel,
        out_shape=tuple(outs),
        in_specs=[WHOLE] * len(operands),
        out_specs=tuple([WHOLE] * len(outs)),
        scratch_shapes=scratch,
        compiler_params=pltpu.CompilerParams(
            collective_id=collective_id, has_side_effects=True, vmem_limit_bytes=VMEM_BYTES
        ),
        cost_estimate=pl.CostEstimate(flops=flops, bytes_accessed=total, transcendentals=0),
    )(*operands)


def per_device(
    tokens,
    routes,
    gain_attn,
    w_query,
    key_matrix,
    value_matrix,
    w_out,
    gain_moe,
    w_router,
    w_gate,
    w_up,
    w_down,
    cotangent,
):
    shaped = jax.ShapeDtypeStruct
    rows, width = tokens.shape
    nc, n = lax.axis_size("ctx"), lax.axis_size("tp")
    half = SEQUENCE_LENGTH // nc
    seqs = rows // half
    both = ("fsdp", "ctx")
    cos, sin = angle_tables(placed(lax.axis_index("ctx"), half))
    q_wide, k_wide, o_wide = w_query.shape[1], key_matrix.shape[1], w_out.shape[0]
    qkv_wide = q_wide + 2 * k_wide
    ffn = w_gate.shape[2]
    shard = w_gate.shape[1]

    small = jnp.concatenate(
        [
            w_query,
            key_matrix,
            value_matrix,
            w_out.T,
            w_router,
            gain_attn[:, None],
            gain_moe[:, None],
            jnp.zeros((shard, LANES - E - 2), bf16),
        ],
        1,
    )
    small_full = lax.all_gather(small, both, axis=0, tiled=True)
    wqkv = small_full[:, :qkv_wide]
    wout = small_full[:, qkv_wide : qkv_wide + o_wide]
    router = small_full[:, qkv_wide + o_wide :]
    gains = router[:, E : E + 2].astype(f32).T
    gain_one, gain_two = gains[:1], gains[1:]

    pairs = E // 2
    gates_up = jnp.stack(
        [w_gate.reshape(pairs, 2, shard, ffn), w_up.reshape(pairs, 2, shard, ffn)], 1
    )
    gates_up = gates_up.transpose(3, 0, 1, 2, 4).reshape(shard, 2 * E * ffn)
    down = w_down.transpose(2, 0, 1).reshape(shard, E * ffn)
    experts = lax.all_gather(jnp.concatenate([gates_up, down], 1), both, axis=0, tiled=True)

    named = jnp.any(routes[:, :, None] == jnp.arange(LANES, dtype=jnp.int32)[None, None, :], 1)
    named = named.astype(f32)
    kv_sems = pltpu.SemaphoreType.DMA((nc - 1, seqs, 2))

    query, kv, mixed, state, normed_two, gates = call(
        functools.partial(front_kernel, n, nc),
        [
            shaped((rows, q_wide), bf16),
            shaped((seqs, SEQUENCE_LENGTH, 2 * k_wide), bf16),
            shaped((rows, q_wide), bf16),
            shaped((rows, width), f32),
            shaped((rows, width), bf16),
            shaped((rows, LANES), f32),
        ],
        [
            pltpu.VMEM((seqs, SEQUENCE_LENGTH, 2 * k_wide), bf16),
            pltpu.VMEM((rows, width), bf16),
            kv_sems,
            kv_sems,
            *line_scratch(rows, width, rows // 128),
        ],
        0,
        (tokens, wqkv, wout, router, named, gain_one, gain_two, cos, sin),
    )

    block = 256
    gu_wide, down_wide = 2 * E * ffn, E * ffn

    def by_rows(wide):
        return pl.BlockSpec((block, wide), lambda i: (i, 0))

    hidden, gu_grad, dots, moe_part, dx_part = pl.pallas_call(
        moe_kernel,
        grid=(rows // block,),
        out_shape=(
            shaped((rows, down_wide), bf16),
            shaped((rows, gu_wide), bf16),
            shaped((rows, LANES), f32),
            shaped((rows, width), bf16),
            shaped((rows, width), bf16),
        ),
        in_specs=[
            by_rows(width),
            by_rows(width),
            by_rows(LANES),
            pl.BlockSpec(
                (width, gu_wide + down_wide), lambda i: (0, 0), pipeline_mode=pl.Buffered(1)
            ),
        ],
        out_specs=(
            by_rows(down_wide),
            by_rows(gu_wide),
            by_rows(LANES),
            by_rows(width),
            by_rows(width),
        ),
        compiler_params=pltpu.CompilerParams(vmem_limit_bytes=VMEM_BYTES),
        cost_estimate=pl.CostEstimate(
            flops=12 * rows * width * down_wide,
            bytes_accessed=2 * width * (gu_wide + down_wide),
            transcendentals=0,
        ),
    )(normed_two, cotangent, gates, experts)
    dots = lax.psum(dots[:, :E], "tp")
    dots = jnp.pad(dots, ((0, 0), (0, LANES - E)))

    column = 512
    gu_blocks, down_blocks = gu_wide // column, down_wide // column
    grad_experts = pl.pallas_call(
        functools.partial(weight_kernel, gu_blocks),
        grid=(gu_blocks + down_blocks,),
        out_shape=shaped((width, gu_wide + down_wide), bf16),
        in_specs=[
            pl.BlockSpec((width, rows), lambda i: (0, 0), pipeline_mode=pl.Buffered(1)),
            pl.BlockSpec((width, rows), lambda i: (0, 0), pipeline_mode=pl.Buffered(1)),
            pl.BlockSpec((rows, column), lambda i: (0, jnp.minimum(i, gu_blocks - 1))),
            pl.BlockSpec((rows, column), lambda i: (0, jnp.maximum(i - gu_blocks, 0))),
        ],
        out_specs=pl.BlockSpec((width, column), lambda i: (0, i)),
        compiler_params=pltpu.CompilerParams(vmem_limit_bytes=VMEM_BYTES),
        cost_estimate=pl.CostEstimate(
            flops=6 * rows * width * down_wide,
            bytes_accessed=2 * width * (gu_wide + down_wide),
            transcendentals=0,
        ),
    )(normed_two.T, cotangent.T, gu_grad, hidden)
    grad_experts = lax.psum_scatter(grad_experts, both, scatter_dimension=0, tiled=True)

    scratch = line_scratch(rows, width, rows // 64)
    dstate, dlogits, dgain_two = call(
        functools.partial(middle_kernel, n),
        [shaped((rows, width), f32), shaped((rows, LANES), bf16), shaped((8, width), f32)],
        scratch,
        1,
        (dx_part, state, cotangent, gates, dots, router, gain_two),
    )
    low, dqkv = call(
        functools.partial(back_kernel, nc),
        [shaped((rows, width), bf16), shaped((rows, qkv_wide), bf16)],
        [
            pltpu.VMEM((half // 2, q_wide), bf16),
            pltpu.VMEM((rows, q_wide), f32),
            pltpu.VMEM((seqs, SEQUENCE_LENGTH, 2 * k_wide), f32),
            pltpu.VMEM((nc - 1, seqs, 2, half // 2, 2 * k_wide), f32),
            kv_sems,
            kv_sems,
        ],
        2,
        (dstate, wout, query, kv, cos, sin),
    )
    inputs = tokens.astype(f32)
    scale_one = lax.rsqrt(jnp.mean(inputs * inputs, -1, keepdims=True) + epsilon)
    normed = (inputs * scale_one * gain_one).astype(bf16)
    grad_qkv = jnp.einsum("td,tc->dc", normed, dqkv, preferred_element_type=f32)
    grad_out = jnp.einsum("td,tc->dc", low, mixed, preferred_element_type=f32)
    grad_router = jnp.einsum("td,te->de", normed_two, dlogits, preferred_element_type=f32)
    grad_small = jnp.concatenate(
        [grad_qkv.astype(bf16), grad_out.astype(bf16), grad_router.astype(bf16)], 1
    )
    grad_small = lax.psum_scatter(grad_small, both, scatter_dimension=0, tiled=True)
    input_grad, dgain_one = call(
        functools.partial(tail_kernel, n),
        [shaped((rows, width), bf16), shaped((8, width), f32)],
        [pltpu.VMEM((rows, width), bf16), *scratch],
        3,
        (dqkv, wqkv, tokens, dstate, gain_one),
    )
    (activations,) = call(
        functools.partial(output_kernel, n),
        [shaped((rows, width), bf16)],
        scratch,
        4,
        (moe_part, state),
    )
    dgains = jnp.stack([jnp.sum(dgain_one, 0), jnp.sum(dgain_two, 0)])
    dgains = lax.psum_scatter(dgains, both, scatter_dimension=1, tiled=True)
    grad_small = grad_small.astype(f32)
    grad_experts = grad_experts.astype(f32)
    grad_gu = grad_experts[:, :gu_wide].reshape(shard, pairs, 2, 2, ffn).transpose(2, 1, 3, 0, 4)
    grad_gu = grad_gu.reshape(2, E, shard, ffn)
    grad_down = grad_experts[:, gu_wide:].reshape(shard, E, ffn).transpose(1, 2, 0)
    at = q_wide + k_wide
    return (
        activations,
        input_grad,
        dgains[0],
        grad_small[:, :q_wide],
        grad_small[:, q_wide:at],
        grad_small[:, at:qkv_wide],
        grad_small[:, qkv_wide : qkv_wide + o_wide].T,
        dgains[1],
        grad_small[:, qkv_wide + o_wide : qkv_wide + o_wide + E],
        grad_gu[0],
        grad_gu[1],
        grad_down,
    )


def solution(mesh):
    specs = (
        P(("fsdp", "ctx"), None),
        P(("fsdp", "ctx"), None),
        P(("fsdp", "ctx")),
        P(("fsdp", "ctx"), "tp"),
        P(("fsdp", "ctx"), "tp"),
        P(("fsdp", "ctx"), "tp"),
        P("tp", ("fsdp", "ctx")),
        P(("fsdp", "ctx")),
        P(("fsdp", "ctx"), None),
        P(None, ("fsdp", "ctx"), "tp"),
        P(None, ("fsdp", "ctx"), "tp"),
        P(None, "tp", ("fsdp", "ctx")),
        P(("fsdp", "ctx"), None),
    )
    return jax.shard_map(
        per_device,
        mesh=mesh,
        in_specs=specs,
        out_specs=(
            P(("fsdp", "ctx"), None),
            P(("fsdp", "ctx"), None),
            P(("fsdp", "ctx")),
            P(("fsdp", "ctx"), "tp"),
            P(("fsdp", "ctx"), "tp"),
            P(("fsdp", "ctx"), "tp"),
            P("tp", ("fsdp", "ctx")),
            P(("fsdp", "ctx")),
            P(("fsdp", "ctx"), None),
            P(None, ("fsdp", "ctx"), "tp"),
            P(None, ("fsdp", "ctx"), "tp"),
            P(None, "tp", ("fsdp", "ctx")),
        ),
        check_vma=False,
    )
```

time: 1130 us -> 756 us (0.67)
  waiting for transfers between devices: 706 us -> 116 us
  Pallas kernels: 0 us -> 530 us
  matrix products: 185 us -> 4.57 us
  local copies, waits for them, and re-layouts: 147 us -> 65.8 us
  other arithmetic: 62.2 us -> 16.8 us
    pallas_call x0 -> x7, Pallas kernels: none -> 530 us  [the longest x5 439 us: call(): pl.pallas_call(kernel, out_shape=tuple(outs), in_specs=[WHOLE] * len(oper...]
    psum x4 -> x1, waiting for transfers between devices: 406 us -> 37.2 us  [per_device(): dots = lax.psum(dots[:, :E], 'tp')]
    dot_general x29 -> x3, matrix products: 185 us -> 4.57 us  [the longest x1 2.51 us: per_device(): grad_qkv = jnp.einsum('td,tc->dc', normed, dqkv, preferred_element_type=f32)]
    all_gather x3 -> x1, waiting for transfers between devices: 99.5 us -> 0.02 us  [per_device(): lax.all_gather(jnp.concatenate([gates_up, down], 1), both, axis=0, tiled=...]
    reduce_scatter x3 -> x1, waiting for transfers between devices: 118 us -> 64.5 us  [per_device(): lax.psum_scatter(grad_experts, both, scatter_dimension=0, tiled=True)]
    unnamed x13 -> x8, waiting for transfers between devices: 47.7 us -> 0.12 us
    dynamic_update_slice x14 -> x0, local copies, waits for them, and re-layouts: 35 us -> none  [the longest x10 34.4 us: per_device(): lax.map(backward_one, (query_rot4, keys_all, values_all, log_total, mixed...]
    convert_element_type x3 -> x0, local copies, waits for them, and re-layouts: 26.4 us -> none  [the longest x1 17.1 us: per_device(): grad_gu.astype(bf16)]
  transfers between devices with their start and end apart: 12 -> 6, of which waited for: 11 -> 3; matrix products, arithmetic and copies ran while one was open for 16% -> 7% of each run, Pallas kernels for 0% -> 31%
where the time goes in v2:
time: 756 us; the launch traced here: 748 us
  Pallas kernels  530 us (70%)
  waiting for transfers between devices  116 us (15%)
  local copies, waits for them, and re-layouts  65.8 us (9%)
  other arithmetic  16.8 us (2%)
  between operations  15 us (2%)
    pallas_call x5, Pallas kernels, call(): pl.pallas_call(kernel, out_shape=tuple(outs), in_specs=[WHOLE] * len(oper...  439 us
    reduce_scatter x1, waiting for transfers between devices, per_device(): lax.psum_scatter(grad_experts, both, scatter_dimension=0, tiled=True)  64.5 us
    pallas_call x1, Pallas kernels, per_device(): pl.pallas_call(moe_kernel, grid=(rows // block,), out_shape=(shaped((rows...  63.8 us
    psum x1, waiting for transfers between devices, per_device(): dots = lax.psum(dots[:, :E], 'tp')  37.2 us
    pallas_call x1, Pallas kernels, per_device(): pl.pallas_call(functools.partial(weight_kernel, gu_blocks), grid=(gu_bloc...  26.9 us
    unnamed x47, local copies, waits for them, and re-layouts  26.1 us
  transfers between devices with their start and end apart: 6, of which 3 were waited for; matrix products, arithmetic and copies ran while one was open for 7% of the time, Pallas kernels for 31%

profile of v2, /device:TPU:0, one launch (start us, length us, event | category | flops | bytes accessed | tf_op | source)
XLA Modules:
  0.0 748.4 jit_solution(5856614690763530443)
XLA Ops:
  9.7 1.9 concatenate.9
  11.7 1.9 copy.123
  14.5 2.2 maximum_bitcast_fusion
  16.7 2.4 reshape.125
  19.2 3.0 pad_maximum_fusion.1
  23.3 6.8 fusion.3
  33.7 14.7 %all-gather.3.cloned.1.call-done = bf16[1536,1152]{1,0:T(8,128)(2,1)} async-done(((bf16[192,1152]{1,0:T(8,128)(2,1)}), bf16[1536,1152]{1,0:T(8,128)(2,1)}) %all-gather.3.cloned.1.call-update) | async-done | bytes 3538960 | tf_op jit(solution)/shard_map/all_gather | solution.py:639
  49.9 3.0 slice.75.wqkv_ref
  52.9 2.4 slice.76.wout_ref
  55.3 1.8 slice.77.router_ref
  57.6 107.9 %shard_map.220 = (bf16[1024,384]{1,0:T(8,128)(2,1)}, bf16[2,1024,256]{2,1,0:T(8,128)(2,1)}, bf16[1024,384]{1,0:T(8,128)(2,1)}, f32[1024,1536]{1,0:T(8,128)}, bf1...) custom-call(bf16[1024,1536]{1,0:T(8,128)(2,1)} %x_ref.3, bf16[1536,640]{1,0:T(8,128)(2,1)} %slice.75.wqkv_ref, ...), custom_call_target="tpu_custom_call" | custom-call | bytes 20328448 | tf_op jit(solution)/shard_map/pallas_call | solution.py:586
  165.5 63.8 %shard_map.221 = (bf16[1024,2048]{1,0:T(8,128)(2,1)}, bf16[1024,4096]{1,0:T(8,128)(2,1)}, f32[1024,128]{1,0:T(8,128)}, bf16[1024,1536]{1,0:T(8,128)(2,1)}, bf16[1024,1536]{1,0:T(8,128)(2,1)}) custom-call(bf16[1024,1536]{1,0:T(8,128)(2,1)} %get-tuple-element.30.x_ref, bf16[1024,1536]{1,0:T(8,128)(2,1)} %dy_ref.3, f32[1024,128]{1,0:T(8,128)} %get-tuple-element.31.gates_ref, ...), custom_call_target="tpu_custom_call" | custom-call | flops 38654705664 | bytes 18874368 | tf_op jit(solution)/shard_map/pallas_call | solution.py:685
  229.4 37.2 %all-reduce.3.cloned.1.call-done = f32[1024,16]{1,0:T(8,128)} async-done(((f32[1024,16]{1,0:T(8,128)}), f32[1024,16]{1,0:T(8,128)}) %all-reduce.3.cloned.1.call-update) | async-done | bytes 65552 | tf_op jit(solution)/shard_map/psum | solution.py:717
  266.6 1.9 pad.4.dots_ref
  268.5 96.5 %shard_map.223 = (f32[1024,1536]{1,0:T(8,128)}, bf16[1024,128]{1,0:T(8,128)(2,1)}, f32[8,1536]{1,0:T(8,128)}) custom-call(bf16[1024,1536]{1,0:T(8,128)(2,1)} %get-tuple-element.34.own, f32[1024,1536]{1,0:T(8,128)} %get-tuple-element.33.state_ref, bf16[1024,1536]{1,0:T(8,128)(2,1)} %dy_ref.3, f32[1024,128]{1,0:T(8,128)} %get-tuple-element.31.gates_ref, ...), custom_call_target="tpu_custom_call" | custom-call | bytes 20633600 | tf_op jit(solution)/shard_map/pallas_call | solution.py:586
  365.0 43.4 %shard_map.224 = (bf16[1024,1536]{1,0:T(8,128)(2,1)}, bf16[1024,640]{1,0:T(8,128)(2,1)}) custom-call(f32[1024,1536]{1,0:T(8,128)} %get-tuple-element.36.dstate_ref, bf16[1536,384]{1,0:T(8,128)(2,1)} %slice.76.wout_ref, bf16[1024,384]{1,0:T(8,128)(2,1)} %get-tuple-element.37.query_ref, bf16[2,1024,256]{2,1,0:T(8,128)(2,1)} %get-tuple-element.38.kv_ref, ...), custom_call_target="tpu_custom_call" | custom-call | bytes 14286848 | tf_op jit(solution)/shard_map/pallas_call | solution.py:586
  408.4 96.3 %shard_map.225 = (bf16[1024,1536]{1,0:T(8,128)(2,1)}, f32[8,1536]{1,0:T(8,128)}) custom-call(bf16[1024,640]{1,0:T(8,128)(2,1)} %get-tuple-element.39.dqkv_ref, bf16[1536,640]{1,0:T(8,128)(2,1)} %slice.75.wqkv_ref, bf16[1024,1536]{1,0:T(8,128)(2,1)} %x_ref.3, f32[1024,1536]{1,0:T(8,128)} %get-tuple-element.36.dstate_ref, ...), custom_call_target="tpu_custom_call" | custom-call | bytes 15915008 | tf_op jit(solution)/shard_map/pallas_call | solution.py:586
  509.0 1.4 convolution_convert_fusion.1
  511.3 2.5 convolution_convert_fusion
  514.1 3.8 copy.138
  518.0 1.8 copy-done.5
  519.8 3.1 copy.128
  523.0 4.6 copy.127
  527.6 26.9 %shard_map.226 = bf16[1536,6144]{1,0:T(8,128)(2,1)} custom-call(bf16[1536,1024]{1,0:T(8,128)(2,1)} %bitcast.41, bf16[1536,1024]{1,0:T(8,128)(2,1)} %bitcast.40, bf16[1024,4096]{1,0:T(8,128)(2,1)} %get-tuple-element.46.grad_ref, bf16[1024,2048]{1,0:T(8,128)(2,1)} %get-tuple-element.47.hidden_ref), custom_call_target="tpu_custom_call" | custom-call | flops 19327352832 | bytes 18874368 | tf_op jit(solution)/shard_map/pallas_call | solution.py:722
  554.6 94.7 %shard_map.222 = bf16[1024,1536]{1,0:T(8,128)(2,1)} custom-call(bf16[1024,1536]{1,0:T(8,128)(2,1)} %get-tuple-element.32.own, f32[1024,1536]{1,0:T(8,128)} %get-tuple-element.33.state_ref), custom_call_target="tpu_custom_call" | custom-call | bytes 12582912 | tf_op jit(solution)/shard_map/pallas_call | solution.py:586
  657.0 64.5 %reduce-scatter.8.cloned.1.call-done = bf16[192,6144]{1,0:T(8,128)(2,1)} async-done(((bf16[1536,6144]{1,0:T(8,128)(2,1)}), bf16[192,6144]{1,0:T(8,128)(2,1)}) %reduce-scatter.8.cloned.1.call-update) | async-done | bytes 2359312 | tf_op jit(solution)/shard_map/reduce_scatter | solution.py:740
  721.4 3.4 slice.88
  724.9 4.2 reshape.127
  730.2 1.6 copy.129
  731.8 1.6 copy.130
  736.5 1.7 copy.151
  739.5 1.7 copy.152
  (90 shorter events, 28.7 us)
Async XLA Ops:
  7.2 11.9 %copy-start = (bf16[16,128,192]{1,2,0:T(8,128)(2,1)S(1)}, bf16[16,128,192]{1,2,0:T(8,128)(2,1)}, u32[]{:S(2)}) copy-start(bf16[16,128,192]{1,2,0:T(8,128)(2,1)} %param.24) | copy-start | bytes 2359300
  7.2 6.4 copy-start.10
  7.2 41.3 %all-gather.3.cloned.1.call-start = ((), (), s32[]{:S(2)}) async-start(), calls=%async_computation.3 | async-start | bytes 3981312 | tf_op jit(solution)/shard_map/all_gather | solution.py:639
  11.6 153.9 %all-gather.5.cloned.1.call-start = ((), (), s32[]{:S(2)}) async-start(), calls=%async_computation.4 | async-start | bytes 21233664 | tf_op jit(solution)/shard_map/all_gather | solution.py:652
  19.2 3.1 copy-start.12
  22.3 10.8 %copy-start.2 = (bf16[1024,1536]{1,0:T(8,128)(2,1)S(1)}, bf16[1024,1536]{1,0:T(8,128)(2,1)}, u32[]{:S(2)}) copy-start(bf16[1024,1536]{1,0:T(8,128)(2,1)} %x_ref.3) | copy-start | bytes 9437188
  22.3 244.3 %all-reduce.3.cloned.1.call-start = ((), (), s32[]{:S(2)}) async-start(), calls=%async_computation.5 | async-start | bytes 1048576 | tf_op jit(solution)/shard_map/psum | solution.py:717
  229.4 419.9 %reduce-scatter.10.cloned.1.call-start = ((), (), s32[]{:S(2)}) async-start(), calls=%async_computation.7 | async-start | bytes 884736
  408.4 96.3 %copy-start.11 = (f32[8,1536]{1,0:T(8,128)S(1)}, f32[8,1536]{1,0:T(8,128)}, u32[]{:S(2)}) copy-start(f32[8,1536]{1,0:T(8,128)} %get-tuple-element.42) | copy-start | bytes 147460
  408.4 98.5 %copy-start.8 = (bf16[1024,1536]{1,0:T(8,128)(2,1)S(1)}, bf16[1024,1536]{1,0:T(8,128)(2,1)}, u32[]{:S(2)}) copy-start(bf16[1024,1536]{1,0:T(8,128)(2,1)} %get-tuple-element.30.x_ref) | copy-start | bytes 9437188
  408.4 98.5 %copy-start.15 = (bf16[1024,128]{1,0:T(8,128)(2,1)S(1)}, bf16[1024,128]{1,0:T(8,128)(2,1)}, u32[]{:S(2)}) copy-start(bf16[1024,128]{1,0:T(8,128)(2,1)} %get-tuple-element.45) | copy-start | bytes 786436
  506.8 144.8 %reduce-scatter.12.cloned.1.call-start = ((), (), s32[]{:S(2)}) async-start(), calls=%async_computation.8 | async-start | bytes 3981312
  506.9 1.9 copy-start.13
  506.9 2.1 copy-start.14
  509.0 1.9 copy-start.3
  509.0 2.3 copy-start.9
  517.9 1.9 copy-start.5
  518.0 203.5 %reduce-scatter.8.cloned.1.call-start = ((), (), s32[]{:S(2)}) async-start(), calls=%async_computation.6 | async-start | bytes 21233664 | tf_op jit(solution)/shard_map/reduce_scatter | solution.py:740
  730.2 3.3 copy-start.4
  734.0 2.5 copy-start.6
  736.5 3.0 copy-start.7
  736.5 4.7 copy-start.1
Sparse Core Ops, SparseCore 0:
  11.8 36.6 all-gather.2
  50.9 98.7 all-gather.4
  229.5 37.0 all-reduce.2
  507.0 33.3 reduce-scatter.9
  543.7 48.0 reduce-scatter.11
  595.3 126.0 reduce-scatter.7

commit v3 on v2

--- a/solution.py
+++ b/solution.py
@@ -59,13 +59,16 @@
     return jnp.concatenate([table] * (wide // LANES), 1)
 
 
-def line_scratch(rows, width, chunks):
-    buffer = pltpu.VMEM((rows, width), bf16)
-    sems = pltpu.SemaphoreType.DMA((chunks,))
-    return [buffer] * 4 + [sems] * 4
-
-
-def line_barrier(n, me, others=()):
+SLOTS = 4
+
+
+def line_scratch(rows, width, size):
+    sems = pltpu.SemaphoreType.DMA((rows // size,))
+    slots = pltpu.VMEM((SLOTS * size, width), bf16)
+    return [pltpu.VMEM((2 * rows, width), bf16), slots, slots, *[sems] * 4]
+
+
+def greet(me, n, others=()):
     barrier = pltpu.get_barrier_semaphore()
 
     @pl.when(me > 0)
@@ -87,108 +90,152 @@
 
 
 class Line:
-    def __init__(self, n, me, chunks, own, finish, scratch):
-        self.n, self.me, self.chunks, self.own, self.finish = n, me, chunks, own, finish
-        self.from_left, self.from_right, self.to_right, self.to_left = scratch[:4]
-        self.send_right, self.recv_left, self.send_left, self.recv_right = scratch[4:]
-        self.size = own.shape[0] // chunks
-        self.steps = chunks + n - 1
-
-    def clear(self):
-        @pl.when(self.me == 0)
-        def _():
-            self.from_left[...] = jnp.zeros_like(self.from_left)
-
-        @pl.when(self.me == self.n - 1)
-        def _():
-            self.from_right[...] = jnp.zeros_like(self.from_right)
+    def __init__(self, n, me, own, finish, scratch, base=0, lag=0, hop=1):
+        self.n, self.me, self.own, self.finish = n, me, own, finish
+        self.arrived, self.to_right, self.to_left = scratch[:3]
+        self.send_right, self.recv_left, self.send_left, self.recv_right = scratch[3:]
+        self.size = self.to_right.shape[0] // SLOTS
+        self.total = self.arrived.shape[0] // 2
+        self.chunks = self.total // self.size
+        self.base, self.lag, self.hop = base, lag, hop
+        self.steps = self.chunks + lag + hop * (n - 3)
+        self.middle = (me > 0) & (me < n - 1)
 
     def rows(self, c):
+        return aligned(self.base + c * self.size, self.size)
+
+    def left_rows(self, c):
         return aligned(c * self.size, self.size)
 
-    def right(self, c):
+    def right_rows(self, c):
+        return aligned(self.total + c * self.size, self.size)
+
+    def slot(self, c):
+        return aligned(lax.rem(c, SLOTS) * self.size, self.size)
+
+    def right(self, c, end=False):
         return pltpu.make_async_remote_copy(
-            src_ref=self.to_right.at[self.rows(c)],
-            dst_ref=self.from_left.at[self.rows(c)],
+            src_ref=self.own.at[self.rows(c)] if end else self.to_right.at[self.slot(c)],
+            dst_ref=self.arrived.at[self.left_rows(c)],
             send_sem=self.send_right.at[c],
             recv_sem=self.recv_left.at[c],
             device_id={"tp": lax.rem(self.me + 1, self.n)},
             device_id_type=MESH,
         )
 
-    def left(self, c):
+    def left(self, c, end=False):
         return pltpu.make_async_remote_copy(
-            src_ref=self.to_left.at[self.rows(c)],
-            dst_ref=self.from_right.at[self.rows(c)],
+            src_ref=self.own.at[self.rows(c)] if end else self.to_left.at[self.slot(c)],
+            dst_ref=self.arrived.at[self.right_rows(c)],
             send_sem=self.send_left.at[c],
             recv_sem=self.recv_right.at[c],
             device_id={"tp": lax.rem(self.me + self.n - 1, self.n)},
             device_id_type=MESH,
         )
 
+    def offer(self, c):
+        @pl.when(self.me == 0)
+        def _():
+            self.right(c, True).start()
+
+        @pl.when(self.me == self.n - 1)
+        def _():
+            self.left(c, True).start()
+
     def step(self, t):
         n, me, chunks = self.n, self.me, self.chunks
-        to_go = t - me
-
-        @pl.when((me < n - 1) & (to_go >= 0) & (to_go < chunks))
-        def _():
-            rows = self.rows(to_go)
-
-            @pl.when(me > 0)
-            def _():
-                self.right(to_go).wait_recv()
-
-            total = self.own[rows].astype(f32) + self.from_left[rows].astype(f32)
-            self.to_right[rows] = total.astype(bf16)
-            self.right(to_go).start()
-
-        to_come = t - (n - 1 - me)
-
-        @pl.when((me > 0) & (to_come >= 0) & (to_come < chunks))
-        def _():
-            rows = self.rows(to_come)
-
-            @pl.when(me < n - 1)
-            def _():
-                self.left(to_come).wait_recv()
-
-            total = self.own[rows].astype(f32) + self.from_right[rows].astype(f32)
-            self.to_left[rows] = total.astype(bf16)
-            self.left(to_come).start()
-
-        done = t - jnp.maximum(me, n - 1 - me)
-
-        @pl.when((done >= 0) & (done < chunks))
-        def _():
-            @pl.when(me == 0)
-            def _():
-                self.left(done).wait_recv()
-
-            @pl.when(me == n - 1)
-            def _():
-                self.right(done).wait_recv()
-
+        go, come = t - self.lag - self.hop * (me - 1), t - self.lag - self.hop * (n - 2 - me)
+        done = jnp.minimum(go, come)
+        nearer_left = me < n - 1 - me
+
+        def arrival(c):
+            return self.middle & (c >= 0) & (c < chunks)
+
+        @pl.when(arrival(go) & nearer_left)
+        def _():
+            self.right_pass(go)
+
+        @pl.when(arrival(come))
+        def _():
+            self.left_pass(come)
+
+        @pl.when(arrival(go) & jnp.logical_not(nearer_left))
+        def _():
+            self.right_pass(go)
+
+        @pl.when(arrival(done))
+        def _():
             rows = self.rows(done)
             total = (
                 self.own[rows].astype(f32)
-                + self.from_left[rows].astype(f32)
-                + self.from_right[rows].astype(f32)
+                + self.arrived[self.left_rows(done)].astype(f32)
+                + self.arrived[self.right_rows(done)].astype(f32)
             )
             self.finish(done, rows, total)
 
-    def sent(self):
-        def one(c, carry):
-            @pl.when(self.me < self.n - 1)
-            def _():
+    def right_pass(self, c):
+        self.right(c).wait_recv()
+
+        @pl.when(c >= SLOTS)
+        def _():
+            self.right(c - SLOTS).wait_send()
+
+        total = self.own[self.rows(c)].astype(f32) + self.arrived[self.left_rows(c)].astype(f32)
+        self.to_right[self.slot(c)] = total.astype(bf16)
+        self.right(c).start()
+
+    def left_pass(self, c):
+        self.left(c).wait_recv()
+
+        @pl.when(c >= SLOTS)
+        def _():
+            self.left(c - SLOTS).wait_send()
+
+        total = self.own[self.rows(c)].astype(f32) + self.arrived[self.right_rows(c)].astype(f32)
+        self.to_left[self.slot(c)] = total.astype(bf16)
+        self.left(c).start()
+
+    def rest(self, start):
+        @pl.when(self.middle)
+        def _():
+            loop(start, self.steps, self.step)
+
+            def sent(c):
                 self.right(c).wait_send()
-
-            @pl.when(self.me > 0)
-            def _():
                 self.left(c).wait_send()
 
-            return carry
-
-        lax.fori_loop(0, self.chunks, one, 0)
+            loop(max(self.chunks - SLOTS, 0), self.chunks, sent)
+
+        @pl.when(jnp.logical_not(self.middle))
+        def _():
+            def end(c):
+                @pl.when(self.me == 0)
+                def _():
+                    self.left(c).wait_recv()
+
+                @pl.when(self.me == self.n - 1)
+                def _():
+                    self.right(c).wait_recv()
+
+                rows = self.rows(c)
+                other = aligned(
+                    jnp.where(self.me == 0, self.total, 0) + c * self.size, self.size
+                )
+                total = self.own[rows].astype(f32) + self.arrived[other].astype(f32)
+                self.finish(c, rows, total)
+
+            loop(0, self.chunks, end)
+
+            def sent(c):
+                @pl.when(self.me == 0)
+                def _():
+                    self.right(c, True).wait_send()
+
+                @pl.when(self.me == self.n - 1)
+                def _():
+                    self.left(c, True).wait_send()
+
+            loop(0, self.chunks, sent)
 
 
 def loop(low, high, body):
@@ -268,9 +315,8 @@
         raised = jnp.where(named, jnp.exp(logits - top), 0.0)
         gates_ref[rows] = raised / jnp.sum(raised, -1, keepdims=True)
 
-    line = Line(n, me, own.shape[0] // 128, own, finish, scratch)
-    line_barrier(n, me, [{"ctx": places.after(o)} for o in range(1, nc)])
-    line.clear()
+    line = Line(n, me, own, finish, scratch, hop=2)
+    greet(me, n, [{"ctx": places.after(o)} for o in range(1, nc)])
 
     def kv_copy(s, part, o, rank):
         where = kv_all.at[s, places.rows(rank, part)]
@@ -325,13 +371,13 @@
                 mixed_ref[rows, h * HEAD_SIZE : (h + 1) * HEAD_SIZE] = dot(probs, value).astype(bf16)
             own[rows] = dot(mixed_ref[rows], wout_ref[...], (1, 1)).astype(bf16)
             per = quarter // line.size
-            for i in range(per):
-                line.step((2 * s + part) * per + i)
+            first = (2 * s + part) * per
+            loop(first, first + per, line.offer)
+            loop(first, first + per, line.step)
 
     loop(0, seqs, attend)
-    loop(line.chunks, line.steps, line.step)
     kv_ref[...] = kv_all[...]
-    line.sent()
+    line.rest(line.chunks)
 
     def kv_sent(s):
         for part in range(2):
@@ -341,20 +387,131 @@
     loop(0, seqs, kv_sent)
 
 
-def moe_kernel(x_ref, dy_ref, gates_ref, w_ref, hidden_ref, grad_ref, dots_ref, out_ref, dx_ref):
-    rows = x_ref.shape[0]
+def expert_kernel(
+    n,
+    x_ref,
+    dy_ref,
+    gates_ref,
+    w_ref,
+    state_hbm,
+    router_ref,
+    gain_ref,
+    hidden_ref,
+    grad_ref,
+    out_ref,
+    dstate_hbm,
+    dlogits_ref,
+    dgain_ref,
+    own,
+    dots,
+    dots_all,
+    dots_rows,
+    state_in,
+    dstate_out,
+    state_sem,
+    dstate_sem,
+    send_dots,
+    recv_dots,
+    *scratch,
+):
+    me = lax.axis_index("tp")
+    block, steps = pl.program_id(0), pl.num_programs(0)
+    size_in = x_ref.shape[0]
+    width = x_ref.shape[1]
     pair = hidden_ref.shape[1] // (E // 2)
     single = pair // 2
     gu_wide = grad_ref.shape[1]
-    lane = lax.broadcasted_iota(jnp.int32, (rows, LANES), 1)
-    first = lax.broadcasted_iota(jnp.int32, (rows, pair), 1) < single
-    dots_ref[...] = jnp.zeros_like(dots_ref)
+    here = aligned(block * size_in, size_in)
+
+    def dots_copy(o, b):
+        mine = dots_all.at[me, b]
+        return pltpu.make_async_remote_copy(
+            src_ref=mine,
+            dst_ref=mine,
+            send_sem=send_dots.at[o - 1, b],
+            recv_sem=recv_dots.at[o - 1, b],
+            device_id={"tp": lax.rem(me + o, n)},
+            device_id_type=MESH,
+        )
+
+    def state_copy(c):
+        return pltpu.make_async_copy(
+            state_hbm.at[line.rows(c)], state_in.at[lax.rem(c, 2)], state_sem.at[lax.rem(c, 2)]
+        )
+
+    def dstate_copy(c):
+        return pltpu.make_async_copy(
+            dstate_out.at[lax.rem(c, 2)], dstate_hbm.at[line.rows(c)], dstate_sem.at[lax.rem(c, 2)]
+        )
+
+    def finish(c, rows, total):
+        per = size_in // line.size
+
+        @pl.when(lax.rem(c, per) == 0)
+        def _():
+            b = c // per
+            for o in range(1, n):
+                dots_copy(o, b).wait_recv()
+            summed = dots_all[0, b]
+            for i in range(1, n):
+                summed = summed + dots_all[i, b]
+            summed = jnp.concatenate(
+                [summed, jnp.zeros((LANES - summed.shape[0], summed.shape[1]), f32)], 0
+            )
+            dots_rows[aligned(b * size_in, size_in)] = summed.T
+
+        @pl.when(c == 0)
+        def _():
+            state_copy(c).start()
+
+        @pl.when(c + 1 < line.chunks)
+        def _():
+            state_copy(c + 1).start()
+
+        state_copy(c).wait()
+
+        @pl.when(c >= 2)
+        def _():
+            dstate_copy(c - 2).wait()
+
+        gates = gates_ref[rows]
+        lane = lax.broadcasted_iota(jnp.int32, gates.shape, 1)
+        product = gates * dots_rows[rows]
+        dlogits = product - gates * jnp.sum(product, -1, keepdims=True)
+        dlogits = jnp.where(lane < E, dlogits, 0.0).astype(bf16)
+        dlogits_ref[rows] = dlogits
+        dn = total + dot(dlogits, router_ref[...], (1, 1))
+        state = state_in[lax.rem(c, 2)]
+        scale = lax.rsqrt(jnp.mean(state * state, -1, keepdims=True) + epsilon)
+        unit = state * scale
+        scaled = dn * gain_ref[...]
+        inner = jnp.mean(scaled * unit, -1, keepdims=True)
+        dstate_out[lax.rem(c, 2)] = dy_ref[rows].astype(f32) + scale * (scaled - unit * inner)
+        dstate_copy(c).start()
+        dgain_ref[...] += folded(dn * unit)
+
+    line = Line(n, me, own, finish, scratch, lag=size_in // (scratch[1].shape[0] // SLOTS), hop=2)
+    per = size_in // line.size
+
+    @pl.when(block == 0)
+    def _():
+        barrier = pltpu.get_barrier_semaphore()
+        for o in range(1, n):
+            pl.semaphore_signal(
+                barrier, inc=1, device_id={"tp": lax.rem(me + o, n)}, device_id_type=MESH
+            )
+        pl.semaphore_wait(barrier, n - 1)
+        dgain_ref[...] = jnp.zeros_like(dgain_ref)
+
+    lane = lax.broadcasted_iota(jnp.int32, (size_in, LANES), 1)
+    first = lax.broadcasted_iota(jnp.int32, (size_in, pair), 1) < single
+    dots[...] = jnp.zeros_like(dots)
 
     def experts(p):
         gu = dot(x_ref[...], w_ref[:, aligned(p * 2 * pair, 2 * pair)])
-        raw = dot(dy_ref[...], w_ref[:, aligned(gu_wide + p * pair, pair)])
+        raw = dot(dy_ref[here], w_ref[:, aligned(gu_wide + p * pair, pair)])
         gate_pre, up_pre = gu[:, :pair], gu[:, pair:]
-        gates = gates_ref[...]
+        gates = gates_ref[here]
         gate = jnp.where(
             first,
             jnp.sum(jnp.where(lane == 2 * p, gates, 0.0), 1, keepdims=True),
@@ -365,7 +522,7 @@
         hidden = (silu * up_pre).astype(bf16).astype(f32)
         hidden_ref[:, aligned(p * pair, pair)] = (hidden * gate).astype(bf16)
         both = hidden * raw
-        dots_ref[...] += jnp.where(
+        dots[...] += jnp.where(
             lane == 2 * p, jnp.sum(both[:, :single], 1, keepdims=True), 0.0
         ) + jnp.where(lane == 2 * p + 1, jnp.sum(both[:, single:], 1, keepdims=True), 0.0)
         dh = raw * gate
@@ -374,19 +531,58 @@
         ).astype(bf16)
         grad_ref[:, aligned(p * 2 * pair + pair, pair)] = (dh * silu).astype(bf16)
 
-    loop(0, E // 2, experts)
     tile = 256
 
     def outward(i):
         at = aligned(i * tile, tile)
         out_ref[:, at] = dot(hidden_ref[...], w_ref[at, gu_wide:], (1, 1)).astype(bf16)
-        dx_ref[:, at] = dot(grad_ref[...], w_ref[at, :gu_wide], (1, 1)).astype(bf16)
-
-    loop(0, out_ref.shape[1] // tile, outward)
-
-
-def weight_kernel(gu_blocks, x_ref, dy_ref, grad_ref, hidden_ref, out_ref):
+        own[here, at] = dot(grad_ref[...], w_ref[at, :gu_wide], (1, 1)).astype(bf16)
+
+    def experts_step(i):
+        loop(i * (E // 4), (i + 1) * (E // 4), experts)
+        line.step(block * per + i)
+
+    loop(0, 2, experts_step)
+    dots_all[me, block] = dots[...].T[:E]
+    for o in range(1, n):
+        dots_copy(o, block).start()
+    tiles = width // tile // (per - 2)
+
+    def outward_step(i):
+        loop(i * tiles, (i + 1) * tiles, outward)
+        line.step(block * per + 2 + i)
+
+    loop(0, per - 2, outward_step)
+    loop(block * per, block * per + per, line.offer)
+
+    @pl.when(block == steps - 1)
+    def _():
+        line.rest(line.chunks)
+        for c in range(line.chunks - 2, line.chunks):
+            dstate_copy(c).wait()
+
+        def dots_sent(b):
+            for o in range(1, n):
+                dots_copy(o, b).wait_send()
+
+        loop(0, steps, dots_sent)
+
+
+def weight_kernel(
+    n, gu_blocks, x_ref, dy_ref, grad_ref, hidden_ref, moe_ref, state_ref, out_ref, act_ref, *scratch
+):
+    me = lax.axis_index("tp")
     step = pl.program_id(0)
+
+    def finish(c, rows, total):
+        act_ref[rows] = (state_ref[rows] + total).astype(bf16)
+
+    line = Line(n, me, moe_ref, finish, scratch, lag=1, hop=3)
+
+    @pl.when(step == 0)
+    def _():
+        greet(me, n)
+        loop(0, line.chunks, line.offer)
 
     @pl.when(step < gu_blocks)
     def _():
@@ -396,62 +592,19 @@
     def _():
         out_ref[...] = dot(dy_ref[...], hidden_ref[...]).astype(bf16)
 
-
-def middle_kernel(
+    line.step(step)
+
+    @pl.when(step == pl.num_programs(0) - 1)
+    def _():
+        line.rest(pl.num_programs(0))
+
+
+def back_kernel(
     n,
-    own,
+    nc,
+    base,
+    moe_ref,
     state_ref,
-    dy_ref,
-    gates_ref,
-    dots_ref,
-    router_ref,
-    gain_ref,
-    dstate_ref,
-    dlogits_ref,
-    dgain_ref,
-    *scratch,
-):
-    me = lax.axis_index("tp")
-    dgain_ref[...] = jnp.zeros_like(dgain_ref)
-
-    def finish(c, rows, total):
-        gates = gates_ref[rows]
-        lane = lax.broadcasted_iota(jnp.int32, gates.shape, 1)
-        product = gates * dots_ref[rows]
-        dlogits = product - gates * jnp.sum(product, -1, keepdims=True)
-        dlogits = jnp.where(lane < E, dlogits, 0.0).astype(bf16)
-        dlogits_ref[rows] = dlogits
-        dn = total + dot(dlogits, router_ref[...], (1, 1))
-        state = state_ref[rows]
-        scale = lax.rsqrt(jnp.mean(state * state, -1, keepdims=True) + epsilon)
-        unit = state * scale
-        scaled = dn * gain_ref[...]
-        inner = jnp.mean(scaled * unit, -1, keepdims=True)
-        dstate_ref[rows] = dy_ref[rows].astype(f32) + scale * (scaled - unit * inner)
-        dgain_ref[...] += folded(dn * unit)
-
-    line = Line(n, me, own.shape[0] // 64, own, finish, scratch)
-    line_barrier(n, me)
-    line.clear()
-    loop(0, line.steps, line.step)
-    line.sent()
-
-
-def output_kernel(n, own, state_ref, out_ref, *scratch):
-    me = lax.axis_index("tp")
-
-    def finish(c, rows, total):
-        out_ref[rows] = (state_ref[rows] + total).astype(bf16)
-
-    line = Line(n, me, own.shape[0] // 64, own, finish, scratch)
-    line_barrier(n, me)
-    line.clear()
-    loop(0, line.steps, line.step)
-    line.sent()
-
-
-def back_kernel(
-    nc,
     dstate_ref,
     wout_ref,
     query_ref,
@@ -460,25 +613,30 @@
     sin_ref,
     low_ref,
     dqkv_ref,
+    act_ref,
     dmixed,
     dquery,
     dkv,
     dkv_in,
     send_kv,
     recv_kv,
+    *scratch,
 ):
+    me = lax.axis_index("tp")
     places = Places(nc)
     quarter = places.quarter
     seqs = kv_ref.shape[0]
     q_wide, k_wide = query_ref.shape[1], kv_ref.shape[2] // 2
     group = q_wide // k_wide
     factor = 1.0 / math.sqrt(HEAD_SIZE)
-    barrier = pltpu.get_barrier_semaphore()
-    for o in range(1, nc):
-        pl.semaphore_signal(
-            barrier, inc=1, device_id={"ctx": places.after(o)}, device_id_type=MESH
-        )
-    pl.semaphore_wait(barrier, nc - 1)
+
+    def finish(c, rows, total):
+        act_ref[line.left_rows(c)] = (state_ref[rows] + total).astype(bf16)
+
+    line = Line(n, me, moe_ref, finish, scratch, base=base, lag=2, hop=3)
+    greet(me, n, [{"ctx": places.after(o)} for o in range(1, nc)])
+    loop(0, line.chunks, line.offer)
+    kv_heads = k_wide // HEAD_SIZE
 
     def kv_copy(s, part, o, rank):
         return pltpu.make_async_remote_copy(
@@ -526,6 +684,9 @@
                         dkv[s, :keys, lanes] = add
                     else:
                         dkv[s, :keys, lanes] += add
+                turn = ((2 * s + 1 - part) * kv_heads + k) * 2
+                line.step(turn)
+                line.step(turn + 1)
         for part in range(2):
             for o in range(1, nc):
                 kv_copy(s, part, o, places.after(o)).start()
@@ -548,13 +709,66 @@
             dqkv_ref[rows, q_wide + k_wide :] = mine[:, k_wide:].astype(bf16)
 
     loop(0, seqs, turn_back)
+    line.rest(4 * seqs * kv_heads)
 
 
 def tail_kernel(
-    n, dqkv_ref, wqkv_ref, x_ref, dstate_ref, gain_ref, out_ref, dgain_ref, own, *scratch
+    n,
+    nf,
+    nc,
+    dqkv_ref,
+    wqkv_ref,
+    x_ref,
+    dstate_ref,
+    gain_ref,
+    dgain_two_ref,
+    low_ref,
+    mixed_ref,
+    normed_two_ref,
+    dlogits_ref,
+    out_ref,
+    dgains_ref,
+    grads_ref,
+    own,
+    normed,
+    dgain,
+    gains_in,
+    grads,
+    grads_in,
+    send_gain,
+    recv_gain,
+    send_grad,
+    recv_grad,
+    *scratch,
 ):
     me = lax.axis_index("tp")
-    dgain_ref[...] = jnp.zeros_like(dgain_ref)
+    flat = lax.axis_index("fsdp") * nc + lax.axis_index("ctx")
+    peers, shard = grads.shape[0], grads.shape[1]
+    dgain[...] = jnp.zeros_like(dgain)
+
+    def peer(o):
+        other = lax.rem(flat + o, peers)
+        return {"fsdp": other // nc, "ctx": lax.rem(other, nc)}
+
+    def grad_copy(o):
+        return pltpu.make_async_remote_copy(
+            src_ref=grads.at[lax.rem(flat + o, peers)],
+            dst_ref=grads_in.at[o],
+            send_sem=send_grad.at[o],
+            recv_sem=recv_grad.at[o],
+            device_id=peer(o),
+            device_id_type=MESH,
+        )
+
+    def gain_copy(o):
+        return pltpu.make_async_remote_copy(
+            src_ref=gains_in.at[0],
+            dst_ref=gains_in.at[o],
+            send_sem=send_gain.at[o],
+            recv_sem=recv_gain.at[o],
+            device_id=peer(o),
+            device_id_type=MESH,
+        )
 
     def finish(c, rows, total):
         x = x_ref[rows].astype(f32)
@@ -563,22 +777,72 @@
         scaled = total * gain_ref[...]
         inner = jnp.mean(scaled * unit, -1, keepdims=True)
         out_ref[rows] = (dstate_ref[rows] + scale * (scaled - unit * inner)).astype(bf16)
-        dgain_ref[...] += folded(total * unit)
-
-    line = Line(n, me, own.shape[0] // 64, own, finish, scratch)
-    line_barrier(n, me)
-    line.clear()
+        dgain[...] += folded(total * unit)
+
+    line = Line(n, me, own, finish, scratch, hop=2)
+    greet(me, n, [peer(o) for o in range(1, peers)])
     block = 256
 
     def start(i):
         rows = aligned(i * block, block)
         own[rows] = dot(dqkv_ref[rows], wqkv_ref[...], (1, 1)).astype(bf16)
-        for j in range(block // line.size):
-            line.step(i * (block // line.size) + j)
+        per = block // line.size
+        loop(i * per, i * per + per, line.offer)
+        x = x_ref[rows].astype(f32)
+        scale = lax.rsqrt(jnp.mean(x * x, -1, keepdims=True) + epsilon)
+        normed[rows] = (x * scale * gain_ref[...]).astype(bf16)
 
     loop(0, own.shape[0] // block, start)
-    loop(line.chunks, line.steps, line.step)
-    line.sent()
+    wide, mid = dqkv_ref.shape[1], dqkv_ref.shape[1] + mixed_ref.shape[1]
+    span = max(LANES, shard * LANES // math.gcd(shard, LANES))
+    count = span // shard
+    turns = 2
+
+    def weights(i):
+        at = aligned(i * span, span)
+        to = pl.ds(i * count, count)
+
+        def put(lanes, value):
+            grads[to, :, lanes] = value.reshape(count, shard, value.shape[1]).astype(grads.dtype)
+
+        put(slice(0, wide), dot(normed[:, at], dqkv_ref[...], (0, 0)))
+        put(slice(wide, mid), dot(low_ref[:, at], mixed_ref[...], (0, 0)))
+        put(slice(mid, grads.shape[2]), dot(normed_two_ref[:, at], dlogits_ref[...], (0, 0)))
+        for j in range(turns):
+            line.step(i * turns + j)
+
+    spans = normed.shape[1] // span
+    loop(0, spans, weights)
+    loop(1, peers, lambda o: grad_copy(o).start())
+    line.rest(spans * turns)
+    one = jnp.sum(dgain[...], 0, keepdims=True)
+    two = jnp.sum(dgain_two_ref[...], 0, keepdims=True)
+    gains_in[0] = jnp.concatenate([one, two, jnp.zeros((6, one.shape[1]), f32)], 0)
+    loop(1, peers, lambda o: gain_copy(o).start())
+    grads_ref[...] = grads[flat].astype(f32)
+
+    def add_grad(o):
+        grad_copy(o).wait()
+        grads_ref[...] += grads_in[o].astype(f32)
+
+    loop(1, peers, add_grad)
+    loop(1, peers, lambda o: gain_copy(o).wait())
+    dgains_ref[...] = gains_in[0]
+
+    def add(o):
+        dgains_ref[...] += gains_in[o]
+
+    loop(1, peers, add)
+
+
+def split_kernel(ffn, grads_ref, gate_ref, up_ref, down_ref):
+    gu_wide = 2 * E * ffn
+    for e in range(E):
+        at = (e // 2) * 4 * ffn + (e % 2) * ffn
+        gate_ref[e] = grads_ref[:, at : at + ffn].astype(f32)
+        up_ref[e] = grads_ref[:, at + 2 * ffn : at + 3 * ffn].astype(f32)
+        at = gu_wide + e * ffn
+        down_ref[e] = grads_ref[:, at : at + ffn].astype(f32).T
 
 
 def call(kernel, outs, scratch, collective_id, operands, flops=0):
@@ -670,7 +934,7 @@
             pltpu.VMEM((rows, width), bf16),
             kv_sems,
             kv_sems,
-            *line_scratch(rows, width, rows // 128),
+            *line_scratch(rows, width, 32),
         ],
         0,
         (tokens, wqkv, wout, router, named, gain_one, gain_two, cos, sin),
@@ -682,74 +946,105 @@
     def by_rows(wide):
         return pl.BlockSpec((block, wide), lambda i: (i, 0))
 
-    hidden, gu_grad, dots, moe_part, dx_part = pl.pallas_call(
-        moe_kernel,
-        grid=(rows // block,),
+    def constant(*dims):
+        return pl.BlockSpec(
+            dims, lambda i: (0,) * len(dims), pipeline_mode=pl.Buffered(1)
+        )
+
+    anywhere = pl.BlockSpec(memory_space=pl.ANY)
+    blocks = rows // block
+    size = 64
+    dots_sems = pltpu.SemaphoreType.DMA((n - 1, blocks))
+    hidden, gu_grad, moe_part, dstate, dlogits, dgain_two = pl.pallas_call(
+        functools.partial(expert_kernel, n),
+        grid=(blocks,),
         out_shape=(
             shaped((rows, down_wide), bf16),
             shaped((rows, gu_wide), bf16),
-            shaped((rows, LANES), f32),
             shaped((rows, width), bf16),
-            shaped((rows, width), bf16),
+            shaped((rows, width), f32),
+            shaped((rows, LANES), bf16),
+            shaped((8, width), f32),
         ),
         in_specs=[
             by_rows(width),
-            by_rows(width),
-            by_rows(LANES),
-            pl.BlockSpec(
-                (width, gu_wide + down_wide), lambda i: (0, 0), pipeline_mode=pl.Buffered(1)
-            ),
+            constant(rows, width),
+            constant(rows, LANES),
+            constant(width, gu_wide + down_wide),
+            anywhere,
+            constant(width, LANES),
+            constant(1, width),
         ],
         out_specs=(
             by_rows(down_wide),
             by_rows(gu_wide),
-            by_rows(LANES),
             by_rows(width),
-            by_rows(width),
+            anywhere,
+            pl.BlockSpec((rows, LANES), lambda i: (0, 0)),
+            pl.BlockSpec((8, width), lambda i: (0, 0)),
         ),
-        compiler_params=pltpu.CompilerParams(vmem_limit_bytes=VMEM_BYTES),
+        scratch_shapes=[
+            pltpu.VMEM((rows, width), bf16),
+            pltpu.VMEM((block, LANES), f32),
+            pltpu.VMEM((n, blocks, E, block), f32),
+            pltpu.VMEM((rows, LANES), f32),
+            pltpu.VMEM((2, size, width), f32),
+            pltpu.VMEM((2, size, width), f32),
+            pltpu.SemaphoreType.DMA((2,)),
+            pltpu.SemaphoreType.DMA((2,)),
+            dots_sems,
+            dots_sems,
+            *line_scratch(rows, width, size),
+        ],
+        compiler_params=pltpu.CompilerParams(
+            collective_id=1, has_side_effects=True, vmem_limit_bytes=VMEM_BYTES
+        ),
         cost_estimate=pl.CostEstimate(
             flops=12 * rows * width * down_wide,
             bytes_accessed=2 * width * (gu_wide + down_wide),
             transcendentals=0,
         ),
-    )(normed_two, cotangent, gates, experts)
-    dots = lax.psum(dots[:, :E], "tp")
-    dots = jnp.pad(dots, ((0, 0), (0, LANES - E)))
+    )(normed_two, cotangent, gates, experts, state, router, gain_two)
 
     column = 512
+    early = rows * 3 // 8
     gu_blocks, down_blocks = gu_wide // column, down_wide // column
-    grad_experts = pl.pallas_call(
-        functools.partial(weight_kernel, gu_blocks),
+    grad_experts, act_early = pl.pallas_call(
+        functools.partial(weight_kernel, n, gu_blocks),
         grid=(gu_blocks + down_blocks,),
-        out_shape=shaped((width, gu_wide + down_wide), bf16),
+        out_shape=(shaped((width, gu_wide + down_wide), bf16), shaped((early, width), bf16)),
         in_specs=[
-            pl.BlockSpec((width, rows), lambda i: (0, 0), pipeline_mode=pl.Buffered(1)),
-            pl.BlockSpec((width, rows), lambda i: (0, 0), pipeline_mode=pl.Buffered(1)),
+            constant(width, rows),
+            constant(width, rows),
             pl.BlockSpec((rows, column), lambda i: (0, jnp.minimum(i, gu_blocks - 1))),
             pl.BlockSpec((rows, column), lambda i: (0, jnp.maximum(i - gu_blocks, 0))),
+            constant(early, width),
+            constant(early, width),
         ],
-        out_specs=pl.BlockSpec((width, column), lambda i: (0, i)),
-        compiler_params=pltpu.CompilerParams(vmem_limit_bytes=VMEM_BYTES),
+        out_specs=(
+            pl.BlockSpec((width, column), lambda i: (0, i)),
+            pl.BlockSpec((early, width), lambda i: (0, 0)),
+        ),
+        scratch_shapes=line_scratch(early, width, 32),
+        compiler_params=pltpu.CompilerParams(
+            collective_id=2, has_side_effects=True, vmem_limit_bytes=VMEM_BYTES
+        ),
         cost_estimate=pl.CostEstimate(
             flops=6 * rows * width * down_wide,
             bytes_accessed=2 * width * (gu_wide + down_wide),
             transcendentals=0,
         ),
-    )(normed_two.T, cotangent.T, gu_grad, hidden)
+    )(normed_two.T, cotangent.T, gu_grad, hidden, moe_part, state)
+    dstate, grad_experts = lax.optimization_barrier((dstate, grad_experts))
     grad_experts = lax.psum_scatter(grad_experts, both, scatter_dimension=0, tiled=True)
 
-    scratch = line_scratch(rows, width, rows // 64)
-    dstate, dlogits, dgain_two = call(
-        functools.partial(middle_kernel, n),
-        [shaped((rows, width), f32), shaped((rows, LANES), bf16), shaped((8, width), f32)],
-        scratch,
-        1,
-        (dx_part, state, cotangent, gates, dots, router, gain_two),
-    )
-    low, dqkv = call(
-        functools.partial(back_kernel, nc),
-        [shaped((rows, width), bf16), shaped((rows, qkv_wide), bf16)],
+    low, dqkv, act_late = call(
+        functools.partial(back_kernel, n, nc, early),
+        [
+            shaped((rows, width), bf16),
+            shaped((rows, qkv_wide), bf16),
+            shaped((rows - early, width), bf16),
+        ],
         [
             pltpu.VMEM((half // 2, q_wide), bf16),
             pltpu.VMEM((rows, q_wide), f32),
@@ -757,41 +1052,47 @@
             pltpu.VMEM((nc - 1, seqs, 2, half // 2, 2 * k_wide), f32),
             kv_sems,
             kv_sems,
+            *line_scratch(rows - early, width, 32),
         ],
-        2,
-        (dstate, wout, query, kv, cos, sin),
+        3,
+        (moe_part, state, dstate, wout, query, kv, cos, sin),
     )
-    inputs = tokens.astype(f32)
-    scale_one = lax.rsqrt(jnp.mean(inputs * inputs, -1, keepdims=True) + epsilon)
-    normed = (inputs * scale_one * gain_one).astype(bf16)
-    grad_qkv = jnp.einsum("td,tc->dc", normed, dqkv, preferred_element_type=f32)
-    grad_out = jnp.einsum("td,tc->dc", low, mixed, preferred_element_type=f32)
-    grad_router = jnp.einsum("td,te->de", normed_two, dlogits, preferred_element_type=f32)
-    grad_small = jnp.concatenate(
-        [grad_qkv.astype(bf16), grad_out.astype(bf16), grad_router.astype(bf16)], 1
+    activations = jnp.concatenate([act_early, act_late], 0)
+    nf = lax.axis_size("fsdp")
+    peers = nf * nc
+    link = bf16 if shard % 16 == 0 else f32
+    peer_sems = pltpu.SemaphoreType.DMA((peers,))
+    input_grad, dgains, grad_small = call(
+        functools.partial(tail_kernel, n, nf, nc),
+        [
+            shaped((rows, width), bf16),
+            shaped((8, width), f32),
+            shaped((shard, small.shape[1]), f32),
+        ],
+        [
+            pltpu.VMEM((rows, width), bf16),
+            pltpu.VMEM((rows, width), bf16),
+            pltpu.VMEM((8, width), f32),
+            pltpu.VMEM((peers, 8, width), f32),
+            pltpu.VMEM((peers, shard, small.shape[1]), link),
+            pltpu.VMEM((peers, shard, small.shape[1]), link),
+            *[peer_sems] * 4,
+            *line_scratch(rows, width, 32),
+        ],
+        4,
+        (dqkv, wqkv, tokens, dstate, gain_one, dgain_two, low, mixed, normed_two, dlogits),
     )
-    grad_small = lax.psum_scatter(grad_small, both, scatter_dimension=0, tiled=True)
-    input_grad, dgain_one = call(
-        functools.partial(tail_kernel, n),
-        [shaped((rows, width), bf16), shaped((8, width), f32)],
-        [pltpu.VMEM((rows, width), bf16), *scratch],
-        3,
-        (dqkv, wqkv, tokens, dstate, gain_one),
-    )
-    (activations,) = call(
-        functools.partial(output_kernel, n),
-        [shaped((rows, width), bf16)],
-        scratch,
-        4,
-        (moe_part, state),
-    )
-    dgains = jnp.stack([jnp.sum(dgain_one, 0), jnp.sum(dgain_two, 0)])
-    dgains = lax.psum_scatter(dgains, both, scatter_dimension=1, tiled=True)
-    grad_small = grad_small.astype(f32)
-    grad_experts = grad_experts.astype(f32)
-    grad_gu = grad_experts[:, :gu_wide].reshape(shard, pairs, 2, 2, ffn).transpose(2, 1, 3, 0, 4)
-    grad_gu = grad_gu.reshape(2, E, shard, ffn)
-    grad_down = grad_experts[:, gu_wide:].reshape(shard, E, ffn).transpose(1, 2, 0)
+    flat = lax.axis_index("fsdp") * nc + lax.axis_index("ctx")
+    dgains = lax.dynamic_slice_in_dim(dgains, flat * shard, shard, 1)
+    grad_gate, grad_up, grad_down = pl.pallas_call(
+        functools.partial(split_kernel, ffn),
+        out_shape=(
+            shaped((E, shard, ffn), f32),
+            shaped((E, shard, ffn), f32),
+            shaped((E, ffn, shard), f32),
+        ),
+        compiler_params=pltpu.CompilerParams(vmem_limit_bytes=VMEM_BYTES),
+    )(grad_experts)
     at = q_wide + k_wide
     return (
         activations,
@@ -803,8 +1104,8 @@
         grad_small[:, qkv_wide : qkv_wide + o_wide].T,
         dgains[1],
         grad_small[:, qkv_wide + o_wide : qkv_wide + o_wide + E],
-        grad_gu[0],
-        grad_gu[1],
+        grad_gate,
+        grad_up,
         grad_down,
     )
 

time: 756 us -> 522 us (0.69)
  waiting for transfers between devices: 116 us -> 12.6 us
  Pallas kernels: 530 us -> 430 us
  local copies, waits for them, and re-layouts: 65.8 us -> 42 us
    pallas_call x5 -> x3, Pallas kernels: 439 us -> 272 us  [call(): pl.pallas_call(kernel, out_shape=tuple(outs), in_specs=[WHOLE] * len(oper...]
    pallas_call x2 -> x3, Pallas kernels: 90.7 us -> 158 us  [the longest x1 111 us: per_device(): pl.pallas_call(functools.partial(expert_kernel, n), grid=(blocks,), out_s...]
    reduce_scatter x1, waiting for transfers between devices: 64.5 us -> 0.01 us  [per_device(): lax.psum_scatter(grad_experts, both, scatter_dimension=0, tiled=True)]
    psum x1 -> x0, waiting for transfers between devices: 37.2 us -> none  [per_device(): dots = lax.psum(dots[:, :E], 'tp')]
    unnamed x47 -> x17, local copies, waits for them, and re-layouts: 26.1 us -> 13.2 us
    slice x5 -> x0, local copies, waits for them, and re-layouts: 7.8 us -> none  [the longest x1 3.43 us: per_device(): grad_experts[:, :gu_wide].reshape(shard, pairs, 2, 2, ffn)]
  transfers between devices with their start and end apart: 6 -> 3, of which waited for: 3 -> 1; matrix products, arithmetic and copies ran while one was open for 7% -> 9% of each run, Pallas kernels for 31% -> 53%
where the time goes in v3:
time: 522 us; the launch traced here: 515 us
  Pallas kernels  430 us (82%)
  local copies, waits for them, and re-layouts  42 us (8%)
  other arithmetic  16.5 us (3%)
  between operations  14.2 us (3%)
  waiting for transfers between devices  12.6 us (2%)
    pallas_call x3, Pallas kernels, call(): pl.pallas_call(kernel, out_shape=tuple(outs), in_specs=[WHOLE] * len(oper...  272 us
    pallas_call x1, Pallas kernels, per_device(): pl.pallas_call(functools.partial(expert_kernel, n), grid=(blocks,), out_s...  111 us
    pallas_call x1, Pallas kernels, per_device(): pl.pallas_call(functools.partial(weight_kernel, n, gu_blocks), grid=(gu_b...  42.5 us
    unnamed x17, local copies, waits for them, and re-layouts  13.2 us
    all_gather x1, waiting for transfers between devices, per_device(): small_full = lax.all_gather(small, both, axis=0, tiled=True)  12.6 us
  transfers between devices with their start and end apart: 3, of which 1 were waited for; matrix products, arithmetic and copies ran while one was open for 9% of the time, Pallas kernels for 53%

profile of v3, /device:TPU:0, one launch (start us, length us, event | category | flops | bytes accessed | tf_op | source)
XLA Modules:
  0.0 515.4 jit_solution(8589480409659010704)
XLA Ops:
  7.3 0.8 broadcast_in_dim.16
  8.9 0.8 copy.95
  9.7 1.9 concatenate.9
  11.7 1.9 copy.104
  13.6 0.8 copy.105
  14.5 2.2 maximum_bitcast_fusion
  16.7 2.4 reshape.106
  19.2 3.1 pad_maximum_fusion.1
  22.7 0.8 copy.101.sin_ref
  23.6 0.8 copy.100.cos_ref
  24.6 5.8 %fusion = pred[1024,128]{1,0:T(8,128)(4,1)S(1)} fusion(s32[1024,8]{1,0:T(8,128)S(1)} %copy.98), kind=kLoop, calls=%fused_computation.1 | loop fusion | flops 1966080 | bytes 163840 | tf_op jit(solution)/shard_map/reduce_or | solution.py:918
  30.4 0.8 convert_element_type.11.named_ref
  31.3 4.6 copy.103
  35.9 12.6 %all-gather.3.cloned.1.call-done = bf16[1536,1152]{1,0:T(8,128)(2,1)} async-done(((bf16[192,1152]{1,0:T(8,128)(2,1)}), bf16[1536,1152]{1,0:T(8,128)(2,1)}) %all-gather.3.cloned.1.call-update) | async-done | bytes 3538960 | tf_op jit(solution)/shard_map/all_gather | solution.py:903
  48.5 1.2 slice_convert_fusion
  49.9 1.8 slice.55.router_ref
  51.7 2.4 slice.54.wout_ref
  54.1 3.0 slice.53.wqkv_ref
  57.7 103.9 %shard_map.220 = (bf16[1024,384]{1,0:T(8,128)(2,1)}, bf16[2,1024,256]{2,1,0:T(8,128)(2,1)}, bf16[1024,384]{1,0:T(8,128)(2,1)}, f32[1024,1536]{1,0:T(8,128)}, bf1...) custom-call(bf16[1024,1536]{1,0:T(8,128)(2,1)} %x_ref.3, bf16[1536,640]{1,0:T(8,128)(2,1)} %slice.53.wqkv_ref, ...), custom_call_target="tpu_custom_call" | custom-call | bytes 20328448 | tf_op jit(solution)/shard_map/pallas_call | solution.py:850
  161.6 4.6 copy.102
  166.3 110.8 %shard_map.221 = (bf16[1024,2048]{1,0:T(8,128)(2,1)}, bf16[1024,4096]{1,0:T(8,128)(2,1)}, bf16[1024,1536]{1,0:T(8,128)(2,1)}, f32[1024,1536]{1,0:T(8,128)}, bf16...) custom-call(bf16[1024,1536]{1,0:T(8,128)(2,1)} %get-tuple-element.37.x_ref.normed_two_ref, bf16[1024,1536]{1,0:T(8,128)(2,1)} %dy_ref.1, ...), custom_call_target="tpu_custom_call" | custom-call | flops 38654705664 | bytes 18874368 | tf_op jit(solution)/shard_map/pallas_call | solution.py:958
  277.0 42.5 %shard_map.222 = (bf16[1536,6144]{1,0:T(8,128)(2,1)}, bf16[384,1536]{1,0:T(8,128)(2,1)}) custom-call(bf16[1536,1024]{1,0:T(8,128)(2,1)} %bitcast.21, bf16[1536,1024]{1,0:T(8,128)(2,1)} %bitcast.20, bf16[1024,4096]{1,0:T(8,128)(2,1)} %get-tuple-element.40.grad_ref, bf16[1024,2048]{1,0:T(8,128)(2,1)} %get-tuple-element.41.hidden_ref, ...), custom_call_target="tpu_custom_call" | custom-call | flops 19327352832 | bytes 18874368 | tf_op jit(solution)/shard_map/pallas_call | solution.py:1012
  319.6 71.0 %shard_map.223 = (bf16[1024,1536]{1,0:T(8,128)(2,1)}, bf16[1024,640]{1,0:T(8,128)(2,1)}, bf16[640,1536]{1,0:T(8,128)(2,1)}) custom-call(bf16[1024,1536]{1,0:T(8,128)(2,1)} %get-tuple-element.42.moe_ref, f32[1024,1536]{1,0:T(8,128)} %get-tuple-element.39.state_hbm.state_ref, f32[1024,1536]{1,0:T(8,128)} %get-tuple-element.46.dstate_ref, ...), custom_call_target="tpu_custom_call" | custom-call | bytes 25690112 | tf_op jit(solution)/shard_map/pallas_call | solution.py:850
  390.6 97.4 %shard_map.224 = (bf16[1024,1536]{1,0:T(8,128)(2,1)}, f32[8,1536]{1,0:T(8,128)}, f32[192,1152]{1,0:T(8,128)}) custom-call(bf16[1024,640]{1,0:T(8,128)(2,1)} %get-tuple-element.50.dqkv_ref, bf16[1536,640]{1,0:T(8,128)(2,1)} %slice.53.wqkv_ref, bf16[1024,1536]{1,0:T(8,128)(2,1)} %x_ref.3, f32[1024,1536]{1,0:T(8,128)} %get-tuple-element.46.dstate_ref, ...), custom_call_target="tpu_custom_call" | custom-call | bytes 24188928 | tf_op jit(solution)/shard_map/pallas_call | solution.py:850
  488.0 0.9 slice.52
  489.5 1.4 fusion.2
  491.0 1.6 fusion.1
  492.6 1.9 slice_bitcast_fusion
  494.5 3.1 pad_maximum_fusion
  497.6 4.4 shard_map.225
  502.1 2.8 copy.110
  504.9 3.8 copy.116
  (30 shorter events, 3.2 us)
Async XLA Ops:
  7.2 11.9 %copy-start = (bf16[16,128,192]{1,2,0:T(8,128)(2,1)S(1)}, bf16[16,128,192]{1,2,0:T(8,128)(2,1)}, u32[]{:S(2)}) copy-start(bf16[16,128,192]{1,2,0:T(8,128)(2,1)} %param.24) | copy-start | bytes 2359300
  7.2 6.4 %copy-start.3 = (bf16[16,192,128]{2,1,0:T(8,128)(2,1)S(1)}, bf16[16,192,128]{2,1,0:T(8,128)(2,1)}, u32[]{:S(2)}) copy-start(bf16[16,192,128]{2,1,0:T(8,128)(2,1)} %param.23) | copy-start | bytes 2359300
  7.2 41.3 %all-gather.3.cloned.1.call-start = ((), (), s32[]{:S(2)}) async-start(), calls=%async_computation.1 | async-start | bytes 3981312 | tf_op jit(solution)/shard_map/all_gather | solution.py:903
  11.6 154.6 %all-gather.5.cloned.1.call-start = ((), (), s32[]{:S(2)}) async-start(), calls=%async_computation.2 | async-start | bytes 21233664 | tf_op jit(solution)/shard_map/all_gather | solution.py:916
  22.3 2.2 copy-start.4
  22.3 475.3 %reduce-scatter.2.cloned.1.call-start = ((), (), s32[]{:S(2)}) async-start(), calls=%async_computation.3 | async-start | bytes 21233664 | tf_op jit(solution)/shard_map/reduce_scatter | solution.py:1039
  390.6 103.9 %copy-start.2 = (bf16[640,1536]{1,0:T(8,128)(2,1)S(1)}, bf16[640,1536]{1,0:T(8,128)(2,1)}, u32[]{:S(2)}) copy-start(bf16[640,1536]{1,0:T(8,128)(2,1)} %get-tuple-element.49) | copy-start | bytes 5898244
  504.8 3.8 copy-start.1
Sparse Core Ops, SparseCore 0:
  11.8 36.6 all-gather.2
  50.3 98.7 all-gather.4
  319.7 158.0 reduce-scatter.1

commit v4 on v3

v4 whole, which is shorter than its diff:
```python
import functools
import math

import jax
import jax.numpy as jnp
from jax import lax
from jax.experimental import pallas as pl
from jax.experimental.pallas import tpu as pltpu
from jax.sharding import PartitionSpec as P

HEAD_SIZE = 64
TOPK = 8
E = 16
SEQUENCE_LENGTH = 1024
LANES = 128
VMEM_BYTES = 60 * 2**20

epsilon = 1e-06
f32 = jnp.float32
bf16 = jnp.bfloat16
MESH = pl.DeviceIdType.MESH
WHOLE = pl.BlockSpec(memory_space=pltpu.VMEM)


def placed(ranks, half):
    quarter = half // 2
    steps = jnp.arange(half, dtype=jnp.int32)
    early = ranks * quarter + steps
    late = SEQUENCE_LENGTH - (ranks + 1) * quarter + steps - quarter
    return jnp.where(steps < quarter, early, late)


def angle_tables(token_places):
    halfway = HEAD_SIZE // 2
    freqs = jnp.exp(
        jnp.arange(halfway, dtype=f32) * (-2.0 * math.log(10000.0) / HEAD_SIZE)
    )
    angles = token_places.astype(f32)[:, None] * freqs[None, :]
    copies = LANES // halfway
    return jnp.tile(jnp.cos(angles), (1, copies)), jnp.tile(jnp.sin(angles), (1, copies))


def aligned(start, size):
    return pl.ds(pl.multiple_of(start, size), size)


def dot(a, b, at=(1, 0)):
    return lax.dot_general(a, b, (((at[0],), (at[1],)), ((), ())), preferred_element_type=f32)


def swapped_halves(y):
    wide, halfway = y.shape[1], HEAD_SIZE // 2
    lane = lax.broadcasted_iota(jnp.int32, y.shape, 1)
    lower = lax.rem(lane, HEAD_SIZE) < halfway
    return jnp.where(lower, -pltpu.roll(y, wide - halfway, 1), pltpu.roll(y, halfway, 1))


def widened(table, wide):
    return jnp.concatenate([table] * (wide // LANES), 1)


SLOTS = 4


def line_scratch(rows, width, size):
    sems = pltpu.SemaphoreType.DMA((rows // size,))
    slots = pltpu.VMEM((SLOTS * size, width), bf16)
    return [pltpu.VMEM((2 * rows, width), bf16), slots, slots, *[sems] * 4]


def greet(me, n, others=()):
    barrier = pltpu.get_barrier_semaphore()

    @pl.when(me > 0)
    def _():
        pl.semaphore_signal(
            barrier, inc=1, device_id={"tp": lax.rem(me + n - 1, n)}, device_id_type=MESH
        )

    @pl.when(me < n - 1)
    def _():
        pl.semaphore_signal(
            barrier, inc=1, device_id={"tp": lax.rem(me + 1, n)}, device_id_type=MESH
        )

    for other in others:
        pl.semaphore_signal(barrier, inc=1, device_id=other, device_id_type=MESH)
    count = jnp.where(me > 0, 1, 0) + jnp.where(me < n - 1, 1, 0) + len(others)
    pl.semaphore_wait(barrier, count)


class Line:
    def __init__(self, n, me, own, finish, scratch, base=0, lag=0, hop=1):
        self.n, self.me, self.own, self.finish = n, me, own, finish
        self.arrived, self.to_right, self.to_left = scratch[:3]
        self.send_right, self.recv_left, self.send_left, self.recv_right = scratch[3:]
        self.size = self.to_right.shape[0] // SLOTS
        self.total = self.arrived.shape[0] // 2
        self.chunks = self.total // self.size
        self.base, self.lag, self.hop = base, lag, hop
        self.steps = self.chunks + lag + hop * (n - 2)
        self.middle = (me > 0) & (me < n - 1)

    def rows(self, c):
        return aligned(self.base + c * self.size, self.size)

    def left_rows(self, c):
        return aligned(c * self.size, self.size)

    def right_rows(self, c):
        return aligned(self.total + c * self.size, self.size)

    def slot(self, c):
        return aligned(lax.rem(c, SLOTS) * self.size, self.size)

    def right(self, c, end=False):
        return pltpu.make_async_remote_copy(
            src_ref=self.own.at[self.rows(c)] if end else self.to_right.at[self.slot(c)],
            dst_ref=self.arrived.at[self.left_rows(c)],
            send_sem=self.send_right.at[c],
            recv_sem=self.recv_left.at[c],
            device_id={"tp": lax.rem(self.me + 1, self.n)},
            device_id_type=MESH,
        )

    def left(self, c, end=False):
        return pltpu.make_async_remote_copy(
            src_ref=self.own.at[self.rows(c)] if end else self.to_left.at[self.slot(c)],
            dst_ref=self.arrived.at[self.right_rows(c)],
            send_sem=self.send_left.at[c],
            recv_sem=self.recv_right.at[c],
            device_id={"tp": lax.rem(self.me + self.n - 1, self.n)},
            device_id_type=MESH,
        )

    def offer(self, c):
        @pl.when(self.me == 0)
        def _():
            self.right(c, True).start()

        @pl.when(self.me == self.n - 1)
        def _():
            self.left(c, True).start()

    def step(self, t):
        n, me, chunks = self.n, self.me, self.chunks
        go, come = t - self.lag - self.hop * (me - 1), t - self.lag - self.hop * (n - 2 - me)
        done = jnp.minimum(go, come)
        nearer_left = me < n - 1 - me

        def inside(c):
            return (c >= 0) & (c < chunks)

        @pl.when(self.middle & inside(go) & nearer_left)
        def _():
            self.right_pass(go)

        @pl.when(self.middle & inside(come))
        def _():
            self.left_pass(come)

        @pl.when(self.middle & inside(go) & jnp.logical_not(nearer_left))
        def _():
            self.right_pass(go)

        @pl.when(inside(done))
        def _():
            @pl.when(me == 0)
            def _():
                self.left(done).wait_recv()
                self.right(done, True).wait_send()

            @pl.when(me == n - 1)
            def _():
                self.right(done).wait_recv()
                self.left(done, True).wait_send()

            rows = self.rows(done)
            at = done * self.size
            one = aligned(jnp.where(me == 0, self.total, 0) + at, self.size)
            two = aligned(jnp.where(me == n - 1, 0, self.total) + at, self.size)
            total = self.own[rows].astype(f32) + self.arrived[one].astype(f32)
            other = self.arrived[two].astype(f32)
            self.finish(done, rows, total + jnp.where(self.middle, other, 0.0))

    def right_pass(self, c):
        self.right(c).wait_recv()

        @pl.when(c >= SLOTS)
        def _():
            self.right(c - SLOTS).wait_send()

        total = self.own[self.rows(c)].astype(f32) + self.arrived[self.left_rows(c)].astype(f32)
        self.to_right[self.slot(c)] = total.astype(bf16)
        self.right(c).start()

    def left_pass(self, c):
        self.left(c).wait_recv()

        @pl.when(c >= SLOTS)
        def _():
            self.left(c - SLOTS).wait_send()

        total = self.own[self.rows(c)].astype(f32) + self.arrived[self.right_rows(c)].astype(f32)
        self.to_left[self.slot(c)] = total.astype(bf16)
        self.left(c).start()

    def rest(self, start):
        loop(start, self.steps, self.step)

        @pl.when(self.middle)
        def _():
            def sent(c):
                self.right(c).wait_send()
                self.left(c).wait_send()

            loop(max(self.chunks - SLOTS, 0), self.chunks, sent)


def loop(low, high, body):
    lax.fori_loop(low, high, lambda i, carry: (body(i), carry)[1], 0)


def folded(values):
    rows, width = values.shape
    return jnp.sum(values.reshape(rows // 8, 8, width), 0)


class Places:
    def __init__(self, nc):
        self.nc = nc
        self.c = lax.axis_index("ctx")
        self.quarter = SEQUENCE_LENGTH // nc // 2

    def slot(self, rank, part):
        return rank if part == 0 else 2 * self.nc - 1 - rank

    def rows(self, rank, part):
        return aligned(self.slot(rank, part) * self.quarter, self.quarter)

    def own(self, s, part):
        return aligned((2 * s + part) * self.quarter, self.quarter)

    def keys(self, part):
        return self.quarter * (self.nc if part == 0 else 2 * self.nc)

    def after(self, o):
        return lax.rem(self.c + o, self.nc)

    def before(self, o):
        return lax.rem(self.c + self.nc - o, self.nc)


def gather_kernel(
    nf,
    nc,
    ffn,
    query_ref,
    key_ref,
    value_ref,
    out_ref,
    router_ref,
    gain_one_ref,
    gain_two_ref,
    gate_ref,
    up_ref,
    down_ref,
    wqkv_ref,
    wout_ref,
    router_all_ref,
    gains_ref,
    experts_ref,
    small_all,
    send_f,
    recv_f,
    send_c,
    recv_c,
):
    f, c = lax.axis_index("fsdp"), lax.axis_index("ctx")
    shard = small_all.shape[1]
    kind = small_all.dtype
    mine = f * nc + c

    def from_f(o):
        return lax.rem(f + nf - o, nf)

    def to_peer(o):
        return {"fsdp": lax.rem(f + o, nf)}

    def to_near(p):
        return {"ctx": lax.rem(c + p, nc)}

    barrier = pltpu.get_barrier_semaphore()
    for other in [to_peer(o) for o in range(1, nf)] + [to_near(p) for p in range(1, nc)]:
        pl.semaphore_signal(barrier, inc=1, device_id=other, device_id_type=MESH)
    gains = [gain_one_ref[...].astype(f32), gain_two_ref[...].astype(f32)]
    blank = jnp.zeros((LANES - E - 2, shard), f32)
    last = jnp.concatenate([router_ref[...].astype(f32), *gains, blank], 0).T
    at = 0
    for piece in (query_ref[...], key_ref[...], value_ref[...], out_ref[...], last):
        small_all[mine, :, at : at + piece.shape[1]] = piece.astype(kind)
        at += piece.shape[1]
    pl.semaphore_wait(barrier, nf + nc - 2)

    def far_copy(o, rank):
        block = small_all.at[rank * nc + c]
        return pltpu.make_async_remote_copy(
            src_ref=block,
            dst_ref=block,
            send_sem=send_f.at[o],
            recv_sem=recv_f.at[o],
            device_id=to_peer(o),
            device_id_type=MESH,
        )

    def near_copy(p, o, rank):
        block = small_all.at[from_f(o) * nc + rank]
        return pltpu.make_async_remote_copy(
            src_ref=block,
            dst_ref=block,
            send_sem=send_c.at[p - 1, o],
            recv_sem=recv_c.at[p - 1, o],
            device_id=to_near(p),
            device_id_type=MESH,
        )

    def share(o):
        for p in range(1, nc):
            near_copy(p, o, c).start()

    loop(1, nf, lambda o: far_copy(o, f).start())
    share(0)
    for e in range(E):
        at = (e // 2) * 4 * ffn + (e % 2) * ffn
        experts_ref[:, at : at + ffn] = gate_ref[e]
        experts_ref[:, at + 2 * ffn : at + 3 * ffn] = up_ref[e]
        at = 2 * E * ffn + e * ffn
        experts_ref[:, at : at + ffn] = down_ref[e]

    def pass_on(o):
        far_copy(o, from_f(o)).wait_recv()
        share(o)

    loop(1, nf, pass_on)

    def shared(o):
        for p in range(1, nc):
            near_copy(p, o, lax.rem(c + nc - p, nc)).wait_recv()

    loop(0, nf, shared)
    at = 0
    for ref in (wqkv_ref, wout_ref, router_all_ref):
        rows, wide = ref.shape
        ref[...] = small_all[:, :, at : at + wide].reshape(rows, wide).astype(bf16)
        at += wide
    gains_ref[...] = router_all_ref[...].astype(f32).T[E : E + 8]
    loop(1, nf, lambda o: far_copy(o, f).wait_send())

    def near_sent(o):
        for p in range(1, nc):
            near_copy(p, o, c).wait_send()

    loop(0, nf, near_sent)


def front_kernel(
    n,
    nc,
    x_ref,
    wqkv_ref,
    wout_ref,
    router_ref,
    gains_ref,
    routes_ref,
    cos_ref,
    sin_ref,
    query_ref,
    kv_ref,
    mixed_ref,
    state_ref,
    normed_ref,
    gates_ref,
    kv_all,
    own,
    send_kv,
    recv_kv,
    *scratch,
):
    me = lax.axis_index("tp")
    places = Places(nc)
    quarter = places.quarter
    seqs = kv_ref.shape[0]
    q_wide, k_wide = query_ref.shape[1], kv_ref.shape[2] // 2
    group = q_wide // k_wide

    def finish(c, rows, total):
        state = x_ref[rows].astype(f32) + total
        scale = lax.rsqrt(jnp.mean(state * state, -1, keepdims=True) + epsilon)
        normed = (state * scale * gains_ref[1:2]).astype(bf16)
        state_ref[rows] = state.astype(bf16)
        normed_ref[rows] = normed
        routes = routes_ref[rows]
        lane = lax.broadcasted_iota(jnp.int32, (line.size, LANES), 1)
        named = lane == routes[:, :1]
        for k in range(1, TOPK):
            named = named | (lane == routes[:, k : k + 1])
        logits = jnp.where(named, dot(normed, router_ref[...]), -1e30)
        top = jnp.max(logits, -1, keepdims=True)
        raised = jnp.where(named, jnp.exp(logits - top), 0.0)
        gates_ref[rows] = raised / jnp.sum(raised, -1, keepdims=True)

    line = Line(n, me, own, finish, scratch, hop=2)

    greet(me, n, [{"ctx": places.after(o)} for o in range(1, nc)])

    def kv_copy(s, part, o, rank):
        where = kv_all.at[s, places.rows(rank, part)]
        return pltpu.make_async_remote_copy(
            src_ref=where,
            dst_ref=where,
            send_sem=send_kv.at[o - 1, s, part],
            recv_sem=recv_kv.at[o - 1, s, part],
            device_id={"ctx": places.after(o)},
            device_id_type=MESH,
        )

    def project(s):
        for part in range(2):
            rows = places.own(s, part)
            x = x_ref[rows].astype(f32)
            scale = lax.rsqrt(jnp.mean(x * x, -1, keepdims=True) + epsilon)
            normed = (x * scale * gains_ref[:1]).astype(bf16)
            qkv = dot(normed, wqkv_ref[...])
            qk = qkv[:, : q_wide + k_wide]
            here = pl.ds(part * quarter, quarter)
            cos, sin = widened(cos_ref[here], q_wide + k_wide), widened(sin_ref[here], q_wide + k_wide)
            rot = qk * cos + swapped_halves(qk) * sin
            query_ref[rows] = (rot[:, :q_wide] * (1.0 / math.sqrt(HEAD_SIZE))).astype(bf16)
            slot = places.rows(places.c, part)
            kv_all[s, slot, :k_wide] = rot[:, q_wide:].astype(bf16)
            kv_all[s, slot, k_wide:] = qkv[:, q_wide + k_wide :].astype(bf16)
            for o in range(1, nc):
                kv_copy(s, part, o, places.c).start()

    loop(0, seqs, project)

    def attend(s):
        for part in range(2):
            for o in range(1, nc):
                kv_copy(s, part, o, places.before(o)).wait_recv()
        for part in range(2):
            rows = places.own(s, part)
            keys = places.keys(part)
            base = places.slot(places.c, part) * quarter
            allowed = lax.broadcasted_iota(jnp.int32, (quarter, keys), 1) <= (
                base + lax.broadcasted_iota(jnp.int32, (quarter, keys), 0)
            )
            for h in range(q_wide // HEAD_SIZE):
                at = h // group * HEAD_SIZE
                query = query_ref[rows, h * HEAD_SIZE : (h + 1) * HEAD_SIZE]
                key = kv_all[s, :keys, at : at + HEAD_SIZE]
                value = kv_all[s, :keys, k_wide + at : k_wide + at + HEAD_SIZE]
                scores = jnp.where(allowed, dot(query, key, (1, 1)), -1e30)
                raised = jnp.exp(scores - jnp.max(scores, -1, keepdims=True))
                probs = (raised * (1.0 / jnp.sum(raised, -1, keepdims=True))).astype(bf16)
                mixed_ref[rows, h * HEAD_SIZE : (h + 1) * HEAD_SIZE] = dot(probs, value).astype(bf16)
            own[rows] = dot(mixed_ref[rows], wout_ref[...], (1, 1)).astype(bf16)
            per = quarter // line.size
            first = (2 * s + part) * per
            loop(first, first + per, line.offer)
            loop(first, first + per, line.step)

    loop(0, seqs, attend)
    kv_ref[...] = kv_all[...]
    line.rest(line.chunks)

    def kv_sent(s):
        for part in range(2):
            for o in range(1, nc):
                kv_copy(s, part, o, places.c).wait_send()

    loop(0, seqs, kv_sent)


def expert_kernel(
    n,
    x_ref,
    dy_ref,
    gates_ref,
    w_hbm,
    state_ref,
    router_ref,
    gains_ref,
    out_ref,
    grads_hbm,
    dstate_hbm,
    dlogits_ref,
    dgain_ref,
    own,
    hidden_ref,
    grad_ref,
    x_turned,
    dy_turned,
    dots,    dots_all,
    dots_rows,
    w_ref,
    dstate_out,
    w_sem,
    grads_sem,
    dstate_sem,
    send_dots,
    recv_dots,
    *scratch,
):
    me = lax.axis_index("tp")
    block, steps = pl.program_id(0), pl.num_programs(0)
    size_in, width = out_ref.shape
    pair = hidden_ref.shape[1] // (E // 2)
    single = pair // 2
    gu_wide = grad_ref.shape[1]
    here = aligned(block * size_in, size_in)

    def dots_copy(o, b):
        mine = dots_all.at[me, b]
        return pltpu.make_async_remote_copy(
            src_ref=mine,
            dst_ref=mine,
            send_sem=send_dots.at[o - 1, b],
            recv_sem=recv_dots.at[o - 1, b],
            device_id={"tp": lax.rem(me + o, n)},
            device_id_type=MESH,
        )

    def w_copies(p):
        spans = (aligned(p * 4 * pair, 4 * pair), aligned(gu_wide + p * 2 * pair, 2 * pair))
        return [
            pltpu.make_async_copy(w_hbm.at[:, span], w_ref.at[:, span], w_sem.at[i, p])
            for i, span in enumerate(spans)
        ]

    def dstate_copy(c):
        return pltpu.make_async_copy(
            dstate_out.at[lax.rem(c, 2)], dstate_hbm.at[line.rows(c)], dstate_sem.at[lax.rem(c, 2)]
        )

    def finish(c, rows, total):
        per = size_in // line.size

        @pl.when(lax.rem(c, per) == 0)
        def _():
            b = c // per
            for o in range(1, n):
                dots_copy(o, b).wait_recv()
            summed = dots_all[0, b]
            for i in range(1, n):
                summed = summed + dots_all[i, b]
            summed = jnp.concatenate(
                [summed, jnp.zeros((LANES - summed.shape[0], summed.shape[1]), f32)], 0
            )
            dots_rows[aligned(b * size_in, size_in)] = summed.T

        @pl.when(c >= 2)
        def _():
            dstate_copy(c - 2).wait()

        gates = gates_ref[rows]
        lane = lax.broadcasted_iota(jnp.int32, gates.shape, 1)
        product = gates * dots_rows[rows]
        dlogits = product - gates * jnp.sum(product, -1, keepdims=True)
        dlogits = jnp.where(lane < E, dlogits, 0.0).astype(bf16)
        dlogits_ref[rows] = dlogits
        dn = total + dot(dlogits, router_ref[...], (1, 1))
        state = state_ref[rows].astype(f32)
        scale = lax.rsqrt(jnp.mean(state * state, -1, keepdims=True) + epsilon)
        unit = state * scale
        scaled = dn * gains_ref[1:2]
        inner = jnp.mean(scaled * unit, -1, keepdims=True)
        dstate = dy_ref[rows].astype(f32) + scale * (scaled - unit * inner)
        dstate_out[lax.rem(c, 2)] = dstate.astype(bf16)
        dstate_copy(c).start()
        dgain_ref[...] += folded(dn * unit)

    line = Line(n, me, own, finish, scratch, lag=size_in // (scratch[1].shape[0] // SLOTS), hop=2)
    per = size_in // line.size

    @pl.when(block == 0)
    def _():
        barrier = pltpu.get_barrier_semaphore()
        for o in range(1, n):
            pl.semaphore_signal(
                barrier, inc=1, device_id={"tp": lax.rem(me + o, n)}, device_id_type=MESH
            )
        pl.semaphore_wait(barrier, n - 1)
        dgain_ref[...] = jnp.zeros_like(dgain_ref)

        def fetch(p):
            for copy in w_copies(p):
                copy.start()

        loop(0, E // 4, fetch)

    lane = lax.broadcasted_iota(jnp.int32, (size_in, LANES), 1)
    first = lax.broadcasted_iota(jnp.int32, (size_in, pair), 1) < single
    dots[...] = jnp.zeros_like(dots)

    def gating(p, gate_pre, up_pre, raw):
        gates = gates_ref[here]
        gate = jnp.where(
            first,
            jnp.sum(jnp.where(lane == 2 * p, gates, 0.0), 1, keepdims=True),
            jnp.sum(jnp.where(lane == 2 * p + 1, gates, 0.0), 1, keepdims=True),
        )
        sigma = jax.nn.sigmoid(gate_pre)
        silu = gate_pre * sigma
        hidden = (silu * up_pre).astype(bf16).astype(f32)
        hidden_ref[here, aligned(p * pair, pair)] = (hidden * gate).astype(bf16)
        both = hidden * raw
        dots[...] += jnp.where(
            lane == 2 * p, jnp.sum(both[:, :single], 1, keepdims=True), 0.0
        ) + jnp.where(lane == 2 * p + 1, jnp.sum(both[:, single:], 1, keepdims=True), 0.0)
        dh = raw * gate
        grad_ref[here, aligned(p * 2 * pair, pair)] = (
            dh * up_pre * (sigma + silu * (1.0 - sigma))
        ).astype(bf16)
        grad_ref[here, aligned(p * 2 * pair + pair, pair)] = (dh * silu).astype(bf16)

    def two_pairs(i):
        @pl.when(block == 0)
        def _():
            for copy in w_copies(i):
                copy.wait()

        gu = dot(x_ref[here], w_ref[:, aligned(i * 4 * pair, 4 * pair)])
        raw = dot(dy_ref[here], w_ref[:, aligned(gu_wide + i * 2 * pair, 2 * pair)])
        for j in range(2):
            at = 2 * j * pair
            gating(
                2 * i + j,
                gu[:, at : at + pair],
                gu[:, at + pair : at + 2 * pair],
                raw[:, j * pair : (j + 1) * pair],
            )

    tile = 512

    def outward(i):
        at = aligned(i * tile, tile)
        carried = jnp.where(me == n // 2, state_ref[here, at].astype(f32), 0.0)
        moe = dot(hidden_ref[here], w_ref[at, gu_wide:], (1, 1))
        out_ref[:, at] = (moe + carried).astype(bf16)
        own[here, at] = dot(grad_ref[here], w_ref[at, :gu_wide], (1, 1)).astype(bf16)

    halves = E // 8

    def experts_step(i):
        loop(i * 2, i * 2 + 2, two_pairs)
        line.step(block * per + i)

    loop(0, halves, experts_step)
    dots_all[me, block] = dots[...].T[:E]
    for o in range(1, n):
        dots_copy(o, block).start()
    tiles = width // tile

    def outward_step(i):
        outward(i)

        @pl.when(i != 1)
        def _():
            line.step(block * per + halves + jnp.minimum(i, 1))

    loop(0, tiles, outward_step)
    loop(block * per, block * per + per, line.offer)

    @pl.when(block == steps - 1)
    def _():
        tall = x_turned.shape[0]
        count = width // tall
        wide = 4 * pair

        def grads_copy(m):
            rows = aligned(m * tall, tall)
            return pltpu.make_async_copy(w_ref.at[rows], grads_hbm.at[rows], grads_sem.at[m])

        def gradients(m):
            at = aligned(m * tall, tall)
            x_turned[...] = x_ref[:, at].T
            dy_turned[...] = dy_ref[:, at].T
            for i in range(gu_wide // wide):
                to = slice(i * wide, (i + 1) * wide)
                w_ref[at, to] = dot(x_turned[...], grad_ref[:, to]).astype(bf16)
            for i in range(gu_wide // wide // 2):
                to = slice(i * wide, (i + 1) * wide)
                w_ref[at, gu_wide + i * wide : gu_wide + (i + 1) * wide] = dot(
                    dy_turned[...], hidden_ref[:, to]
                ).astype(bf16)
            grads_copy(m).start()
            line.step(steps * per + m)

        loop(0, count, gradients)
        line.rest(steps * per + count)
        for c in range(line.chunks - 2, line.chunks):
            dstate_copy(c).wait()

        def dots_sent(b):
            for o in range(1, n):
                dots_copy(o, b).wait_send()

        loop(0, steps, dots_sent)
        loop(0, count, lambda m: grads_copy(m).wait())


def rear_kernel(
    n,
    nf,
    nc,
    moe_hbm,
    low_hbm,
    x_hbm,
    normed_two_hbm,
    wout_ref,
    wqkv_ref,
    query_ref,
    kv_ref,
    mixed_ref,
    dlogits_ref,
    gains_ref,
    dgain_two_ref,
    cos_ref,
    sin_ref,
    act_hbm,
    input_hbm,
    dgains_ref,
    grads_ref,
    moe_ref,
    low_ref,
    x_ref,
    normed_two_ref,
    dmixed,
    dquery,
    dkv,
    dkv_in,
    dqkv_ref,
    own,
    scales,
    dgain,
    gains_in,
    grads,
    grads_in,
    load_sem,
    store_sem,
    send_kv,
    recv_kv,
    send_gain,
    recv_gain,
    send_grad,
    recv_grad,
    *scratch,
):
    me = lax.axis_index("tp")
    flat = lax.axis_index("fsdp") * nc + lax.axis_index("ctx")
    places = Places(nc)
    quarter = places.quarter
    seqs = kv_ref.shape[0]
    q_wide, k_wide = query_ref.shape[1], kv_ref.shape[2] // 2
    group = q_wide // k_wide
    kv_heads = k_wide // HEAD_SIZE
    factor = 1.0 / math.sqrt(HEAD_SIZE)
    peers, padded = grads.shape[:2]
    shard = grads_ref.shape[0]
    loads = [
        pltpu.make_async_copy(source, target, load_sem.at[i])
        for i, (source, target) in enumerate(
            (
                (moe_hbm, moe_ref),
                (low_hbm, low_ref),
                (x_hbm, x_ref),
                (normed_two_hbm, normed_two_ref),
            )
        )
    ]
    for load in loads:
        load.start()

    def peer(o):
        other = lax.rem(flat + o, peers)
        return {"fsdp": other // nc, "ctx": lax.rem(other, nc)}

    def grad_copy(o):
        return pltpu.make_async_remote_copy(
            src_ref=grads.at[lax.rem(flat + o, peers)],
            dst_ref=grads_in.at[o],
            send_sem=send_grad.at[o],
            recv_sem=recv_grad.at[o],
            device_id=peer(o),
            device_id_type=MESH,
        )

    def gain_copy(o):
        return pltpu.make_async_remote_copy(
            src_ref=gains_in.at[0],
            dst_ref=gains_in.at[o],
            send_sem=send_gain.at[o],
            recv_sem=recv_gain.at[o],
            device_id=peer(o),
            device_id_type=MESH,
        )

    def kv_copy(s, part, o, rank):
        return pltpu.make_async_remote_copy(
            src_ref=dkv.at[s, places.rows(rank, part)],
            dst_ref=dkv_in.at[o - 1, s, part],
            send_sem=send_kv.at[o - 1, s, part],
            recv_sem=recv_kv.at[o - 1, s, part],
            device_id={"ctx": places.after(o)},
            device_id_type=MESH,
        )

    def finish_out(c, rows, total):
        moe_ref[rows] = total.astype(bf16)

    def finish_in(c, rows, total):
        x = x_ref[rows].astype(f32)
        scale = lax.rsqrt(jnp.mean(x * x, -1, keepdims=True) + epsilon)
        unit = x * scale
        scaled = total * gains_ref[:1]
        inner = jnp.mean(scaled * unit, -1, keepdims=True)
        own[rows] = (low_ref[rows].astype(f32) + scale * (scaled - unit * inner)).astype(bf16)
        dgain[...] += folded(total * unit)

    outward = Line(n, me, moe_ref, finish_out, scratch[:7], lag=1, hop=2)
    inward = Line(n, me, own, finish_in, scratch[7:], hop=2)
    dgain[...] = jnp.zeros_like(dgain)
    greet(me, n, [peer(o) for o in range(1, peers)])
    loads[0].wait()
    loop(0, outward.chunks, outward.offer)
    loads[1].wait()

    def turned_back(y, part):
        wide = y.shape[1]
        here = pl.ds(part * quarter, quarter)
        return y * widened(cos_ref[here], wide) - swapped_halves(y) * widened(sin_ref[here], wide)

    def attend(s):
        for part in (1, 0):
            rows = places.own(s, part)
            keys = places.keys(part)
            dmixed[...] = dot(low_ref[rows], wout_ref[...]).astype(bf16)
            start = places.slot(places.c, part) * quarter
            allowed = lax.broadcasted_iota(jnp.int32, (keys, quarter), 0) <= (
                start + lax.broadcasted_iota(jnp.int32, (keys, quarter), 1)
            )
            for k in range(kv_heads):
                at = k * HEAD_SIZE
                key = kv_ref[s, :keys, at : at + HEAD_SIZE]
                value = kv_ref[s, :keys, k_wide + at : k_wide + at + HEAD_SIZE]
                dkey = dvalue = None
                for h in range(k * group, (k + 1) * group):
                    head = slice(h * HEAD_SIZE, (h + 1) * HEAD_SIZE)
                    query = query_ref[rows, head]
                    dout = dmixed[:, head]
                    scores = jnp.where(allowed, dot(key, query, (1, 1)), -1e30)
                    raised = jnp.exp(scores - jnp.max(scores, 0, keepdims=True))
                    probs = raised * (1.0 / jnp.sum(raised, 0, keepdims=True))
                    product = probs * dot(value, dout, (1, 1))
                    dscores = product - probs * jnp.sum(product, 0, keepdims=True)
                    dscores = dscores.astype(bf16)
                    dquery[:, head] = dot(dscores, key, (0, 0)) * factor
                    dk, dv = dot(dscores, query), dot(probs.astype(bf16), dout)
                    dkey = dk if dkey is None else dkey + dk
                    dvalue = dv if dvalue is None else dvalue + dv
                for first, add in ((at, dkey), (k_wide + at, dvalue)):
                    lanes = slice(first, first + HEAD_SIZE)
                    if part == 1:
                        dkv[s, :keys, lanes] = add
                    else:
                        dkv[s, :keys, lanes] += add
                outward.step((2 * s + 1 - part) * kv_heads + k)
            dqkv_ref[rows, :q_wide] = turned_back(dquery[...], part).astype(bf16)
        for part in range(2):
            for o in range(1, nc):
                kv_copy(s, part, o, places.after(o)).start()

    loop(0, seqs, attend)
    done = 2 * seqs * kv_heads
    loads[2].wait()
    loads[3].wait()
    per = quarter // inward.size

    def turn_back(s):
        for part in range(2):
            rows = places.own(s, part)
            mine = dkv[s, places.rows(places.c, part)]
            for o in range(1, nc):
                kv_copy(s, part, o, places.after(o)).wait()
                mine = mine + dkv_in[o - 1, s, part]
            dqkv_ref[rows, q_wide : q_wide + k_wide] = turned_back(mine[:, :k_wide], part).astype(
                bf16
            )
            dqkv_ref[rows, q_wide + k_wide :] = mine[:, k_wide:].astype(bf16)
            own[rows] = dot(dqkv_ref[rows], wqkv_ref[...], (1, 1)).astype(bf16)
            first = (2 * s + part) * per
            loop(first, first + per, inward.offer)
            outward.step(done + 2 * s + part)
            x = x_ref[rows].astype(f32)
            scale = lax.rsqrt(jnp.mean(x * x, -1, keepdims=True) + epsilon)
            scales[rows] = jnp.broadcast_to(scale, (quarter, LANES))

    loop(0, seqs, turn_back)
    wide, mid = dqkv_ref.shape[1], dqkv_ref.shape[1] + mixed_ref.shape[1]
    span = max(LANES, shard * LANES // math.gcd(shard, LANES))
    count = span // shard

    def weights(i):
        at = aligned(i * span, span)
        to = pl.ds(i * count, count)

        def put(lanes, value):
            value = value.reshape(count, shard, value.shape[1])
            if padded > shard:
                more = jnp.zeros((count, padded - shard, value.shape[2]), f32)
                value = jnp.concatenate([value, more], 1)
            grads[to, :, lanes] = value.astype(bf16)

        normed = x_ref[:, at].astype(f32) * widened(scales[...], span) * gains_ref[:1, at]
        put(slice(0, wide), dot(normed.astype(bf16), dqkv_ref[...], (0, 0)))
        put(slice(wide, mid), dot(low_ref[:, at], mixed_ref[...], (0, 0)))
        put(slice(mid, grads.shape[2]), dot(normed_two_ref[:, at], dlogits_ref[...], (0, 0)))
        outward.step(done + 2 * seqs + i)

    spans = x_ref.shape[1] // span
    loop(0, spans, weights)
    loop(1, peers, lambda o: grad_copy(o).start())
    outward.rest(done + 2 * seqs + spans)
    stores = [
        pltpu.make_async_copy(source, target, store_sem.at[i])
        for i, (source, target) in enumerate(((moe_ref, act_hbm), (own, input_hbm)))
    ]
    stores[0].start()
    inward.rest(0)
    stores[1].start()
    one = jnp.sum(dgain[...], 0, keepdims=True)
    two = jnp.sum(dgain_two_ref[...], 0, keepdims=True)
    gains_in[0] = jnp.concatenate([one, two], 1)
    loop(1, peers, lambda o: gain_copy(o).start())
    grads_ref[...] = grads[flat].astype(f32)[:shard]

    def add_grad(o):
        grad_copy(o).wait()
        grads_ref[...] += grads_in[o].astype(f32)[:shard]

    loop(1, peers, add_grad)
    loop(1, peers, lambda o: gain_copy(o).wait())
    dgains_ref[...] = gains_in[0]

    def add(o):
        dgains_ref[...] += gains_in[o]

    loop(1, peers, add)
    for store in stores:
        store.wait()


def split_kernel(
    ffn,
    grads_ref,
    small_ref,
    out_hbm,
    input_hbm,
    gate_ref,
    up_ref,
    down_ref,
    query_ref,
    key_ref,
    value_ref,
    out_ref,
    router_ref,
    act_hbm,
    grad_hbm,
    act,
    grad,
    load,
    store,
):
    loads = [
        pltpu.make_async_copy(input_hbm, grad, load.at[0]),
        pltpu.make_async_copy(out_hbm, act, load.at[1]),
    ]
    stores = [
        pltpu.make_async_copy(grad, grad_hbm, store.at[0]),
        pltpu.make_async_copy(act, act_hbm, store.at[1]),
    ]
    for copy in loads:
        copy.start()
    gu_wide = 2 * E * ffn
    at = 0
    for ref in (query_ref, key_ref, value_ref, out_ref, router_ref):
        ref[...] = small_ref[:, at : at + ref.shape[1]]
        at += ref.shape[1]
    loads[0].wait()
    stores[0].start()
    loads[1].wait()
    stores[1].start()
    for e in range(E):
        at = (e // 2) * 4 * ffn + (e % 2) * ffn
        gate_ref[e] = grads_ref[:, at : at + ffn].astype(f32)
        up_ref[e] = grads_ref[:, at + 2 * ffn : at + 3 * ffn].astype(f32)
        at = gu_wide + e * ffn
        down_ref[e] = grads_ref[:, at : at + ffn].astype(f32)
    for copy in stores:
        copy.wait()


def call(kernel, outs, scratch, collective_id, operands, flops=0):
    total = sum(math.prod(o.shape) * o.dtype.itemsize for o in [*outs, *operands])
    return pl.pallas_call(
        kernel,
        out_shape=tuple(outs),
        in_specs=[WHOLE] * len(operands),
        out_specs=tuple([WHOLE] * len(outs)),
        scratch_shapes=scratch,
        compiler_params=pltpu.CompilerParams(
            collective_id=collective_id, has_side_effects=True, vmem_limit_bytes=VMEM_BYTES
        ),
        cost_estimate=pl.CostEstimate(flops=flops, bytes_accessed=total, transcendentals=0),
    )(*operands)


def per_device(
    tokens,
    routes,
    gain_attn,
    w_query,
    key_matrix,
    value_matrix,
    w_out,
    gain_moe,
    w_router,
    w_gate,
    w_up,
    w_down,
    cotangent,
):
    shaped = jax.ShapeDtypeStruct
    rows, width = tokens.shape
    nc, n = lax.axis_size("ctx"), lax.axis_size("tp")
    half = SEQUENCE_LENGTH // nc
    seqs = rows // half
    both = ("fsdp", "ctx")
    cos, sin = angle_tables(placed(lax.axis_index("ctx"), half))
    q_wide, k_wide, o_wide = w_query.shape[1], key_matrix.shape[1], w_out.shape[0]
    qkv_wide = q_wide + 2 * k_wide
    ffn = w_gate.shape[2]
    shard = w_gate.shape[1]

    gu_wide, down_wide = 2 * E * ffn, E * ffn
    small_wide = qkv_wide + o_wide + LANES
    nf = lax.axis_size("fsdp")
    peers = nf * nc
    link = bf16 if shard % 16 == 0 else f32
    def sems(*dims):
        return pltpu.SemaphoreType.DMA(dims)

    wqkv, wout, router, gains, packed = call(
        functools.partial(gather_kernel, nf, nc, ffn),
        [
            shaped((width, qkv_wide), bf16),
            shaped((width, o_wide), bf16),
            shaped((width, LANES), bf16),
            shaped((8, width), f32),
            shaped((shard, gu_wide + down_wide), bf16),
        ],
        [
            pltpu.VMEM((peers, shard, small_wide), link),
            sems(nf),
            sems(nf),
            sems(nc - 1, nf),
            sems(nc - 1, nf),
        ],
        4,
        (
            w_query,
            key_matrix,
            value_matrix,
            w_out.T,
            w_router.T,
            gain_attn[None],
            gain_moe[None],
            w_gate,
            w_up,
            jnp.swapaxes(w_down, 1, 2),
        ),
    )
    experts = lax.all_gather(packed, both, axis=0, tiled=True)
    kv_sems = sems(nc - 1, seqs, 2)
    query, kv, mixed, state, normed_two, gates = call(
        functools.partial(front_kernel, n, nc),
        [
            shaped((rows, q_wide), bf16),
            shaped((seqs, SEQUENCE_LENGTH, 2 * k_wide), bf16),
            shaped((rows, q_wide), bf16),
            shaped((rows, width), bf16),
            shaped((rows, width), bf16),
            shaped((rows, LANES), f32),
        ],
        [
            pltpu.VMEM((seqs, SEQUENCE_LENGTH, 2 * k_wide), bf16),
            pltpu.VMEM((rows, width), bf16),
            kv_sems,
            kv_sems,
            *line_scratch(rows, width, 32),
        ],
        0,
        (tokens, wqkv, wout, router, gains, routes, cos, sin),
    )

    block = 256

    def by_rows(wide):
        return pl.BlockSpec((block, wide), lambda i: (i, 0))

    def constant(*dims):
        return pl.BlockSpec(
            dims, lambda i: (0,) * len(dims), pipeline_mode=pl.Buffered(1)
        )

    anywhere = pl.BlockSpec(memory_space=pl.ANY)
    blocks = rows // block
    size, tall = 64, 256
    dots_sems = pltpu.SemaphoreType.DMA((n - 1, blocks))
    moe_part, grad_experts, low, dlogits, dgain_two = pl.pallas_call(
        functools.partial(expert_kernel, n),
        grid=(blocks,),
        out_shape=(
            shaped((rows, width), bf16),
            shaped((width, gu_wide + down_wide), bf16),
            shaped((rows, width), bf16),
            shaped((rows, LANES), bf16),
            shaped((8, width), f32),
        ),
        in_specs=[
            constant(rows, width),
            constant(rows, width),
            constant(rows, LANES),
            anywhere,
            constant(rows, width),
            constant(width, LANES),
            constant(8, width),
        ],
        out_specs=(
            by_rows(width),
            anywhere,
            anywhere,
            pl.BlockSpec((rows, LANES), lambda i: (0, 0)),
            pl.BlockSpec((8, width), lambda i: (0, 0)),
        ),
        scratch_shapes=[
            pltpu.VMEM((rows, width), bf16),
            pltpu.VMEM((rows, down_wide), bf16),
            pltpu.VMEM((rows, gu_wide), bf16),
            pltpu.VMEM((tall, rows), bf16),
            pltpu.VMEM((tall, rows), bf16),
            pltpu.VMEM((block, LANES), f32),
            pltpu.VMEM((n, blocks, E, block), f32),
            pltpu.VMEM((rows, LANES), f32),
            pltpu.VMEM((width, gu_wide + down_wide), bf16),
            pltpu.VMEM((2, size, width), bf16),
            sems(2, E // 4),
            sems(width // tall),
            sems(2),
            dots_sems,
            dots_sems,
            *line_scratch(rows, width, size),
        ],
        compiler_params=pltpu.CompilerParams(
            collective_id=1, has_side_effects=True, vmem_limit_bytes=VMEM_BYTES
        ),
        cost_estimate=pl.CostEstimate(
            flops=18 * rows * width * down_wide,
            bytes_accessed=2 * width * (gu_wide + down_wide),
            transcendentals=0,
        ),
    )(normed_two, cotangent, gates, experts, state, router, gains)

    low, grad_experts = lax.optimization_barrier((low, grad_experts))
    grad_experts = lax.psum_scatter(grad_experts, both, scatter_dimension=0, tiled=True)

    small_block = pltpu.VMEM((peers, -(-shard // 16) * 16, small_wide), bf16)
    whole = pltpu.VMEM((rows, width), bf16)
    operands = (
        (moe_part, low, tokens, normed_two)
        + (wout, wqkv, query, kv, mixed, dlogits, gains, dgain_two, cos, sin)
    )
    activations, input_grad, dgains, grad_small = pl.pallas_call(
        functools.partial(rear_kernel, n, nf, nc),
        out_shape=(
            shaped((rows, width), bf16),
            shaped((rows, width), bf16),
            shaped((1, 2 * width), f32),
            shaped((shard, small_wide), f32),
        ),
        in_specs=[anywhere] * 4 + [WHOLE] * (len(operands) - 4),
        out_specs=(anywhere, anywhere, WHOLE, WHOLE),
        scratch_shapes=[
            whole,
            whole,
            whole,
            whole,
            pltpu.VMEM((half // 2, q_wide), bf16),
            pltpu.VMEM((half // 2, q_wide), f32),
            pltpu.VMEM((seqs, SEQUENCE_LENGTH, 2 * k_wide), f32),
            pltpu.VMEM((nc - 1, seqs, 2, half // 2, 2 * k_wide), f32),
            pltpu.VMEM((rows, qkv_wide), bf16),
            whole,
            pltpu.VMEM((rows, LANES), f32),
            pltpu.VMEM((8, width), f32),
            pltpu.VMEM((peers, 1, 2 * width), f32),
            small_block,
            small_block,
            sems(4),
            sems(2),
            kv_sems,
            kv_sems,
            *[sems(peers)] * 4,
            *line_scratch(rows, width, size),
            *line_scratch(rows, width, 32),
        ],
        compiler_params=pltpu.CompilerParams(
            collective_id=3, has_side_effects=True, vmem_limit_bytes=VMEM_BYTES
        ),
        cost_estimate=pl.CostEstimate(
            flops=12 * rows * width * small_wide,
            bytes_accessed=16 * rows * width,
            transcendentals=0,
        ),
    )(*operands)
    flat = lax.axis_index("fsdp") * nc + lax.axis_index("ctx")
    dgains = lax.dynamic_slice_in_dim(dgains.reshape(2, width), flat * shard, shard, 1)
    results = pl.pallas_call(
        functools.partial(split_kernel, ffn),
        out_shape=(
            shaped((E, shard, ffn), f32),
            shaped((E, shard, ffn), f32),
            shaped((E, shard, ffn), f32),
            shaped((shard, q_wide), f32),
            shaped((shard, k_wide), f32),
            shaped((shard, k_wide), f32),
            shaped((shard, o_wide), f32),
            shaped((shard, E), f32),
            shaped((rows, width), bf16),
            shaped((rows, width), bf16),
        ),
        in_specs=[WHOLE, WHOLE, anywhere, anywhere],
        out_specs=(*[WHOLE] * 8, anywhere, anywhere),
        scratch_shapes=[
            pltpu.VMEM((rows, width), bf16),
            pltpu.VMEM((rows, width), bf16),
            sems(2),
            sems(2),
        ],
        compiler_params=pltpu.CompilerParams(vmem_limit_bytes=VMEM_BYTES),
    )(grad_experts, grad_small, activations, input_grad)
    grad_gate, grad_up, grad_down, grad_query, grad_key, grad_value, grad_out, grad_router = results[:8]
    return (
        results[8],
        results[9],
        dgains[0],
        grad_query,
        grad_key,
        grad_value,
        grad_out.T,
        dgains[1],
        grad_router,
        grad_gate,
        grad_up,
        jnp.swapaxes(grad_down, 1, 2),
    )


def solution(mesh):
    specs = (
        P(("fsdp", "ctx"), None),
        P(("fsdp", "ctx"), None),
        P(("fsdp", "ctx")),
        P(("fsdp", "ctx"), "tp"),
        P(("fsdp", "ctx"), "tp"),
        P(("fsdp", "ctx"), "tp"),
        P("tp", ("fsdp", "ctx")),
        P(("fsdp", "ctx")),
        P(("fsdp", "ctx"), None),
        P(None, ("fsdp", "ctx"), "tp"),
        P(None, ("fsdp", "ctx"), "tp"),
        P(None, "tp", ("fsdp", "ctx")),
        P(("fsdp", "ctx"), None),
    )
    return jax.shard_map(
        per_device,
        mesh=mesh,
        in_specs=specs,
        out_specs=(
            P(("fsdp", "ctx"), None),
            P(("fsdp", "ctx"), None),
            P(("fsdp", "ctx")),
            P(("fsdp", "ctx"), "tp"),
            P(("fsdp", "ctx"), "tp"),
            P(("fsdp", "ctx"), "tp"),
            P("tp", ("fsdp", "ctx")),
            P(("fsdp", "ctx")),
            P(("fsdp", "ctx"), None),
            P(None, ("fsdp", "ctx"), "tp"),
            P(None, ("fsdp", "ctx"), "tp"),
            P(None, "tp", ("fsdp", "ctx")),
        ),
        check_vma=False,
    )
```

time: 522 us -> 456 us (0.87)
  local copies, waits for them, and re-layouts: 42 us -> 7.9 us
  other arithmetic: 16.5 us -> 1.71 us
  waiting for transfers between devices: 12.6 us -> 0.06 us
  Pallas kernels: 430 us -> 423 us
    pallas_call x3 -> x2, Pallas kernels: 272 us -> 140 us  [call(): pl.pallas_call(kernel, out_shape=tuple(outs), in_specs=[WHOLE] * len(oper...]
    pallas_call x1, Pallas kernels: 42.5 us -> 167 us  [per_device(): pl.pallas_call(functools.partial(rear_kernel, n, nf, nc), out_shape=(shap...]
    all_gather x2 -> x1, waiting for transfers between devices: 12.6 us -> 0.02 us  [per_device(): experts = lax.all_gather(packed, both, axis=0, tiled=True)]
    unnamed x17 -> x4, local copies, waits for them, and re-layouts: 13.2 us -> 2.57 us
    slice x6 -> x0, local copies, waits for them, and re-layouts: 10.3 us -> none  [the longest x1 3.01 us: per_device(): wqkv = small_full[:, :qkv_wide]]
    concatenate x2 -> x0, other arithmetic: 6.19 us -> none  [the longest x1 3.14 us: per_device(): activations = jnp.concatenate([act_early, act_late], 0)]
    reduce_or x1 -> x0, other arithmetic: 5.79 us -> none  [per_device(): jnp.any(routes[:, :, None] == jnp.arange(LANES, dtype=jnp.int32)[None, No...]
  transfers between devices with their start and end apart: 3 -> 2, of which waited for: 1 -> 0; matrix products, arithmetic and copies ran while one was open for 9% -> 1% of each run, Pallas kernels for 53% -> 62%
where the time goes in v4:
time: 456 us; the launch traced here: 448 us
  Pallas kernels  423 us (93%)
  between operations  14.6 us (3%)
  local copies, waits for them, and re-layouts  7.9 us (2%)
    pallas_call x1, Pallas kernels, per_device(): pl.pallas_call(functools.partial(rear_kernel, n, nf, nc), out_shape=(shap...  167 us
    pallas_call x2, Pallas kernels, call(): pl.pallas_call(kernel, out_shape=tuple(outs), in_specs=[WHOLE] * len(oper...  140 us
    pallas_call x1, Pallas kernels, per_device(): pl.pallas_call(functools.partial(expert_kernel, n), grid=(blocks,), out_s...  108 us
  transfers between devices with their start and end apart: 2, of which 0 were waited for; matrix products, arithmetic and copies ran while one was open for 1% of the time, Pallas kernels for 62%

profile of v4, /device:TPU:0, one launch (start us, length us, event | category | flops | bytes accessed | tf_op | source)
XLA Modules:
  0.0 447.7 jit_solution(9801223307809722693)
XLA Ops:
  7.2 0.0 all-gather.2.cloned.1.call-start
  7.2 1.2 broadcast_in_dim.8.gain_one_ref
  8.4 1.2 broadcast_in_dim.9.gain_two_ref
  9.7 0.0 copy-start
  9.7 30.3 %shard_map.220 = (bf16[1536,640]{1,0:T(8,128)(2,1)}, bf16[1536,384]{1,0:T(8,128)(2,1)}, bf16[1536,128]{1,0:T(8,128)(2,1)}, f32[8,1536]{1,0:T(8,128)}, bf16[192,6144]{1,0:T(8,128)(2,1)}) custom-call(bf16[192,384]{1,0:T(8,128)(2,1)} %query_ref.1, bf16[192,128]{1,0:T(8,128)(2,1)} %key_ref.1, bf16[192,128]{1,0:T(8,128)(2,1)} %value_ref.1, ...), custom_call_target="tpu_custom_call" | custom-call | bytes 8706816 | tf_op jit(solution)/shard_map/pallas_call | solution.py:1016
  40.0 0.0 all-gather.2.cloned.1.call-update
  40.0 0.0 reduce-scatter.2.cloned.1.call-start
  40.1 0.3 multiply_sine_fusion
  40.5 0.8 copy.28.cos_ref
  41.3 0.8 copy.29.sin_ref
  42.2 0.0 copy-done
  42.2 1.0 copy.27.routes_ref
  43.2 109.7 %shard_map.221 = (bf16[1024,384]{1,0:T(8,128)(2,1)}, bf16[2,1024,256]{2,1,0:T(8,128)(2,1)}, bf16[1024,384]{1,0:T(8,128)(2,1)}, bf16[1024,1536]{1,0:T(8,128)(2,1)...) custom-call(bf16[1024,1536]{1,0:T(8,128)(2,1)} %x_hbm.1, bf16[1536,640]{1,0:T(8,128)(2,1)} %get-tuple-element.44.wqkv_ref, ...), custom_call_target="tpu_custom_call" | custom-call | bytes 16728064 | tf_op jit(solution)/shard_map/pallas_call | solution.py:1016
  152.8 0.0 all-gather.2.cloned.1.call-done.w_hbm
  152.9 107.8 %shard_map.222 = (bf16[1024,1536]{1,0:T(8,128)(2,1)}, bf16[1536,6144]{1,0:T(8,128)(2,1)}, bf16[1024,1536]{1,0:T(8,128)(2,1)}, bf16[1024,128]{1,0:T(8,128)(2,1)}, f32[8,1536]{1,0:T(8,128)}) custom-call(bf16[1024,1536]{1,0:T(8,128)(2,1)} %get-tuple-element.48.x_ref.normed_two_hbm, bf16[1024,1536]{1,0:T(8,128)(2,1)} %dy_ref.1, ...), custom_call_target="tpu_custom_call" | custom-call | flops 57982058496 | bytes 18874368 | tf_op jit(solution)/shard_map/pallas_call | solution.py:1131
  260.7 0.0 reduce-scatter.2.cloned.1.call-update
  260.7 166.7 %shard_map.223 = (bf16[1024,1536]{1,0:T(8,128)(2,1)}, bf16[1024,1536]{1,0:T(8,128)(2,1)}, f32[1,3072]{1,0:T(1,128)}, f32[192,1152]{1,0:T(8,128)}) custom-call(bf16[1024,1536]{1,0:T(8,128)(2,1)} %get-tuple-element.55.moe_hbm, bf16[1024,1536]{1,0:T(8,128)(2,1)} %get-tuple-element.56.low_hbm, bf16[1024,1536]{1,0:T(8,128)(2,1)} %x_hbm.1, ...), custom_call_target="tpu_custom_call" | custom-call | flops 21743271936 | bytes 25165824 | tf_op jit(solution)/shard_map/pallas_call | solution.py:1194
  427.4 0.5 broadcast.75
  427.9 1.4 reduce.3
  429.3 0.6 fusion
  429.9 0.0 reduce-scatter.2.cloned.1.call-done.grads_ref
  429.9 8.9 %shard_map.224 = (f32[16,192,128]{2,1,0:T(8,128)}, f32[16,192,128]{2,1,0:T(8,128)}, f32[16,192,128]{2,1,0:T(8,128)}, f32[192,384]{1,0:T(8,128)}, f32[192,128]{1,...) custom-call(bf16[192,6144]{1,0:T(8,128)(2,1)} %reduce-scatter.2.clon, ...), custom_call_target="tpu_custom_call" | custom-call | tf_op jit(solution)/shard_map/pallas_call | solution.py:1239
  438.9 1.6 copy.32
  (5 shorter events, 0.1 us)
Async XLA Ops:
  7.2 145.7 %all-gather.2.cloned.1.call-start = ((), (), s32[]{:S(2)}) async-start(), calls=%async_computation.1 | async-start | bytes 21233664 | tf_op jit(solution)/shard_map/all_gather | solution.py:1094
  9.7 32.5 %copy-start = (s32[1024,8]{0,1:T(8,128)S(1)}, s32[1024,8]{0,1:T(8,128)}, u32[]{:S(2)}) copy-start(s32[1024,8]{0,1:T(8,128)} %param.14) | copy-start | bytes 98308
  40.0 389.9 %reduce-scatter.2.cloned.1.call-start = ((), (), s32[]{:S(2)}) async-start(), calls=%async_computation.2 | async-start | bytes 21233664 | tf_op jit(solution)/shard_map/reduce_scatter | solution.py:1186
Sparse Core Ops, SparseCore 0:
  40.2 99.6 all-gather.1
  260.8 161.9 reduce-scatter.1

commit v5 on v4

--- a/solution.py
+++ b/solution.py
@@ -32,12 +32,10 @@
 
 def angle_tables(token_places):
     halfway = HEAD_SIZE // 2
-    freqs = jnp.exp(
-        jnp.arange(halfway, dtype=f32) * (-2.0 * math.log(10000.0) / HEAD_SIZE)
-    )
+    lanes = jnp.arange(LANES, dtype=jnp.int32) % halfway
+    freqs = jnp.exp(lanes.astype(f32) * (-2.0 * math.log(10000.0) / HEAD_SIZE))
     angles = token_places.astype(f32)[:, None] * freqs[None, :]
-    copies = LANES // halfway
-    return jnp.tile(jnp.cos(angles), (1, copies)), jnp.tile(jnp.sin(angles), (1, copies))
+    return jnp.cos(angles), jnp.sin(angles)
 
 
 def aligned(start, size):
@@ -90,19 +88,19 @@
 
 
 class Line:
-    def __init__(self, n, me, own, finish, scratch, base=0, lag=0, hop=1):
+    def __init__(self, n, me, own, finish, scratch, lag=0, hop=1, late=0):
         self.n, self.me, self.own, self.finish = n, me, own, finish
         self.arrived, self.to_right, self.to_left = scratch[:3]
         self.send_right, self.recv_left, self.send_left, self.recv_right = scratch[3:]
         self.size = self.to_right.shape[0] // SLOTS
         self.total = self.arrived.shape[0] // 2
         self.chunks = self.total // self.size
-        self.base, self.lag, self.hop = base, lag, hop
-        self.steps = self.chunks + lag + hop * (n - 2)
+        self.lag, self.hop, self.late = lag, hop, late
+        self.steps = self.chunks + lag + hop * (n - 2) + late
         self.middle = (me > 0) & (me < n - 1)
 
     def rows(self, c):
-        return aligned(self.base + c * self.size, self.size)
+        return aligned(c * self.size, self.size)
 
     def left_rows(self, c):
         return aligned(c * self.size, self.size)
@@ -145,7 +143,7 @@
     def step(self, t):
         n, me, chunks = self.n, self.me, self.chunks
         go, come = t - self.lag - self.hop * (me - 1), t - self.lag - self.hop * (n - 2 - me)
-        done = jnp.minimum(go, come)
+        done = jnp.minimum(go, come) - jnp.where(self.middle, 0, self.late)
         nearer_left = me < n - 1 - me
 
         def inside(c):
@@ -265,12 +263,9 @@
     gate_ref,
     up_ref,
     down_ref,
-    wqkv_ref,
-    wout_ref,
-    router_all_ref,
+    small_all,
     gains_ref,
     experts_ref,
-    small_all,
     send_f,
     recv_f,
     send_c,
@@ -293,7 +288,7 @@
     barrier = pltpu.get_barrier_semaphore()
     for other in [to_peer(o) for o in range(1, nf)] + [to_near(p) for p in range(1, nc)]:
         pl.semaphore_signal(barrier, inc=1, device_id=other, device_id_type=MESH)
-    gains = [gain_one_ref[...].astype(f32), gain_two_ref[...].astype(f32)]
+    gains = [g[...].astype(f32).reshape(1, shard) for g in (gain_one_ref, gain_two_ref)]
     blank = jnp.zeros((LANES - E - 2, shard), f32)
     last = jnp.concatenate([router_ref[...].astype(f32), *gains, blank], 0).T
     at = 0
@@ -348,12 +343,8 @@
             near_copy(p, o, lax.rem(c + nc - p, nc)).wait_recv()
 
     loop(0, nf, shared)
-    at = 0
-    for ref in (wqkv_ref, wout_ref, router_all_ref):
-        rows, wide = ref.shape
-        ref[...] = small_all[:, :, at : at + wide].reshape(rows, wide).astype(bf16)
-        at += wide
-    gains_ref[...] = router_all_ref[...].astype(f32).T[E : E + 8]
+    last = small_all[:, :, small_all.shape[2] - LANES :]
+    gains_ref[...] = last.reshape(nf * nc * shard, LANES).astype(f32).T[E : E + 8]
     loop(1, nf, lambda o: far_copy(o, f).wait_send())
 
     def near_sent(o):
@@ -367,9 +358,7 @@
     n,
     nc,
     x_ref,
-    wqkv_ref,
-    wout_ref,
-    router_ref,
+    small_ref,
     gains_ref,
     routes_ref,
     cos_ref,
@@ -377,11 +366,14 @@
     query_ref,
     kv_ref,
     mixed_ref,
-    state_ref,
-    normed_ref,
+    state_hbm,
+    normed_hbm,
     gates_ref,
     kv_all,
     own,
+    state_ref,
+    normed_ref,
+    store_sem,
     send_kv,
     recv_kv,
     *scratch,
@@ -392,6 +384,16 @@
     seqs = kv_ref.shape[0]
     q_wide, k_wide = query_ref.shape[1], kv_ref.shape[2] // 2
     group = q_wide // k_wide
+    qkv_wide = q_wide + 2 * k_wide
+    wide = small_ref.shape[1] - LANES
+
+    def row_stores(c):
+        rows = line.rows(c)
+        pairs = ((state_ref, state_hbm), (normed_ref, normed_hbm))
+        return [
+            pltpu.make_async_copy(source.at[rows], target.at[rows], store_sem.at[i, c])
+            for i, (source, target) in enumerate(pairs)
+        ]
 
     def finish(c, rows, total):
         state = x_ref[rows].astype(f32) + total
@@ -399,18 +401,19 @@
         normed = (state * scale * gains_ref[1:2]).astype(bf16)
         state_ref[rows] = state.astype(bf16)
         normed_ref[rows] = normed
+        for copy in row_stores(c):
+            copy.start()
         routes = routes_ref[rows]
         lane = lax.broadcasted_iota(jnp.int32, (line.size, LANES), 1)
         named = lane == routes[:, :1]
         for k in range(1, TOPK):
             named = named | (lane == routes[:, k : k + 1])
-        logits = jnp.where(named, dot(normed, router_ref[...]), -1e30)
+        logits = jnp.where(named, dot(normed, small_ref[:, wide:]), -1e30)
         top = jnp.max(logits, -1, keepdims=True)
         raised = jnp.where(named, jnp.exp(logits - top), 0.0)
         gates_ref[rows] = raised / jnp.sum(raised, -1, keepdims=True)
 
-    line = Line(n, me, own, finish, scratch, hop=2)
-
+    line = Line(n, me, own, finish, scratch, hop=2, late=quarter // 16)
     greet(me, n, [{"ctx": places.after(o)} for o in range(1, nc)])
 
     def kv_copy(s, part, o, rank):
@@ -430,7 +433,7 @@
             x = x_ref[rows].astype(f32)
             scale = lax.rsqrt(jnp.mean(x * x, -1, keepdims=True) + epsilon)
             normed = (x * scale * gains_ref[:1]).astype(bf16)
-            qkv = dot(normed, wqkv_ref[...])
+            qkv = dot(normed, small_ref[:, :qkv_wide])
             qk = qkv[:, : q_wide + k_wide]
             here = pl.ds(part * quarter, quarter)
             cos, sin = widened(cos_ref[here], q_wide + k_wide), widened(sin_ref[here], q_wide + k_wide)
@@ -464,7 +467,7 @@
                 raised = jnp.exp(scores - jnp.max(scores, -1, keepdims=True))
                 probs = (raised * (1.0 / jnp.sum(raised, -1, keepdims=True))).astype(bf16)
                 mixed_ref[rows, h * HEAD_SIZE : (h + 1) * HEAD_SIZE] = dot(probs, value).astype(bf16)
-            own[rows] = dot(mixed_ref[rows], wout_ref[...], (1, 1)).astype(bf16)
+            own[rows] = dot(mixed_ref[rows], small_ref[:, qkv_wide:wide], (1, 1)).astype(bf16)
             per = quarter // line.size
             first = (2 * s + part) * per
             loop(first, first + per, line.offer)
@@ -474,6 +477,12 @@
     kv_ref[...] = kv_all[...]
     line.rest(line.chunks)
 
+    def stored(c):
+        for copy in row_stores(c):
+            copy.wait()
+
+    loop(0, line.chunks, stored)
+
     def kv_sent(s):
         for part in range(2):
             for o in range(1, nc):
@@ -484,11 +493,11 @@
 
 def expert_kernel(
     n,
-    x_ref,
-    dy_ref,
+    x_hbm,
+    dy_hbm,
     gates_ref,
     w_hbm,
-    state_ref,
+    state_hbm,
     router_ref,
     gains_ref,
     out_ref,
@@ -496,6 +505,9 @@
     dstate_hbm,
     dlogits_ref,
     dgain_ref,
+    x_ref,
+    dy_ref,
+    state_ref,
     own,
     hidden_ref,
     grad_ref,
@@ -505,6 +517,7 @@
     dots_rows,
     w_ref,
     dstate_out,
+    row_sem,
     w_sem,
     grads_sem,
     dstate_sem,
@@ -537,6 +550,19 @@
             pltpu.make_async_copy(w_hbm.at[:, span], w_ref.at[:, span], w_sem.at[i, p])
             for i, span in enumerate(spans)
         ]
+
+    def row_copy(i, b):
+        source, target = ((x_hbm, x_ref), (dy_hbm, dy_ref), (state_hbm, state_ref))[i]
+        rows = aligned(b * size_in, size_in)
+        return pltpu.make_async_copy(source.at[rows], target.at[rows], row_sem.at[i, b])
+
+    def fetch_rows(b):
+        row_copy(0, b).start()
+        row_copy(1, b).start()
+
+    def fetch_pair(i):
+        for copy in w_copies(i):
+            copy.start()
 
     def dstate_copy(c):
         return pltpu.make_async_copy(
@@ -585,6 +611,9 @@
 
     @pl.when(block == 0)
     def _():
+        fetch_rows(0)
+        fetch_pair(0)
+        fetch_pair(1)
         barrier = pltpu.get_barrier_semaphore()
         for o in range(1, n):
             pl.semaphore_signal(
@@ -593,15 +622,12 @@
         pl.semaphore_wait(barrier, n - 1)
         dgain_ref[...] = jnp.zeros_like(dgain_ref)
 
-        def fetch(p):
-            for copy in w_copies(p):
-                copy.start()
-
-        loop(0, E // 4, fetch)
 
     lane = lax.broadcasted_iota(jnp.int32, (size_in, LANES), 1)
     first = lax.broadcasted_iota(jnp.int32, (size_in, pair), 1) < single
     dots[...] = jnp.zeros_like(dots)
+    row_copy(0, block).wait()
+    row_copy(1, block).wait()
 
     def gating(p, gate_pre, up_pre, raw):
         gates = gates_ref[here]
@@ -630,6 +656,15 @@
             for copy in w_copies(i):
                 copy.wait()
 
+            @pl.when(i + 2 < E // 4)
+            def _():
+                fetch_pair(i + 2)
+
+            @pl.when(i == E // 4 - 2)
+            def _():
+                loop(1, steps, fetch_rows)
+                loop(0, steps, lambda b: row_copy(2, b).start())
+
         gu = dot(x_ref[here], w_ref[:, aligned(i * 4 * pair, 4 * pair)])
         raw = dot(dy_ref[here], w_ref[:, aligned(gu_wide + i * 2 * pair, 2 * pair)])
         for j in range(2):
@@ -643,34 +678,35 @@
 
     tile = 512
 
+    def back(i):
+        at = aligned(i * tile, tile)
+        own[here, at] = dot(grad_ref[here], w_ref[at, :gu_wide], (1, 1)).astype(bf16)
+
     def outward(i):
         at = aligned(i * tile, tile)
         carried = jnp.where(me == n // 2, state_ref[here, at].astype(f32), 0.0)
         moe = dot(hidden_ref[here], w_ref[at, gu_wide:], (1, 1))
         out_ref[:, at] = (moe + carried).astype(bf16)
-        own[here, at] = dot(grad_ref[here], w_ref[at, :gu_wide], (1, 1)).astype(bf16)
-
-    halves = E // 8
-
-    def experts_step(i):
-        loop(i * 2, i * 2 + 2, two_pairs)
-        line.step(block * per + i)
-
-    loop(0, halves, experts_step)
+
+    unit = per // 4
+    tiles = width // tile
+
+    def steps_at(i):
+        first = block * per + i * unit
+        loop(first, first + unit, line.step)
+
+    for i in range(2):
+        loop(i * (E // 8), (i + 1) * (E // 8), two_pairs)
+        steps_at(i)
     dots_all[me, block] = dots[...].T[:E]
     for o in range(1, n):
         dots_copy(o, block).start()
-    tiles = width // tile
-
-    def outward_step(i):
-        outward(i)
-
-        @pl.when(i != 1)
-        def _():
-            line.step(block * per + halves + jnp.minimum(i, 1))
-
-    loop(0, tiles, outward_step)
+    loop(0, tiles, back)
     loop(block * per, block * per + per, line.offer)
+    steps_at(2)
+    row_copy(2, block).wait()
+    loop(0, tiles, outward)
+    steps_at(3)
 
     @pl.when(block == steps - 1)
     def _():
@@ -695,10 +731,10 @@
                     dy_turned[...], hidden_ref[:, to]
                 ).astype(bf16)
             grads_copy(m).start()
-            line.step(steps * per + m)
+            loop(steps * per + m * unit, steps * per + (m + 1) * unit, line.step)
 
         loop(0, count, gradients)
-        line.rest(steps * per + count)
+        line.rest(steps * per + count * unit)
         for c in range(line.chunks - 2, line.chunks):
             dstate_copy(c).wait()
 
@@ -716,14 +752,13 @@
     nc,
     moe_hbm,
     low_hbm,
+    small_hbm,
+    query_hbm,
+    kv_hbm,
     x_hbm,
     normed_two_hbm,
-    wout_ref,
-    wqkv_ref,
-    query_ref,
-    kv_ref,
-    mixed_ref,
-    dlogits_ref,
+    mixed_hbm,
+    dlogits_hbm,
     gains_ref,
     dgain_two_ref,
     cos_ref,
@@ -734,8 +769,14 @@
     grads_ref,
     moe_ref,
     low_ref,
+    wout_ref,
+    query_ref,
+    kv_ref,
+    wqkv_ref,
     x_ref,
     normed_two_ref,
+    mixed_ref,
+    dlogits_ref,
     dmixed,
     dquery,
     dkv,
@@ -746,15 +787,19 @@
     dgain,
     gains_in,
     grads,
-    grads_in,
+    grads_near,
+    grads_far,
+    moe_sem,
     load_sem,
     store_sem,
     send_kv,
     recv_kv,
     send_gain,
     recv_gain,
-    send_grad,
-    recv_grad,
+    send_near,
+    recv_near,
+    send_far,
+    recv_far,
     *scratch,
 ):
     me = lax.axis_index("tp")
@@ -764,6 +809,7 @@
     seqs = kv_ref.shape[0]
     q_wide, k_wide = query_ref.shape[1], kv_ref.shape[2] // 2
     group = q_wide // k_wide
+    qkv_wide = q_wide + 2 * k_wide
     kv_heads = k_wide // HEAD_SIZE
     factor = 1.0 / math.sqrt(HEAD_SIZE)
     peers, padded = grads.shape[:2]
@@ -772,27 +818,51 @@
         pltpu.make_async_copy(source, target, load_sem.at[i])
         for i, (source, target) in enumerate(
             (
-                (moe_hbm, moe_ref),
                 (low_hbm, low_ref),
+                (small_hbm.at[:, pl.ds(qkv_wide, wout_ref.shape[1])], wout_ref),
+                (query_hbm, query_ref),
+                (kv_hbm, kv_ref),
+                (small_hbm.at[:, pl.ds(0, qkv_wide)], wqkv_ref),
                 (x_hbm, x_ref),
                 (normed_two_hbm, normed_two_ref),
+                (mixed_hbm, mixed_ref),
+                (dlogits_hbm, dlogits_ref),
             )
         )
     ]
-    for load in loads:
-        load.start()
+    portions = moe_sem.shape[0]
+    portion = moe_ref.shape[0] // portions
+
+    def moe_load(i):
+        rows = aligned(i * portion, portion)
+        return pltpu.make_async_copy(moe_hbm.at[rows], moe_ref.at[rows], moe_sem.at[i])
+
+    loop(0, portions, lambda i: moe_load(i).start())
 
     def peer(o):
         other = lax.rem(flat + o, peers)
         return {"fsdp": other // nc, "ctx": lax.rem(other, nc)}
 
-    def grad_copy(o):
+    f = lax.axis_index("fsdp")
+
+    def near_copy(p, g):
         return pltpu.make_async_remote_copy(
-            src_ref=grads.at[lax.rem(flat + o, peers)],
-            dst_ref=grads_in.at[o],
-            send_sem=send_grad.at[o],
-            recv_sem=recv_grad.at[o],
-            device_id=peer(o),
+            src_ref=grads.at[g * nc + places.after(p)],
+            dst_ref=grads_near.at[p - 1, g],
+            send_sem=send_near.at[p - 1, g],
+            recv_sem=recv_near.at[p - 1, g],
+            device_id={"ctx": places.after(p)},
+            device_id_type=MESH,
+        )
+
+    def far_copy(o):
+        other = lax.rem(f + o, nf)
+        return pltpu.make_async_remote_copy(
+            src_ref=grads.at[other * nc + places.c],
+            dst_ref=grads_far.at[o],
+            send_sem=send_far.at[o],
+            recv_sem=recv_far.at[o],
+            device_id={"fsdp": other},
             device_id_type=MESH,
         )
 
@@ -832,9 +902,22 @@
     inward = Line(n, me, own, finish_in, scratch[7:], hop=2)
     dgain[...] = jnp.zeros_like(dgain)
     greet(me, n, [peer(o) for o in range(1, peers)])
-    loads[0].wait()
-    loop(0, outward.chunks, outward.offer)
-    loads[1].wait()
+
+    def offer(i):
+        per = outward.chunks // portions
+        moe_load(i).wait()
+        loop(i * per, (i + 1) * per, outward.offer)
+
+    heads, early = q_wide // HEAD_SIZE, 4
+    for load in loads[:4]:
+        load.start()
+    loop(0, portions, offer)
+    loop(0, early, outward.step)
+    for load in loads[:4]:
+        load.wait()
+    for load in loads[4:]:
+        load.start()
+
 
     def turned_back(y, part):
         wide = y.shape[1]
@@ -869,22 +952,22 @@
                     dk, dv = dot(dscores, query), dot(probs.astype(bf16), dout)
                     dkey = dk if dkey is None else dkey + dk
                     dvalue = dv if dvalue is None else dvalue + dv
+                    outward.step(early + (2 * s + 1 - part) * heads + h)
                 for first, add in ((at, dkey), (k_wide + at, dvalue)):
                     lanes = slice(first, first + HEAD_SIZE)
                     if part == 1:
                         dkv[s, :keys, lanes] = add
                     else:
                         dkv[s, :keys, lanes] += add
-                outward.step((2 * s + 1 - part) * kv_heads + k)
             dqkv_ref[rows, :q_wide] = turned_back(dquery[...], part).astype(bf16)
         for part in range(2):
             for o in range(1, nc):
                 kv_copy(s, part, o, places.after(o)).start()
 
     loop(0, seqs, attend)
-    done = 2 * seqs * kv_heads
-    loads[2].wait()
-    loads[3].wait()
+    done = early + 2 * seqs * heads
+    for load in loads[4:]:
+        load.wait()
     per = quarter // inward.size
 
     def turn_back(s):
@@ -930,14 +1013,39 @@
 
     spans = x_ref.shape[1] // span
     loop(0, spans, weights)
-    loop(1, peers, lambda o: grad_copy(o).start())
-    outward.rest(done + 2 * seqs + spans)
+    def send_share(g):
+        for p in range(1, nc):
+            near_copy(p, g).start()
+
+    loop(0, nf, send_share)
+    start = done + 2 * seqs + spans
+    ahead = max(outward.steps - start, 0)
+
+    def both(i):
+        outward.step(start + i)
+        inward.step(i)
+
+    loop(0, ahead, both)
+    outward.rest(start + ahead)
+
+    def add_share(g):
+        mine = g * nc + places.c
+        total = grads[mine].astype(f32)
+        for p in range(1, nc):
+            near_copy(p, g).wait()
+            total = total + grads_near[p - 1, g].astype(f32)
+        grads[mine] = total.astype(bf16)
+
     stores = [
         pltpu.make_async_copy(source, target, store_sem.at[i])
         for i, (source, target) in enumerate(((moe_ref, act_hbm), (own, input_hbm)))
     ]
     stores[0].start()
-    inward.rest(0)
+    enough = ahead + inward.chunks // 2
+    loop(ahead, enough, inward.step)
+    loop(0, nf, add_share)
+    loop(1, nf, lambda o: far_copy(o).start())
+    inward.rest(enough)
     stores[1].start()
     one = jnp.sum(dgain[...], 0, keepdims=True)
     two = jnp.sum(dgain_two_ref[...], 0, keepdims=True)
@@ -946,10 +1054,10 @@
     grads_ref[...] = grads[flat].astype(f32)[:shard]
 
     def add_grad(o):
-        grad_copy(o).wait()
-        grads_ref[...] += grads_in[o].astype(f32)[:shard]
-
-    loop(1, peers, add_grad)
+        far_copy(o).wait()
+        grads_ref[...] += grads_far[o].astype(f32)[:shard]
+
+    loop(1, nf, add_grad)
     loop(1, peers, lambda o: gain_copy(o).wait())
     dgains_ref[...] = gains_in[0]
 
@@ -963,8 +1071,10 @@
 
 def split_kernel(
     ffn,
+    nc,
     grads_ref,
     small_ref,
+    dgains_ref,
     out_hbm,
     input_hbm,
     gate_ref,
@@ -975,6 +1085,7 @@
     value_ref,
     out_ref,
     router_ref,
+    gain_ref,
     act_hbm,
     grad_hbm,
     act,
@@ -994,9 +1105,16 @@
         copy.start()
     gu_wide = 2 * E * ffn
     at = 0
-    for ref in (query_ref, key_ref, value_ref, out_ref, router_ref):
+    for ref in (query_ref, key_ref, value_ref, out_ref):
         ref[...] = small_ref[:, at : at + ref.shape[1]]
         at += ref.shape[1]
+    router_ref[...] = small_ref[:, at:].T[:E]
+    width, shard = input_hbm.shape[1], small_ref.shape[0]
+    flat = lax.axis_index("fsdp") * nc + lax.axis_index("ctx")
+    shift = lax.rem(width - flat * shard, width)
+    for i in range(2):
+        row = jnp.broadcast_to(dgains_ref[:, i * width : (i + 1) * width], (8, width))
+        gain_ref[i : i + 1] = pltpu.roll(row, shift, 1)[:1, :shard]
     loads[0].wait()
     stores[0].start()
     loads[1].wait()
@@ -1011,18 +1129,18 @@
         copy.wait()
 
 
-def call(kernel, outs, scratch, collective_id, operands, flops=0):
+def call(kernel, outs, scratch, collective_id, operands, specs=None):
     total = sum(math.prod(o.shape) * o.dtype.itemsize for o in [*outs, *operands])
     return pl.pallas_call(
         kernel,
         out_shape=tuple(outs),
         in_specs=[WHOLE] * len(operands),
-        out_specs=tuple([WHOLE] * len(outs)),
+        out_specs=specs or (WHOLE,) * len(outs),
         scratch_shapes=scratch,
         compiler_params=pltpu.CompilerParams(
             collective_id=collective_id, has_side_effects=True, vmem_limit_bytes=VMEM_BYTES
         ),
-        cost_estimate=pl.CostEstimate(flops=flops, bytes_accessed=total, transcendentals=0),
+        cost_estimate=pl.CostEstimate(flops=0, bytes_accessed=total, transcendentals=0),
     )(*operands)
 
 
@@ -1061,17 +1179,14 @@
     def sems(*dims):
         return pltpu.SemaphoreType.DMA(dims)
 
-    wqkv, wout, router, gains, packed = call(
+    small, gains, packed = call(
         functools.partial(gather_kernel, nf, nc, ffn),
         [
-            shaped((width, qkv_wide), bf16),
-            shaped((width, o_wide), bf16),
-            shaped((width, LANES), bf16),
+            shaped((peers, shard, small_wide), link),
             shaped((8, width), f32),
             shaped((shard, gu_wide + down_wide), bf16),
         ],
         [
-            pltpu.VMEM((peers, shard, small_wide), link),
             sems(nf),
             sems(nf),
             sems(nc - 1, nf),
@@ -1084,15 +1199,17 @@
             value_matrix,
             w_out.T,
             w_router.T,
-            gain_attn[None],
-            gain_moe[None],
+            gain_attn,
+            gain_moe,
             w_gate,
             w_up,
             jnp.swapaxes(w_down, 1, 2),
         ),
     )
     experts = lax.all_gather(packed, both, axis=0, tiled=True)
+    small = small.reshape(width, small_wide).astype(bf16)
     kv_sems = sems(nc - 1, seqs, 2)
+    anywhere = pl.BlockSpec(memory_space=pl.ANY)
     query, kv, mixed, state, normed_two, gates = call(
         functools.partial(front_kernel, n, nc),
         [
@@ -1105,13 +1222,15 @@
         ],
         [
             pltpu.VMEM((seqs, SEQUENCE_LENGTH, 2 * k_wide), bf16),
-            pltpu.VMEM((rows, width), bf16),
+            *[pltpu.VMEM((rows, width), bf16)] * 3,
+            sems(2, rows // 32),
             kv_sems,
             kv_sems,
             *line_scratch(rows, width, 32),
         ],
         0,
-        (tokens, wqkv, wout, router, gains, routes, cos, sin),
+        (tokens, small, gains, routes, cos, sin),
+        (WHOLE, WHOLE, WHOLE, anywhere, anywhere, WHOLE),
     )
 
     block = 256
@@ -1139,12 +1258,16 @@
             shaped((8, width), f32),
         ),
         in_specs=[
-            constant(rows, width),
-            constant(rows, width),
+            anywhere,
+            anywhere,
             constant(rows, LANES),
             anywhere,
-            constant(rows, width),
-            constant(width, LANES),
+            anywhere,
+            pl.BlockSpec(
+                (width, LANES),
+                lambda i: (0, small_wide // LANES - 1),
+                pipeline_mode=pl.Buffered(1),
+            ),
             constant(8, width),
         ],
         out_specs=(
@@ -1155,7 +1278,7 @@
             pl.BlockSpec((8, width), lambda i: (0, 0)),
         ),
         scratch_shapes=[
-            pltpu.VMEM((rows, width), bf16),
+            *[pltpu.VMEM((rows, width), bf16)] * 4,
             pltpu.VMEM((rows, down_wide), bf16),
             pltpu.VMEM((rows, gu_wide), bf16),
             pltpu.VMEM((tall, rows), bf16),
@@ -1165,6 +1288,7 @@
             pltpu.VMEM((rows, LANES), f32),
             pltpu.VMEM((width, gu_wide + down_wide), bf16),
             pltpu.VMEM((2, size, width), bf16),
+            sems(3, blocks),
             sems(2, E // 4),
             sems(width // tall),
             sems(2),
@@ -1180,16 +1304,25 @@
             bytes_accessed=2 * width * (gu_wide + down_wide),
             transcendentals=0,
         ),
-    )(normed_two, cotangent, gates, experts, state, router, gains)
+    )(normed_two, cotangent, gates, experts, state, small, gains)
 
     low, grad_experts = lax.optimization_barrier((low, grad_experts))
     grad_experts = lax.psum_scatter(grad_experts, both, scatter_dimension=0, tiled=True)
 
-    small_block = pltpu.VMEM((peers, -(-shard // 16) * 16, small_wide), bf16)
+    def small_block(*dims):
+        return pltpu.VMEM((*dims, -(-shard // 16) * 16, small_wide), bf16)
+
     whole = pltpu.VMEM((rows, width), bf16)
-    operands = (
-        (moe_part, low, tokens, normed_two)
-        + (wout, wqkv, query, kv, mixed, dlogits, gains, dgain_two, cos, sin)
+    sources = (moe_part, low, small, query, kv, tokens, normed_two, mixed, dlogits)
+    held = (
+        *[(rows, width)] * 2,
+        (width, o_wide),
+        query.shape,
+        kv.shape,
+        (width, qkv_wide),
+        *[(rows, width)] * 2,
+        mixed.shape,
+        dlogits.shape,
     )
     activations, input_grad, dgains, grad_small = pl.pallas_call(
         functools.partial(rear_kernel, n, nf, nc),
@@ -1199,13 +1332,10 @@
             shaped((1, 2 * width), f32),
             shaped((shard, small_wide), f32),
         ),
-        in_specs=[anywhere] * 4 + [WHOLE] * (len(operands) - 4),
+        in_specs=[anywhere] * len(sources) + [WHOLE] * 4,
         out_specs=(anywhere, anywhere, WHOLE, WHOLE),
         scratch_shapes=[
-            whole,
-            whole,
-            whole,
-            whole,
+            *[pltpu.VMEM(dims, bf16) for dims in held],
             pltpu.VMEM((half // 2, q_wide), bf16),
             pltpu.VMEM((half // 2, q_wide), f32),
             pltpu.VMEM((seqs, SEQUENCE_LENGTH, 2 * k_wide), f32),
@@ -1215,14 +1345,18 @@
             pltpu.VMEM((rows, LANES), f32),
             pltpu.VMEM((8, width), f32),
             pltpu.VMEM((peers, 1, 2 * width), f32),
-            small_block,
-            small_block,
+            small_block(peers),
+            small_block(nc - 1, nf),
+            small_block(nf),
             sems(4),
+            sems(len(held) - 1),
             sems(2),
             kv_sems,
             kv_sems,
-            *[sems(peers)] * 4,
-            *line_scratch(rows, width, size),
+            *[sems(peers)] * 2,
+            *[sems(nc - 1, nf)] * 2,
+            *[sems(nf)] * 2,
+            *line_scratch(rows, width, 32),
             *line_scratch(rows, width, 32),
         ],
         compiler_params=pltpu.CompilerParams(
@@ -1233,11 +1367,9 @@
             bytes_accessed=16 * rows * width,
             transcendentals=0,
         ),
-    )(*operands)
-    flat = lax.axis_index("fsdp") * nc + lax.axis_index("ctx")
-    dgains = lax.dynamic_slice_in_dim(dgains.reshape(2, width), flat * shard, shard, 1)
+    )(*sources, gains, dgain_two, cos, sin)
     results = pl.pallas_call(
-        functools.partial(split_kernel, ffn),
+        functools.partial(split_kernel, ffn, nc),
         out_shape=(
             shaped((E, shard, ffn), f32),
             shaped((E, shard, ffn), f32),
@@ -1246,12 +1378,13 @@
             shaped((shard, k_wide), f32),
             shaped((shard, k_wide), f32),
             shaped((shard, o_wide), f32),
-            shaped((shard, E), f32),
+            shaped((E, shard), f32),
+            shaped((2, shard), f32),
             shaped((rows, width), bf16),
             shaped((rows, width), bf16),
         ),
-        in_specs=[WHOLE, WHOLE, anywhere, anywhere],
-        out_specs=(*[WHOLE] * 8, anywhere, anywhere),
+        in_specs=[WHOLE, WHOLE, WHOLE, anywhere, anywhere],
+        out_specs=(*[WHOLE] * 9, anywhere, anywhere),
         scratch_shapes=[
             pltpu.VMEM((rows, width), bf16),
             pltpu.VMEM((rows, width), bf16),
@@ -1259,18 +1392,19 @@
             sems(2),
         ],
         compiler_params=pltpu.CompilerParams(vmem_limit_bytes=VMEM_BYTES),
-    )(grad_experts, grad_small, activations, input_grad)
-    grad_gate, grad_up, grad_down, grad_query, grad_key, grad_value, grad_out, grad_router = results[:8]
+    )(grad_experts, grad_small, dgains, activations, input_grad)
+    grad_gate, grad_up, grad_down, grad_query, grad_key, grad_value, grad_out = results[:7]
+    grad_router, dgains = results[7:9]
     return (
-        results[8],
         results[9],
+        results[10],
         dgains[0],
         grad_query,
         grad_key,
         grad_value,
         grad_out.T,
         dgains[1],
-        grad_router,
+        grad_router.T,
         grad_gate,
         grad_up,
         jnp.swapaxes(grad_down, 1, 2),

time: 456 us -> 436 us (0.956); the launches traced: 448 us -> 432 us
  Pallas kernels: 423 us -> 414 us
  local copies, waits for them, and re-layouts: 7.9 us -> 2.27 us
    pallas_call x2, Pallas kernels: 140 us -> 131 us  [call(): pl.pallas_call(kernel, out_shape=tuple(outs), in_specs=[WHOLE] * len(oper...]
where the time goes in v5:
time: 436 us; the launch traced here: 432 us
  Pallas kernels  414 us (95%)
  between operations  14.4 us (3%)
    pallas_call x1, Pallas kernels, per_device(): pl.pallas_call(functools.partial(rear_kernel, n, nf, nc), out_shape=(shap...  168 us
    pallas_call x2, Pallas kernels, call(): pl.pallas_call(kernel, out_shape=tuple(outs), in_specs=[WHOLE] * len(oper...  131 us
    pallas_call x1, Pallas kernels, per_device(): pl.pallas_call(functools.partial(expert_kernel, n), grid=(blocks,), out_s...  106 us
    pallas_call x1, Pallas kernels, per_device(): pl.pallas_call(functools.partial(split_kernel, ffn, nc), out_shape=(shape...  9.02 us
  transfers between devices with their start and end apart: 2, of which 0 were waited for; matrix products, arithmetic and copies ran while one was open for 1% of the time, Pallas kernels for 62%

profile of v5, /device:TPU:0, one launch (start us, length us, event | category | flops | bytes accessed | tf_op | source)
XLA Modules:
  0.0 432.5 jit_solution(3905109675901832866)
XLA Ops:
  7.2 0.0 copy-start
  7.2 0.0 all-gather.2.cloned.1.call-start
  7.2 30.4 %shard_map.220 = (bf16[8,192,1152]{2,1,0:T(8,128)(2,1)}, f32[8,1536]{1,0:T(8,128)}, bf16[192,6144]{1,0:T(8,128)(2,1)}) custom-call(bf16[192,384]{1,0:T(8,128)(2,1)} %query_ref.1, bf16[192,128]{1,0:T(8,128)(2,1)} %key_ref.1, bf16[192,128]{1,0:T(8,128)(2,1)} %value_ref.1, bf16[192,384]{1,0:T(8,128)(2,1)} %bitcast.13, bf16[16,192]{1,0:T(8,128)(2,1)} %bitcast.14, ...), custom_call_target="tpu_custom_call" | custom-call | bytes 8706816 | tf_op jit(solution)/shard_map/pallas_call | solution.py:1134
  37.7 0.0 all-gather.2.cloned.1.call-update
  37.7 0.0 reduce-scatter.2.cloned.1.call-start
  37.7 0.0 copy-done
  37.8 1.0 copy.25.routes_ref
  38.8 1.8 multiply_sine_fusion
  40.6 100.4 %shard_map.221 = (bf16[1024,384]{1,0:T(8,128)(2,1)}, bf16[2,1024,256]{2,1,0:T(8,128)(2,1)}, bf16[1024,384]{1,0:T(8,128)(2,1)}, bf16[1024,1536]{1,0:T(8,128)(2,1)...) custom-call(bf16[1024,1536]{1,0:T(8,128)(2,1)} %x_hbm.1, bf16[1536,1152]{1,0:T(8,128)(2,1)} %bitcast.9, ...), custom_call_target="tpu_custom_call" | custom-call | bytes 16728064 | tf_op jit(solution)/shard_map/pallas_call | solution.py:1134
  141.0 0.0 all-gather.2.cloned.1.call-done.w_hbm
  141.1 105.9 %shard_map.222 = (bf16[1024,1536]{1,0:T(8,128)(2,1)}, bf16[1536,6144]{1,0:T(8,128)(2,1)}, bf16[1024,1536]{1,0:T(8,128)(2,1)}, bf16[1024,128]{1,0:T(8,128)(2,1)}, f32[8,1536]{1,0:T(8,128)}) custom-call(bf16[1024,1536]{1,0:T(8,128)(2,1)} %get-tuple-element.45.x_hbm.normed_two_hbm, bf16[1024,1536]{1,0:T(8,128)(2,1)} %dy_hbm.1, ...), custom_call_target="tpu_custom_call" | custom-call | flops 57982058496 | bytes 18874368 | tf_op jit(solution)/shard_map/pallas_call | solution.py:1250
  246.9 0.0 reduce-scatter.2.cloned.1.call-update
  247.0 168.2 %shard_map.223 = (bf16[1024,1536]{1,0:T(8,128)(2,1)}, bf16[1024,1536]{1,0:T(8,128)(2,1)}, f32[1,3072]{1,0:T(1,128)}, f32[192,1152]{1,0:T(8,128)}) custom-call(bf16[1024,1536]{1,0:T(8,128)(2,1)} %get-tuple-element.52.moe_hbm, bf16[1024,1536]{1,0:T(8,128)(2,1)} %get-tuple-element.53.low_hbm, bf16[1536,1152]{1,0:T(8,128)(2,1)} %bitcast.11, ...), custom_call_target="tpu_custom_call" | custom-call | flops 21743271936 | bytes 25165824 | tf_op jit(solution)/shard_map/pallas_call | solution.py:1327
  415.1 0.0 reduce-scatter.2.cloned.1.call-done.grads_ref
  415.1 9.0 %shard_map.224 = (f32[16,192,128]{2,1,0:T(8,128)}, f32[16,192,128]{2,1,0:T(8,128)}, f32[16,192,128]{2,1,0:T(8,128)}, f32[192,384]{1,0:T(8,128)}, f32[192,128]{1,...) custom-call(bf16[192,6144]{1,0:T(8,128)(2,1)} %reduce-scatter.2.clon, ...), custom_call_target="tpu_custom_call" | custom-call | tf_op jit(solution)/shard_map/pallas_call | solution.py:1371
  424.2 1.3 fusion.3
  (2 shorter events, 0.0 us)
Async XLA Ops:
  7.2 30.6 %copy-start = (s32[1024,8]{0,1:T(8,128)S(1)}, s32[1024,8]{0,1:T(8,128)}, u32[]{:S(2)}) copy-start(s32[1024,8]{0,1:T(8,128)} %param.14) | copy-start | bytes 98308
  7.2 133.9 %all-gather.2.cloned.1.call-start = ((), (), s32[]{:S(2)}) async-start(), calls=%async_computation.1 | async-start | bytes 21233664 | tf_op jit(solution)/shard_map/all_gather | solution.py:1209
  37.7 377.4 %reduce-scatter.2.cloned.1.call-start = ((), (), s32[]{:S(2)}) async-start(), calls=%async_computation.2 | async-start | bytes 21233664 | tf_op jit(solution)/shard_map/reduce_scatter | solution.py:1310
Sparse Core Ops, SparseCore 0:
  37.8 99.6 all-gather.1
  247.1 132.5 reduce-scatter.1

commit v6 on v5

--- a/solution.py
+++ b/solution.py
@@ -20,22 +20,6 @@
 bf16 = jnp.bfloat16
 MESH = pl.DeviceIdType.MESH
 WHOLE = pl.BlockSpec(memory_space=pltpu.VMEM)
-
-
-def placed(ranks, half):
-    quarter = half // 2
-    steps = jnp.arange(half, dtype=jnp.int32)
-    early = ranks * quarter + steps
-    late = SEQUENCE_LENGTH - (ranks + 1) * quarter + steps - quarter
-    return jnp.where(steps < quarter, early, late)
-
-
-def angle_tables(token_places):
-    halfway = HEAD_SIZE // 2
-    lanes = jnp.arange(LANES, dtype=jnp.int32) % halfway
-    freqs = jnp.exp(lanes.astype(f32) * (-2.0 * math.log(10000.0) / HEAD_SIZE))
-    angles = token_places.astype(f32)[:, None] * freqs[None, :]
-    return jnp.cos(angles), jnp.sin(angles)
 
 
 def aligned(start, size):
@@ -263,9 +247,13 @@
     gate_ref,
     up_ref,
     down_ref,
+    routes_ref,
     small_all,
     gains_ref,
     experts_ref,
+    cos_ref,
+    sin_ref,
+    named_ref,
     send_f,
     recv_f,
     send_c,
@@ -285,8 +273,14 @@
     def to_near(p):
         return {"ctx": lax.rem(c + p, nc)}
 
+    relay = nf == 4 and shard % 32 == 0
+    across, along = f - lax.rem(f, 2) + 1 - lax.rem(f, 2), lax.rem(f + 2, 4)
+    if relay:
+        far = [{"fsdp": across}, {"fsdp": along}]
+    else:
+        far = [to_peer(o) for o in range(1, nf)]
     barrier = pltpu.get_barrier_semaphore()
-    for other in [to_peer(o) for o in range(1, nf)] + [to_near(p) for p in range(1, nc)]:
+    for other in far + [to_near(p) for p in range(1, nc)]:
         pl.semaphore_signal(barrier, inc=1, device_id=other, device_id_type=MESH)
     gains = [g[...].astype(f32).reshape(1, shard) for g in (gain_one_ref, gain_two_ref)]
     blank = jnp.zeros((LANES - E - 2, shard), f32)
@@ -295,7 +289,36 @@
     for piece in (query_ref[...], key_ref[...], value_ref[...], out_ref[...], last):
         small_all[mine, :, at : at + piece.shape[1]] = piece.astype(kind)
         at += piece.shape[1]
-    pl.semaphore_wait(barrier, nf + nc - 2)
+    pl.semaphore_wait(barrier, len(far) + nc - 1)
+
+    owners = [f, across, along, 3 - f] if relay else [from_f(o) for o in range(nf)]
+
+    def relay_copy(i):
+        owner, to = ((f, across), (f, along), (across, along), (along, across))[i]
+        block = small_all.at[owner * nc + c]
+        if i > 1:
+            block = block.at[pl.ds((i - 2) * (shard // 2), shard // 2)]
+        return pltpu.make_async_remote_copy(
+            src_ref=block,
+            dst_ref=block,
+            send_sem=send_f.at[i],
+            recv_sem=recv_f.at[i],
+            device_id={"fsdp": to},
+            device_id_type=MESH,
+        )
+
+    def relay_arrival(i):
+        block = small_all.at[(across, along, 3 - f, 3 - f)[i] * nc + c]
+        if i > 1:
+            block = block.at[pl.ds((i - 2) * (shard // 2), shard // 2)]
+        return pltpu.make_async_remote_copy(
+            src_ref=block,
+            dst_ref=block,
+            send_sem=send_f.at[i],
+            recv_sem=recv_f.at[i],
+            device_id={"fsdp": across},
+            device_id_type=MESH,
+        )
 
     def far_copy(o, rank):
         block = small_all.at[rank * nc + c]
@@ -309,7 +332,7 @@
         )
 
     def near_copy(p, o, rank):
-        block = small_all.at[from_f(o) * nc + rank]
+        block = small_all.at[owners[o] * nc + rank]
         return pltpu.make_async_remote_copy(
             src_ref=block,
             dst_ref=block,
@@ -323,7 +346,11 @@
         for p in range(1, nc):
             near_copy(p, o, c).start()
 
-    loop(1, nf, lambda o: far_copy(o, f).start())
+    if relay:
+        relay_copy(0).start()
+        relay_copy(1).start()
+    else:
+        loop(1, nf, lambda o: far_copy(o, f).start())
     share(0)
     for e in range(E):
         at = (e // 2) * 4 * ffn + (e % 2) * ffn
@@ -332,26 +359,55 @@
         at = 2 * E * ffn + e * ffn
         experts_ref[:, at : at + ffn] = down_ref[e]
 
-    def pass_on(o):
-        far_copy(o, from_f(o)).wait_recv()
-        share(o)
-
-    loop(1, nf, pass_on)
-
-    def shared(o):
+    half = cos_ref.shape[0]
+    quarter = half // 2
+    row = lax.broadcasted_iota(jnp.int32, (half, LANES), 0)
+    lane = lax.broadcasted_iota(jnp.int32, (half, LANES), 1)
+    late = SEQUENCE_LENGTH - (c + 1) * quarter + row - quarter
+    place = jnp.where(row < quarter, c * quarter + row, late)
+    lane = lax.rem(lane, HEAD_SIZE // 2).astype(f32)
+    angle = place.astype(f32) * jnp.exp(lane * (-2.0 * math.log(10000.0) / HEAD_SIZE))
+    cos_ref[...] = jnp.cos(angle)
+    sin_ref[...] = jnp.sin(angle)
+    expert = lax.broadcasted_iota(jnp.int32, (LANES, LANES), 0)
+
+    def name(i):
+        rows = aligned(i * LANES, LANES)
+        routes = routes_ref[:, rows]
+        named = expert == routes[:1]
+        for k in range(1, TOPK):
+            named = named | (expert == routes[k : k + 1])
+        named_ref[rows] = jnp.where(named, 1.0, 0.0).T
+
+    loop(0, named_ref.shape[0] // LANES, name)
+
+    if relay:
+        relay_arrival(0).wait_recv()
+        relay_copy(2).start()
+        share(1)
+        relay_arrival(1).wait_recv()
+        relay_copy(3).start()
+        share(2)
+        relay_arrival(2).wait_recv()
+        relay_arrival(3).wait_recv()
+        share(3)
+    else:
+        for o in range(1, nf):
+            far_copy(o, from_f(o)).wait_recv()
+            share(o)
+    for o in range(nf):
         for p in range(1, nc):
             near_copy(p, o, lax.rem(c + nc - p, nc)).wait_recv()
-
-    loop(0, nf, shared)
     last = small_all[:, :, small_all.shape[2] - LANES :]
     gains_ref[...] = last.reshape(nf * nc * shard, LANES).astype(f32).T[E : E + 8]
-    loop(1, nf, lambda o: far_copy(o, f).wait_send())
-
-    def near_sent(o):
+    if relay:
+        for i in range(4):
+            relay_copy(i).wait_send()
+    else:
+        loop(1, nf, lambda o: far_copy(o, f).wait_send())
+    for o in range(nf):
         for p in range(1, nc):
             near_copy(p, o, c).wait_send()
-
-    loop(0, nf, near_sent)
 
 
 def front_kernel(
@@ -360,7 +416,7 @@
     x_ref,
     small_ref,
     gains_ref,
-    routes_ref,
+    named_ref,
     cos_ref,
     sin_ref,
     query_ref,
@@ -403,11 +459,7 @@
         normed_ref[rows] = normed
         for copy in row_stores(c):
             copy.start()
-        routes = routes_ref[rows]
-        lane = lax.broadcasted_iota(jnp.int32, (line.size, LANES), 1)
-        named = lane == routes[:, :1]
-        for k in range(1, TOPK):
-            named = named | (lane == routes[:, k : k + 1])
+        named = named_ref[rows] > 0.5
         logits = jnp.where(named, dot(normed, small_ref[:, wide:]), -1e30)
         top = jnp.max(logits, -1, keepdims=True)
         raised = jnp.where(named, jnp.exp(logits - top), 0.0)
@@ -1165,7 +1217,6 @@
     half = SEQUENCE_LENGTH // nc
     seqs = rows // half
     both = ("fsdp", "ctx")
-    cos, sin = angle_tables(placed(lax.axis_index("ctx"), half))
     q_wide, k_wide, o_wide = w_query.shape[1], key_matrix.shape[1], w_out.shape[0]
     qkv_wide = q_wide + 2 * k_wide
     ffn = w_gate.shape[2]
@@ -1179,12 +1230,15 @@
     def sems(*dims):
         return pltpu.SemaphoreType.DMA(dims)
 
-    small, gains, packed = call(
+    small, gains, packed, cos, sin, named = call(
         functools.partial(gather_kernel, nf, nc, ffn),
         [
             shaped((peers, shard, small_wide), link),
             shaped((8, width), f32),
             shaped((shard, gu_wide + down_wide), bf16),
+            shaped((half, LANES), f32),
+            shaped((half, LANES), f32),
+            shaped((rows, LANES), f32),
         ],
         [
             sems(nf),
@@ -1204,6 +1258,7 @@
             w_gate,
             w_up,
             jnp.swapaxes(w_down, 1, 2),
+            routes.T,
         ),
     )
     experts = lax.all_gather(packed, both, axis=0, tiled=True)
@@ -1229,7 +1284,7 @@
             *line_scratch(rows, width, 32),
         ],
         0,
-        (tokens, small, gains, routes, cos, sin),
+        (tokens, small, gains, named, cos, sin),
         (WHOLE, WHOLE, WHOLE, anywhere, anywhere, WHOLE),
     )
 

time: 436 us -> 431 us (0.989)
  transfers between devices with their start and end apart: 2 -> 2, of which waited for: 0 -> 0; matrix products, arithmetic and copies ran while one was open for 1% -> 0% of each run, Pallas kernels for 62% -> 63%
where the time goes in v6:
time: 431 us; the launch traced here: 427 us
  Pallas kernels  411 us (95%)
  between operations  14.3 us (3%)
    pallas_call x1, Pallas kernels, per_device(): pl.pallas_call(functools.partial(rear_kernel, n, nf, nc), out_shape=(shap...  169 us
    pallas_call x2, Pallas kernels, call(): pl.pallas_call(kernel, out_shape=tuple(outs), in_specs=[WHOLE] * len(oper...  127 us
    pallas_call x1, Pallas kernels, per_device(): pl.pallas_call(functools.partial(expert_kernel, n), grid=(blocks,), out_s...  106 us
    pallas_call x1, Pallas kernels, per_device(): pl.pallas_call(functools.partial(split_kernel, ffn, nc), out_shape=(shape...  9.02 us
  transfers between devices with their start and end apart: 2, of which 0 were waited for; matrix products, arithmetic and copies ran while one was open for 0% of the time, Pallas kernels for 63%

profile of v6, /device:TPU:0, one launch (start us, length us, event | category | flops | bytes accessed | tf_op | source)
XLA Modules:
  0.0 426.8 jit_solution(5706411676659806344)
XLA Ops:
  7.2 0.0 all-gather.2.cloned.1.call-start
  7.2 26.7 %shard_map.220 = (bf16[8,192,1152]{2,1,0:T(8,128)(2,1)}, f32[8,1536]{1,0:T(8,128)}, bf16[192,6144]{1,0:T(8,128)(2,1)}, f32[512,128]{1,0:T(8,128)}, f32[512,128]{1,0:T(8,128)}, /*index=5*/f32[1024,128]{1,0:T(8,128)}) custom-call(bf16[192,384]{1,0:T(8,128)(2,1)} %query_ref.1, bf16[192,128]{1,0:T(8,128)(2,1)} %key_ref.1, bf16[192,128]{1,0:T(8,128)(2,1)} %value_ref.1, ...), custom_call_target="tpu_custom_call" | custom-call | bytes 9788160 | tf_op jit(solution)/shard_map/pallas_call | solution.py:1186
  33.9 0.0 all-gather.2.cloned.1.call-update
  33.9 0.0 reduce-scatter.2.cloned.1.call-start
  34.0 100.4 %shard_map.221 = (bf16[1024,384]{1,0:T(8,128)(2,1)}, bf16[2,1024,256]{2,1,0:T(8,128)(2,1)}, bf16[1024,384]{1,0:T(8,128)(2,1)}, bf16[1024,1536]{1,0:T(8,128)(2,1)...) custom-call(bf16[1024,1536]{1,0:T(8,128)(2,1)} %x_hbm.1, bf16[1536,1152]{1,0:T(8,128)(2,1)} %bitcast.10, ...), custom_call_target="tpu_custom_call" | custom-call | bytes 17219584 | tf_op jit(solution)/shard_map/pallas_call | solution.py:1186
  134.4 0.0 all-gather.2.cloned.1.call-done.w_hbm
  134.5 106.0 %shard_map.222 = (bf16[1024,1536]{1,0:T(8,128)(2,1)}, bf16[1536,6144]{1,0:T(8,128)(2,1)}, bf16[1024,1536]{1,0:T(8,128)(2,1)}, bf16[1024,128]{1,0:T(8,128)(2,1)}, f32[8,1536]{1,0:T(8,128)}) custom-call(bf16[1024,1536]{1,0:T(8,128)(2,1)} %get-tuple-element.51.x_hbm.normed_two_hbm, bf16[1024,1536]{1,0:T(8,128)(2,1)} %dy_hbm.1, ...), custom_call_target="tpu_custom_call" | custom-call | flops 57982058496 | bytes 18874368 | tf_op jit(solution)/shard_map/pallas_call | solution.py:1305
  240.5 0.0 reduce-scatter.2.cloned.1.call-update
  240.5 168.9 %shard_map.223 = (bf16[1024,1536]{1,0:T(8,128)(2,1)}, bf16[1024,1536]{1,0:T(8,128)(2,1)}, f32[1,3072]{1,0:T(1,128)}, f32[192,1152]{1,0:T(8,128)}) custom-call(bf16[1024,1536]{1,0:T(8,128)(2,1)} %get-tuple-element.58.moe_hbm, bf16[1024,1536]{1,0:T(8,128)(2,1)} %get-tuple-element.59.low_hbm, bf16[1536,1152]{1,0:T(8,128)(2,1)} %bitcast.12, ...), custom_call_target="tpu_custom_call" | custom-call | flops 21743271936 | bytes 25165824 | tf_op jit(solution)/shard_map/pallas_call | solution.py:1382
  409.4 0.0 reduce-scatter.2.cloned.1.call-done.grads_ref
  409.4 9.0 %shard_map.224 = (f32[16,192,128]{2,1,0:T(8,128)}, f32[16,192,128]{2,1,0:T(8,128)}, f32[16,192,128]{2,1,0:T(8,128)}, f32[192,384]{1,0:T(8,128)}, f32[192,128]{1,...) custom-call(bf16[192,6144]{1,0:T(8,128)(2,1)} %reduce-scatter.2.clon, ...), custom_call_target="tpu_custom_call" | custom-call | tf_op jit(solution)/shard_map/pallas_call | solution.py:1426
  418.4 1.3 fusion
Async XLA Ops:
  7.2 127.3 %all-gather.2.cloned.1.call-start = ((), (), s32[]{:S(2)}) async-start(), calls=%async_computation.1 | async-start | bytes 21233664 | tf_op jit(solution)/shard_map/all_gather | solution.py:1264
  33.9 375.5 %reduce-scatter.2.cloned.1.call-start = ((), (), s32[]{:S(2)}) async-start(), calls=%async_computation.2 | async-start | bytes 21233664 | tf_op jit(solution)/shard_map/reduce_scatter | solution.py:1365
Sparse Core Ops, SparseCore 0:
  34.0 99.1 all-gather.1
  240.6 134.2 reduce-scatter.1

commit v7 on v6

--- a/solution.py
+++ b/solution.py
@@ -951,7 +951,7 @@
         dgain[...] += folded(total * unit)
 
     outward = Line(n, me, moe_ref, finish_out, scratch[:7], lag=1, hop=2)
-    inward = Line(n, me, own, finish_in, scratch[7:], hop=2)
+    inward = Line(n, me, own, finish_in, scratch[7:], hop=3)
     dgain[...] = jnp.zeros_like(dgain)
     greet(me, n, [peer(o) for o in range(1, peers)])
 
@@ -1129,9 +1129,9 @@
     dgains_ref,
     out_hbm,
     input_hbm,
-    gate_ref,
-    up_ref,
-    down_ref,
+    gate_hbm,
+    up_hbm,
+    down_hbm,
     query_ref,
     key_ref,
     value_ref,
@@ -1142,6 +1142,9 @@
     grad_hbm,
     act,
     grad,
+    gate_ref,
+    up_ref,
+    down_ref,
     load,
     store,
 ):
@@ -1152,6 +1155,9 @@
     stores = [
         pltpu.make_async_copy(grad, grad_hbm, store.at[0]),
         pltpu.make_async_copy(act, act_hbm, store.at[1]),
+        pltpu.make_async_copy(gate_ref, gate_hbm, store.at[2]),
+        pltpu.make_async_copy(up_ref, up_hbm, store.at[3]),
+        pltpu.make_async_copy(down_ref, down_hbm, store.at[4]),
     ]
     for copy in loads:
         copy.start()
@@ -1171,12 +1177,13 @@
     stores[0].start()
     loads[1].wait()
     stores[1].start()
-    for e in range(E):
-        at = (e // 2) * 4 * ffn + (e % 2) * ffn
-        gate_ref[e] = grads_ref[:, at : at + ffn].astype(f32)
-        up_ref[e] = grads_ref[:, at + 2 * ffn : at + 3 * ffn].astype(f32)
-        at = gu_wide + e * ffn
-        down_ref[e] = grads_ref[:, at : at + ffn].astype(f32)
+    for kind, ref in enumerate((gate_ref, up_ref, down_ref)):
+        for e in range(E):
+            at = (e // 2) * 4 * ffn + (e % 2) * ffn + kind * 2 * ffn
+            if kind == 2:
+                at = gu_wide + e * ffn
+            ref[e] = grads_ref[:, at : at + ffn].astype(f32)
+        stores[2 + kind].start()
     for copy in stores:
         copy.wait()
 
@@ -1439,12 +1446,13 @@
             shaped((rows, width), bf16),
         ),
         in_specs=[WHOLE, WHOLE, WHOLE, anywhere, anywhere],
-        out_specs=(*[WHOLE] * 9, anywhere, anywhere),
+        out_specs=(*[anywhere] * 3, *[WHOLE] * 6, anywhere, anywhere),
         scratch_shapes=[
             pltpu.VMEM((rows, width), bf16),
             pltpu.VMEM((rows, width), bf16),
+            *[pltpu.VMEM((E, shard, ffn), f32)] * 3,
             sems(2),
-            sems(2),
+            sems(5),
         ],
         compiler_params=pltpu.CompilerParams(vmem_limit_bytes=VMEM_BYTES),
     )(grad_experts, grad_small, dgains, activations, input_grad)

time: 431 us -> 430 us (level)
  no operation moved by 1% of the time
where the time goes in v7:
time: 430 us; the launch traced here: 426 us
  Pallas kernels  411 us (96%)
  between operations  14.3 us (3%)
    pallas_call x1, Pallas kernels, per_device(): pl.pallas_call(functools.partial(rear_kernel, n, nf, nc), out_shape=(shap...  169 us
    pallas_call x2, Pallas kernels, call(): pl.pallas_call(kernel, out_shape=tuple(outs), in_specs=[WHOLE] * len(oper...  127 us
    pallas_call x1, Pallas kernels, per_device(): pl.pallas_call(functools.partial(expert_kernel, n), grid=(blocks,), out_s...  106 us
    pallas_call x1, Pallas kernels, per_device(): pl.pallas_call(functools.partial(split_kernel, ffn, nc), out_shape=(shape...  8.94 us
  transfers between devices with their start and end apart: 2, of which 0 were waited for; matrix products, arithmetic and copies ran while one was open for 0% of the time, Pallas kernels for 63%

profile of v7, /device:TPU:0, one launch (start us, length us, event | category | flops | bytes accessed | tf_op | source)
XLA Modules:
  0.0 426.5 jit_solution(9262122525463036566)
XLA Ops:
  7.2 0.0 all-gather.2.cloned.1.call-start
  7.2 26.7 %shard_map.220 = (bf16[8,192,1152]{2,1,0:T(8,128)(2,1)}, f32[8,1536]{1,0:T(8,128)}, bf16[192,6144]{1,0:T(8,128)(2,1)}, f32[512,128]{1,0:T(8,128)}, f32[512,128]{1,0:T(8,128)}, /*index=5*/f32[1024,128]{1,0:T(8,128)}) custom-call(bf16[192,384]{1,0:T(8,128)(2,1)} %query_ref.1, bf16[192,128]{1,0:T(8,128)(2,1)} %key_ref.1, bf16[192,128]{1,0:T(8,128)(2,1)} %value_ref.1, ...), custom_call_target="tpu_custom_call" | custom-call | bytes 9788160 | tf_op jit(solution)/shard_map/pallas_call | solution.py:1193
  33.9 0.0 all-gather.2.cloned.1.call-update
  33.9 0.0 reduce-scatter.2.cloned.1.call-start
  34.0 100.4 %shard_map.221 = (bf16[1024,384]{1,0:T(8,128)(2,1)}, bf16[2,1024,256]{2,1,0:T(8,128)(2,1)}, bf16[1024,384]{1,0:T(8,128)(2,1)}, bf16[1024,1536]{1,0:T(8,128)(2,1)...) custom-call(bf16[1024,1536]{1,0:T(8,128)(2,1)} %x_hbm.1, bf16[1536,1152]{1,0:T(8,128)(2,1)} %bitcast.10, ...), custom_call_target="tpu_custom_call" | custom-call | bytes 17219584 | tf_op jit(solution)/shard_map/pallas_call | solution.py:1193
  134.4 0.0 all-gather.2.cloned.1.call-done.w_hbm
  134.5 106.0 %shard_map.222 = (bf16[1024,1536]{1,0:T(8,128)(2,1)}, bf16[1536,6144]{1,0:T(8,128)(2,1)}, bf16[1024,1536]{1,0:T(8,128)(2,1)}, bf16[1024,128]{1,0:T(8,128)(2,1)}, f32[8,1536]{1,0:T(8,128)}) custom-call(bf16[1024,1536]{1,0:T(8,128)(2,1)} %get-tuple-element.51.x_hbm.normed_two_hbm, bf16[1024,1536]{1,0:T(8,128)(2,1)} %dy_hbm.1, ...), custom_call_target="tpu_custom_call" | custom-call | flops 57982058496 | bytes 18874368 | tf_op jit(solution)/shard_map/pallas_call | solution.py:1312
  240.5 0.0 reduce-scatter.2.cloned.1.call-update
  240.5 168.6 %shard_map.223 = (bf16[1024,1536]{1,0:T(8,128)(2,1)}, bf16[1024,1536]{1,0:T(8,128)(2,1)}, f32[1,3072]{1,0:T(1,128)}, f32[192,1152]{1,0:T(8,128)}) custom-call(bf16[1024,1536]{1,0:T(8,128)(2,1)} %get-tuple-element.58.moe_hbm, bf16[1024,1536]{1,0:T(8,128)(2,1)} %get-tuple-element.59.low_hbm, bf16[1536,1152]{1,0:T(8,128)(2,1)} %bitcast.12, ...), custom_call_target="tpu_custom_call" | custom-call | flops 21743271936 | bytes 25165824 | tf_op jit(solution)/shard_map/pallas_call | solution.py:1389
  409.1 0.0 reduce-scatter.2.cloned.1.call-done.grads_ref
  409.1 8.9 %shard_map.224 = (f32[16,192,128]{2,1,0:T(8,128)}, f32[16,192,128]{2,1,0:T(8,128)}, f32[16,192,128]{2,1,0:T(8,128)}, f32[192,384]{1,0:T(8,128)}, f32[192,128]{1,...) custom-call(bf16[192,6144]{1,0:T(8,128)(2,1)} %reduce-scatter.2.clon, ...), custom_call_target="tpu_custom_call" | custom-call | tf_op jit(solution)/shard_map/pallas_call | solution.py:1433
  418.1 1.3 fusion
Async XLA Ops:
  7.2 127.3 %all-gather.2.cloned.1.call-start = ((), (), s32[]{:S(2)}) async-start(), calls=%async_computation.1 | async-start | bytes 21233664 | tf_op jit(solution)/shard_map/all_gather | solution.py:1271
  33.9 375.2 %reduce-scatter.2.cloned.1.call-start = ((), (), s32[]{:S(2)}) async-start(), calls=%async_computation.2 | async-start | bytes 21233664 | tf_op jit(solution)/shard_map/reduce_scatter | solution.py:1372
Sparse Core Ops, SparseCore 0:
  34.0 99.1 all-gather.1
  240.6 141.0 reduce-scatter.1
